TPU v7x, 32 devices: a whole 2x2x4 slice. The times are simulated.
32 devices in a mesh: region: 8 (over y, x, core), grp: 4 (over z).
Axes of the slice: x: 2, y: 2, z: 4, core: 2. Of those that a mesh axis runs over, the one named last changes fastest.
Arguments:
- transmission: float32 [2, 640, 5120], P(None, 'grp', 'region'), may hold values from -3 to 3
- probe: bfloat16 [2, 8, 512, 512], P(None, None, 'grp'), may hold values from -1.5 to 1.5
- measured: float32 [8, 512, 512], P('region', 'grp'), may hold values from 0 to 2
- positions: int32 [8, 2], P('region'), may hold values from 0 to 128
- past_steps: float32 [4, 2, 640, 5120], P(None, None, 'grp', 'region'), may hold values from -40 to 40
- past_changes: float32 [3, 2, 640, 5120], P(None, None, 'grp', 'region'), may hold values from -240 to 240
- old_gradient: float32 [2, 640, 5120], P(None, 'grp', 'region'), may hold values from -40 to 40
Outputs:
- updated: float32 [2, 640, 5120], P(None, 'grp', 'region')
- gradient: float32 [2, 640, 5120], P(None, 'grp', 'region')
All inputs are finite; a program needn't handle non-finite values.
Results may differ from a plain program's by a relative error of at most 0.019.
The roundings to bfloat16 on the way count: a program that leaves them out, or rounds other values in their place, can miss the bound.
Values may be sent and summed in bfloat16 or wider, within the bound.
No kernel may reach another device: no remote copies, remote signals or barrier semaphores. Data moves between devices by JAX's collectives and lax.ppermute only.
A program may use at most 64 MiB of HBM per device.

v0:
```python
import math

import jax
import jax.numpy as jnp
from jax import lax
from jax.sharding import PartitionSpec as P

TWO_PI = 2.0 * math.pi
CURVE_FLOOR = 0.25
TIKHONOV = 0.5
EPSILON = 1e-06


def dft_tables(count):
    index = jnp.arange(count, dtype=jnp.int32)
    phase = (index[:, None] * index[None, :] % count).astype(jnp.float32) * (TWO_PI / count)
    factor = 1.0 / math.sqrt(count)
    return (
        (jnp.cos(phase) * factor).astype(jnp.bfloat16),
        (-jnp.sin(phase) * factor).astype(jnp.bfloat16),
    )


def chirp_table(count):
    index = jnp.arange(count, dtype=jnp.int32)
    wavenumber = (index + count // 2) % count - count // 2
    phase = (wavenumber * wavenumber % (4 * count)).astype(jnp.float32) * (TWO_PI / (4 * count))
    return (jnp.cos(phase), -jnp.sin(phase))


def rotate(real_part, imag_part, turn_real, turn_imag):
    return (
        real_part * turn_real - imag_part * turn_imag,
        real_part * turn_imag + imag_part * turn_real,
    )


def narrow(pair):
    return jnp.stack([pair[0], pair[1]]).astype(jnp.bfloat16)


def right_product(field, matrix_real, matrix_imag):

    def single(left, right):
        return jnp.einsum("...k,kj->...j", left, right, preferred_element_type=jnp.float32)

    return (
        single(field[0], matrix_real) - single(field[1], matrix_imag),
        single(field[0], matrix_imag) + single(field[1], matrix_real),
    )


def left_product(matrix_real, matrix_imag, field):

    def single(left, right):
        return jnp.einsum("jk,...kc->...jc", left, right, preferred_element_type=jnp.float32)

    return (
        single(matrix_real, field[0]) - single(matrix_imag, field[1]),
        single(matrix_real, field[1]) + single(matrix_imag, field[0]),
    )


def shards(transmission, probe, measured, positions, past_steps, past_changes, old_gradient):
    member = lax.axis_index("grp")
    frame_len = probe.shape[3]
    rows_here = probe.shape[2]
    tile_len = transmission.shape[2]
    anchor = jnp.zeros((), jnp.int32)
    fwd_real, fwd_imag = dft_tables(frame_len)
    inv_imag = -fwd_imag
    chirp_real, chirp_imag = chirp_table(frame_len)
    probe_wide = probe.astype(jnp.float32)
    tile = lax.all_gather(transmission.astype(jnp.bfloat16), "grp", axis=1, tiled=True)
    frame = 0
    first_row = positions[frame, 0] + member * rows_here
    window = jnp.swapaxes(
        lax.dynamic_slice(
            tile, (anchor, positions[frame, 1], first_row), (2, frame_len, rows_here)
        ),
        1,
        2,
    ).astype(jnp.float32)
    wave = narrow(rotate(probe_wide[0], probe_wide[1], window[0], window[1]))
    section = narrow(rotate(*right_product(wave, fwd_real, fwd_imag), chirp_real, chirp_imag))
    spread = narrow(right_product(section, fwd_real, inv_imag))
    section = narrow(
        rotate(
            *left_product(
                fwd_real,
                fwd_imag,
                lax.all_to_all(spread, "grp", split_axis=3, concat_axis=2, tiled=True),
            ),
            chirp_real[:, None],
            chirp_imag[:, None]
        )
    )
    far_field = narrow(left_product(fwd_real, inv_imag, section))
    near_rows = lax.all_to_all(far_field, "grp", split_axis=2, concat_axis=3, tiled=True)
    field_wide = near_rows.astype(jnp.float32)
    misfit = (
        jnp.sum(field_wide[0] * field_wide[0] + field_wide[1] * field_wide[1], axis=0)
        - measured[frame]
    )
    weighted = (misfit * field_wide).astype(jnp.bfloat16)
    section = narrow(
        rotate(
            *left_product(
                fwd_real,
                fwd_imag,
                lax.all_to_all(weighted, "grp", split_axis=3, concat_axis=2, tiled=True),
            ),
            chirp_real[:, None],
            -chirp_imag[:, None]
        )
    )
    returned = narrow(left_product(fwd_real, inv_imag, section))
    section = narrow(
        rotate(
            *right_product(
                lax.all_to_all(returned, "grp", split_axis=2, concat_axis=3, tiled=True),
                fwd_real,
                fwd_imag,
            ),
            chirp_real,
            -chirp_imag
        )
    )
    back_wave = jnp.stack(right_product(section, fwd_real, inv_imag))
    grad_real = 4.0 * jnp.sum(probe_wide[0] * back_wave[0] + probe_wide[1] * back_wave[1], axis=0)
    grad_imag = 4.0 * jnp.sum(probe_wide[0] * back_wave[1] - probe_wide[1] * back_wave[0], axis=0)
    frame_grads = [jnp.stack([grad_real, grad_imag])]
    scattered = jnp.zeros((2, tile_len, tile_len), jnp.float32)
    frame = 0
    corner = (anchor, positions[frame, 1], positions[frame, 0] + member * rows_here)
    scattered = lax.dynamic_update_slice(scattered, jnp.swapaxes(frame_grads[frame], 1, 2), corner)
    data_grad = lax.psum_scatter(
        scattered.astype(jnp.bfloat16), "grp", scatter_dimension=1, tiled=True
    ).astype(jnp.float32)
    gradient = data_grad + TIKHONOV * transmission
    depth = past_steps.shape[0]
    last = depth - 1
    change_new = gradient - old_gradient
    steps_list = [past_steps[index] for index in range(depth)]
    changes = [past_changes[index] for index in range(depth - 1)] + [change_new]
    alphas = [None] * depth
    curvature, self_dots, change_norm = lax.psum(
        (
            jnp.stack([jnp.sum(steps_list[index] * changes[index]) for index in range(depth)]),
            jnp.sum(past_steps * past_steps, axis=(1, 2, 3)),
            jnp.sum(change_new * change_new),
        ),
        ("region", "grp"),
    )
    weights = [
        1.0 / jnp.maximum(curvature[index], CURVE_FLOOR * self_dots[index])
        for index in range(depth)
    ]
    direction = gradient
    for index in reversed(range(depth)):
        alphas[index] = weights[index] * lax.psum(
            jnp.sum(steps_list[index] * direction), ("region", "grp")
        )
        direction = direction - alphas[index] * changes[index]
    scale = jnp.maximum(curvature[last], CURVE_FLOOR * self_dots[last]) / (change_norm + EPSILON)
    direction = scale * direction
    for index in range(depth):
        beta = weights[index] * lax.psum(jnp.sum(changes[index] * direction), ("region", "grp"))
        direction = direction + (alphas[index] - beta) * steps_list[index]
    return (transmission - direction, gradient)


def solution(mesh):
    return jax.shard_map(
        shards,
        mesh=mesh,
        in_specs=(
            P(None, "grp", "region"),
            P(None, None, "grp", None),
            P("region", "grp", None),
            P("region", None),
            P(None, None, "grp", "region"),
            P(None, None, "grp", "region"),
            P(None, "grp", "region"),
        ),
        out_specs=(P(None, "grp", "region"), P(None, "grp", "region")),
        check_vma=False,
    )
```

profile of v0, /device:TPU:0, one launch (start us, length us, event | category | flops | bytes accessed | tf_op | source)
XLA Modules:
  0.0 910.4 jit_solution(12699570033334490435)
XLA Ops:
  12.5 4.1 convert_element_type.226
  17.3 33.8 %all-gather.2.cloned.1.call-done = bf16[2,640,640]{2,1,0:T(8,128)(2,1)} async-done(((bf16[2,160,640]{2,1,0:T(8,128)(2,1)}), bf16[2,640,640]{2,1,0:T(8,128)(2,1)}) %all-gather.2.cloned.1.call-update) | async-done | bytes 1638416 | tf_op jit(solution)/shard_map/all_gather | solution.py:74
  52.6 2.9 fusion.17
  55.5 5.6 fusion.92
  61.2 5.7 fusion.63
  66.9 6.1 convolution_subtract_fusion.4
  73.0 5.6 add_convert_fusion.6
  78.6 5.6 fusion.89
  84.2 5.9 fusion.53
  90.1 5.6 fusion.7
  95.7 5.5 fusion.8
  101.5 3.1 copy.41
  104.6 51.9 %all_to_all.54 = bf16[2,8,128,512]{2,1,0,3:T(8,128)(2,1)S(1)} all-to-all(bf16[2,8,128,512]{2,1,0,3:T(8,128)(2,1)} %copy.41), channel_id=1, replica_groups=mesh['region'=8,'grp'=4] {'grp'}, dimensions={3} | all-to-all | bytes 4194304 | tf_op jit(solution)/shard_map/all_to_all | solution.py:92
  159.4 6.4 fusion.84
  166.2 5.6 fusion.86
  171.8 6.1 convolution_add_fusion.3
  178.0 5.6 fusion.18
  183.6 15.7 %fusion.82 = f32[8,128,512]{2,1,0:T(8,128)S(1)} fusion(bf16[8,512,128]{1,2,0:T(8,128)(2,1)S(1)} %get-tuple-element.29), kind=kOutput, calls=%fused_computation.142 | convolution fusion | flops 541065216 | bytes 3145728 | tf_op jit(solution)/shard_map/jk,...kc->...jc/dot_general | solution.py:56
  199.3 5.6 fusion.80
  204.9 5.6 fusion.9
  210.5 5.6 fusion.10
  216.2 3.1 copy.43
  219.3 51.3 %all_to_all.55 = bf16[2,8,512,128]{3,1,0,2:T(8,128)(2,1)S(1)} all-to-all(bf16[2,8,512,128]{3,1,0,2:T(8,128)(2,1)} %copy.43), channel_id=1, replica_groups=mesh['region'=8,'grp'=4] {'grp'}, dimensions={2} | all-to-all | bytes 4194304 | tf_op jit(solution)/shard_map/all_to_all | solution.py:99
  271.2 2.5 convert_bitcast_fusion
  273.7 5.4 copy.48
  279.0 2.7 fusion.2
  282.2 2.7 fusion
  284.9 2.7 copy.49
  287.6 3.6 all-to-all-start.2
  291.3 47.1 %all-to-all-done.2 = bf16[2,8,128,512]{2,1,0,3:T(8,128)(2,1)S(1)} async-done(((bf16[2,8,128,512]{2,1,0,3:T(8,128)(2,1)}), bf16[2,8,128,512]{2,1,0,3:T(8,128)(2,1)S(1)}, u32[]{:S(2)}, u32[]{:S(2)}) %all-to-all-start.2) | async-done | bytes 2097184 | tf_op jit(solution)/shard_map/all_to_all | solution.py:111
  340.8 6.4 fusion.76
  348.5 5.6 fusion.78
  354.1 6.1 convolution_add_fusion.2
  360.2 5.6 fusion.20
  365.9 5.6 fusion.74
  371.5 5.8 fusion.72
  377.3 5.6 fusion.11
  382.9 5.6 fusion.12
  388.6 3.1 copy.53
  391.7 51.3 %all_to_all.56 = bf16[2,8,512,128]{3,1,0,2:T(8,128)(2,1)S(1)} all-to-all(bf16[2,8,512,128]{3,1,0,2:T(8,128)(2,1)} %copy.53), channel_id=1, replica_groups=mesh['region'=8,'grp'=4] {'grp'}, dimensions={2} | all-to-all | bytes 4194304 | tf_op jit(solution)/shard_map/all_to_all | solution.py:121
  445.9 6.4 fusion.70
  452.2 6.4 fusion.56
  459.0 6.8 convolution_subtract_fusion.1
  465.8 5.6 add_convert_fusion
  471.4 5.6 fusion.67
  477.0 5.9 fusion.46
  482.9 6.1 convolution_subtract_fusion
  489.1 5.9 fusion.4
  498.3 6.2 dynamic_update_slice.3
  504.9 35.0 %reduce-scatter.2.cloned.1.call-done = bf16[2,160,640]{2,1,0:T(8,128)(2,1)} async-done(((bf16[2,640,640]{2,1,0:T(8,128)(2,1)}), bf16[2,160,640]{2,1,0:T(8,128)(2,1)}) %reduce-scatter.2.cloned.1.call-update) | async-done | bytes 409616 | tf_op jit(solution)/shard_map/reduce_scatter | solution.py:137
  539.9 4.5 fusion.39
  544.4 2.5 pad_maximum_fusion.3
  546.9 39.5 %all-reduce.1 = (f32[4]{0:T(128)S(1)}, f32[4]{0:T(128)S(1)}, f32[]{:T(128)}) all-reduce(f32[4]{0:T(128)S(1)} %pad_maximum_fusion.3, f32[4]{0:T(128)S(1)} %multiply_reduce_fusion, f32[]{:T(128)} %get-tuple-element.7), channel_id=1, replica_groups=mesh['region'=8,'grp'=4] {'region','grp'}, use_global_device_ids=true, to_apply=%region_8.9 | all-reduce | flops 9 | bytes 72 | tf_op jit(solution)/shard_map/psum | solution.py:147
  591.8 40.2 %psum.81 = f32[]{:T(128)} all-reduce(f32[]{:T(128)} %fusion.32), channel_id=1, replica_groups=mesh['region'=8,'grp'=4] {'region','grp'}, use_global_device_ids=true, to_apply=%region_16.17 | all-reduce | flops 1 | bytes 8 | tf_op jit(solution)/shard_map/psum | solution.py:161
  634.0 3.3 fusion.37
  637.4 40.5 %psum.82 = f32[]{:T(128)} all-reduce(f32[]{:T(128)} %get-tuple-element.19), channel_id=1, replica_groups=mesh['region'=8,'grp'=4] {'region','grp'}, use_global_device_ids=true, to_apply=%region_18.19 | all-reduce | flops 1 | bytes 8 | tf_op jit(solution)/shard_map/psum | solution.py:161
  682.0 40.6 %all-reduce = (f32[]{:T(128)}, f32[]{:T(128)}) all-reduce(f32[]{:T(128)} %fusion.43, f32[]{:T(128)} %get-tuple-element.9), channel_id=1, replica_groups=mesh['region'=8,'grp'=4] {'region','grp'}, use_global_device_ids=true, to_apply=%region_20.21 | all-reduce | flops 2 | bytes 16 | tf_op jit(solution)/shard_map/psum | solution.py:161
  725.2 3.4 fusion.42
  728.5 40.6 %psum.84 = f32[]{:T(128)} all-reduce(f32[]{:T(128)} %get-tuple-element.17), channel_id=1, replica_groups=mesh['region'=8,'grp'=4] {'region','grp'}, use_global_device_ids=true, to_apply=%region_22.23 | all-reduce | flops 1 | bytes 8 | tf_op jit(solution)/shard_map/psum | solution.py:168
  772.1 40.3 %psum.85 = f32[]{:T(128)} all-reduce(f32[]{:T(128)} %fusion.36), channel_id=1, replica_groups=mesh['region'=8,'grp'=4] {'region','grp'}, use_global_device_ids=true, to_apply=%region_24.25 | all-reduce | flops 1 | bytes 8 | tf_op jit(solution)/shard_map/psum | solution.py:168
  813.2 3.1 fusion.31
  816.3 40.7 %psum.86 = f32[]{:T(128)} all-reduce(f32[]{:T(128)} %get-tuple-element.15), channel_id=1, replica_groups=mesh['region'=8,'grp'=4] {'region','grp'}, use_global_device_ids=true, to_apply=%region_26.27 | all-reduce | flops 1 | bytes 8 | tf_op jit(solution)/shard_map/psum | solution.py:168
  859.8 40.2 %psum.87 = f32[]{:T(128)} all-reduce(f32[]{:T(128)} %multiply_reduce_fusion.1), channel_id=1, replica_groups=mesh['region'=8,'grp'=4] {'region','grp'}, use_global_device_ids=true, to_apply=%region_28.29 | all-reduce | flops 1 | bytes 8 | tf_op jit(solution)/shard_map/psum | solution.py:168
  900.7 2.4 fusion.28
  (58 shorter events, 30.8 us)
Async XLA Ops:
  7.2 43.9 %all-gather.2.cloned.1.call-start = ((), (), s32[]{:S(2)}) async-start(), calls=%async_computation.5 | async-start | bytes 2048000 | tf_op jit(solution)/shard_map/all_gather | solution.py:74
  166.2 5.7 copy-start.4
  279.0 3.0 copy-start.2
  287.6 50.8 %all-to-all-start.2 = ((bf16[2,8,128,512]{2,1,0,3:T(8,128)(2,1)}), bf16[2,8,128,512]{2,1,0,3:T(8,128)(2,1)S(1)}, u32[]{:S(2)}, u32[]{:S(2)}) async-start(bf16[2,8,128,512]{2,1,0,3:T(8,128)(2,1)} %copy.49), calls=%async_computation.2 | async-start | bytes 4194304 | tf_op jit(solution)/shard_map/all_to_all | solution.py:111
  291.2 248.7 %reduce-scatter.2.cloned.1.call-start = ((), (), s32[]{:S(2)}) async-start(), calls=%async_computation.6 | async-start | bytes 2048000 | tf_op jit(solution)/shard_map/reduce_scatter | solution.py:137
  348.4 5.7 copy-start.3
  459.0 6.8 copy-start.5
  482.9 6.1 copy-start.1
  495.7 8.8 copy-start
Sparse Core Ops, SparseCore 0:
  10.1 40.8 all-gather.1
  504.6 35.2 reduce-scatter.1
where the time goes:
time: 921 us; the launch traced here: 910 us
  blocking collectives  477 us (52%)
  matrix products  197 us (21%)
  waiting for transfers between devices  116 us (13%)
  other arithmetic  48.3 us (5%)
  local copies, waits for them, and re-layouts  40.1 us (4%)
  between operations  28.5 us (3%)
    psum x4, blocking collectives, shards(): lax.psum(jnp.sum(changes[index] * direction), ('region', 'grp'))  162 us
    psum x3, blocking collectives, shards(): lax.psum(jnp.sum(steps_list[index] * direction), ('region', 'grp'))  121 us
    dot_general x16, matrix products, single(): jnp.einsum('jk,...kc->...jc', left, right, preferred_element_type=jnp.flo...  102 us
    dot_general x16, matrix products, single(): jnp.einsum('...k,kj->...j', left, right, preferred_element_type=jnp.float32)  94.3 us
    all_to_all x1, blocking collectives, shards(): lax.all_to_all(spread, 'grp', split_axis=3, concat_axis=2, tiled=True)  51.9 us
    all_to_all x1, blocking collectives, shards(): lax.all_to_all(far_field, 'grp', split_axis=2, concat_axis=3, tiled=True)  51.3 us
    all_to_all x1, blocking collectives, shards(): lax.all_to_all(returned, 'grp', split_axis=2, concat_axis=3, tiled=True)  51.3 us
    all_to_all x1, waiting for transfers between devices, shards(): lax.all_to_all(weighted, 'grp', split_axis=3, concat_axis=2, tiled=True)  47.1 us
  transfers between devices with their start and end apart: 3, of which 3 were waited for; matrix products, arithmetic and copies ran while one was open for 1% of the time, Pallas kernels for 0%

commit v1 on v0

--- a/solution.py
+++ b/solution.py
@@ -1,14 +1,25 @@
+import functools
 import math
 
 import jax
 import jax.numpy as jnp
+import ml_dtypes
+import numpy as np
 from jax import lax
+from jax.experimental import pallas as pl
+from jax.experimental.pallas import tpu as pltpu
 from jax.sharding import PartitionSpec as P
 
 TWO_PI = 2.0 * math.pi
 CURVE_FLOOR = 0.25
 TIKHONOV = 0.5
 EPSILON = 1e-06
+BF = jnp.bfloat16
+F32 = jnp.float32
+AXES = ("region", "grp")
+LANES = 128
+MIB = 1 << 20
+HIST = 4
 
 
 def dft_tables(count):
@@ -61,7 +72,7 @@
     )
 
 
-def shards(transmission, probe, measured, positions, past_steps, past_changes, old_gradient):
+def general(transmission, probe, measured, positions, past_steps, past_changes, old_gradient):
     member = lax.axis_index("grp")
     frame_len = probe.shape[3]
     rows_here = probe.shape[2]
@@ -170,7 +181,459 @@
     return (transmission - direction, gradient)
 
 
+def propagators(count):
+    index = np.arange(count, dtype=np.int64)
+    phase = (index[:, None] * index[None, :] % count).astype(np.float32) * np.float32(TWO_PI / count)
+    factor = np.float32(1.0 / math.sqrt(count))
+    table = (np.cos(phase) * factor).astype(ml_dtypes.bfloat16).astype(np.float64) + 1j * (
+        -np.sin(phase) * factor
+    ).astype(ml_dtypes.bfloat16).astype(np.float64)
+    wavenumber = (index + count // 2) % count - count // 2
+    chirp = np.exp(-1j * (wavenumber * wavenumber % (4 * count)) * (TWO_PI / (4 * count)))
+    folded = (table * chirp[None, :]) @ np.conj(table)
+    real, imag = folded.real, folded.imag
+    right = np.block([[real, imag], [-imag, real]]).astype(ml_dtypes.bfloat16)
+    return right, np.ascontiguousarray(right.T)
+
+
+def dot(left, right, dims=((1,), (0,))):
+    return lax.dot_general(left, right, (dims, ((), ())), preferred_element_type=F32)
+
+
+def shift_table(rows, columns, row_base, column_base):
+    row = lax.broadcasted_iota(jnp.int32, (rows, columns), 0) + row_base
+    column = lax.broadcasted_iota(jnp.int32, (rows, columns), 1) + column_base
+    return jnp.where(row == column, 1.0, 0.0).astype(BF)
+
+
+def cut_kernel(pos_ref, tile_ref, out_ref):
+    tile_len, frame_len = tile_ref.shape[2], out_ref.shape[2]
+    table = shift_table(tile_len, frame_len, 0, pos_ref[0, 0])
+    for part in range(2):
+        out_ref[part] = dot(tile_ref[part].astype(BF), table).astype(BF)
+
+
+def forward_kernel(
+    place_ref, own_ref, side_ref, mates_ref, mine_ref, q0_ref, q1_ref, q2_ref, q3a_ref, q3b_ref, measured_ref,
+    right_ref, left_ref, far_ref, probe_ref, send_ref, keep_ref, tile, window, turned,
+):
+    column, core, place, line, half = (place_ref[index] for index in range(5))
+    piece_len = own_ref.shape[1]
+    chunk, frame_len = mine_ref.shape[2], mine_ref.shape[3]
+    modes = mine_ref.shape[1]
+    piece = 2 * core + half
+    for step, ref in ((0, own_ref), (1, side_ref), (2, mates_ref.at[0]), (3, mates_ref.at[1])):
+        base = pl.multiple_of(lax.bitwise_xor(piece, step) * piece_len, piece_len)
+        for part in range(2):
+            tile[part, pl.ds(base, piece_len), :] = ref[part]
+    table = shift_table(tile.shape[1], frame_len, 0, column)
+    for part in range(2):
+        window[part] = dot(tile[part], table, ((0,), (0,))).astype(BF)
+
+    def rows_of(step):
+        return pl.ds(pl.multiple_of(lax.bitwise_xor(place, step) * chunk, chunk), chunk)
+
+    for part in range(2):
+        for mode in range(modes):
+            probe_ref[part, mode, rows_of(0), :] = mine_ref[part, mode]
+    cut = q3a_ref.shape[0]
+    for turn, ref in ((0, q0_ref), (1, q1_ref), (2, q2_ref), (3, None)):
+        combo = lax.bitwise_xor(line, turn)
+        part, mode = lax.rem(combo, 2), lax.div(combo, 2)
+        for step in range(1, 4):
+            start = (step - 1) * chunk
+            if ref is not None:
+                value = ref[start : start + chunk]
+            elif start + chunk <= cut:
+                value = q3a_ref[start : start + chunk]
+            elif start >= cut:
+                value = q3b_ref[start - cut : start - cut + chunk]
+            else:
+                value = jnp.concatenate([q3a_ref[start:cut], q3b_ref[: start + chunk - cut]], axis=0)
+            probe_ref[part, mode, rows_of(step), :] = value
+
+    block = frame_len // 2
+    for mode in range(modes):
+
+        @pl.loop(0, 2)
+        def _(index):
+            rows = pl.ds(pl.multiple_of(index * block, block), block)
+            low_rows = pl.ds(pl.multiple_of(index * block + frame_len, block), block)
+            pr, pi = probe_ref[0, mode, rows, :].astype(F32), probe_ref[1, mode, rows, :].astype(F32)
+            wr, wi = window[0, rows, :].astype(F32), window[1, rows, :].astype(F32)
+            wave = jnp.concatenate([(pr * wr - pi * wi).astype(BF), (pr * wi + pi * wr).astype(BF)], axis=1)
+            result = dot(wave, right_ref[...]).astype(BF)
+            turned[mode, rows, :] = result[:, :frame_len]
+            turned[mode, low_rows, :] = result[:, frame_len:]
+
+    for out, base in ((send_ref, (1 - core) * block), (keep_ref, core * block)):
+        rows = pl.ds(pl.multiple_of(base, block), block)
+        low_rows = pl.ds(pl.multiple_of(base + frame_len, block), block)
+        total = jnp.zeros((block, frame_len), F32)
+        for mode in range(modes):
+            for part, part_rows in ((0, rows), (1, low_rows)):
+                value = dot(left_ref[part_rows, :], turned[mode]).astype(BF)
+                far_ref[mode, part, rows, :] = value
+                wide = value.astype(F32)
+                total = total + wide * wide
+        out[...] = total
+    own_rows = pl.ds(pl.multiple_of(half * chunk, chunk), chunk)
+    keep_ref[own_rows, :] = keep_ref[own_rows, :] - measured_ref[...]
+
+
+def backward_kernel(
+    place_ref, far_ref, probe_ref, mine_ref, mates_ref, right_ref, left_ref,
+    send_ref, side_ref, keep_ref, misfit, weighted, turned, grad,
+):
+    column, core, half = place_ref[0], place_ref[1], place_ref[4]
+    modes, frame_len = far_ref.shape[0], far_ref.shape[3]
+    block = frame_len // 2
+    piece_len = keep_ref.shape[1]
+    misfit[pl.ds(pl.multiple_of(core * block, block), block), :] = mine_ref[...]
+    misfit[pl.ds(pl.multiple_of((1 - core) * block, block), block), :] = mates_ref[...]
+    for mode in range(modes):
+        for part in range(2):
+            weighted[mode, part * frame_len : (part + 1) * frame_len, :] = (
+                misfit[...] * far_ref[mode, part].astype(F32)
+            ).astype(BF)
+        for index in range(2):
+            rows = slice(index * block, (index + 1) * block)
+            for part in range(2):
+                value = dot(right_ref[part * frame_len + index * block : part * frame_len + (index + 1) * block, :], weighted[mode])
+                turned[mode, rows, part * frame_len : (part + 1) * frame_len] = value.astype(BF)
+
+    @pl.loop(0, 2)
+    def _(index):
+        rows = pl.ds(pl.multiple_of(index * block, block), block)
+        real, imag = jnp.zeros((block, frame_len), F32), jnp.zeros((block, frame_len), F32)
+        for mode in range(modes):
+            back = dot(turned[mode, rows, :], left_ref[...])
+            br, bi = back[:, :frame_len], back[:, frame_len:]
+            pr, pi = probe_ref[0, mode, rows, :].astype(F32), probe_ref[1, mode, rows, :].astype(F32)
+            real = real + (pr * br + pi * bi)
+            imag = imag + (pr * bi - pi * br)
+        grad[0, rows, :] = (4.0 * real).astype(BF)
+        grad[1, rows, :] = (4.0 * imag).astype(BF)
+
+    for target, pair in ((0, 1 - core), (1, core)):
+        for flip in range(2):
+            base = (2 * pair + lax.bitwise_xor(half, 1 - flip)) * piece_len
+            table = shift_table(piece_len, frame_len, base, column)
+            for part in range(2):
+                value = dot(table, grad[part], ((1,), (1,))).astype(BF)
+                if target == 0:
+                    send_ref[flip, part] = value
+                elif flip == 0:
+                    side_ref[part] = value
+                else:
+                    keep_ref[part] = value
+
+
+PAIRS = [("sy", i, j) for j in range(HIST - 1) for i in range(HIST)]
+PAIRS += [("ss", i, i) for i in range(HIST)]
+PAIRS += [("yy", i, j) for j in range(HIST - 1) for i in range(j + 1)]
+OLD_PAIRS = len(PAIRS)
+PAIRS += [("sy", i, HIST - 1) for i in range(HIST)]
+PAIRS += [("yy", i, HIST - 1) for i in range(HIST)]
+PAIRS += [("sg", i, i) for i in range(HIST)]
+PAIRS += [("yg", i, i) for i in range(HIST)]
+SLOT = {pair: index for index, pair in enumerate(PAIRS)}
+
+
+def folded(value):
+    parts, rows, columns = value.shape
+    total = jnp.sum(value.reshape(parts * rows // 8, 8, columns), axis=0)
+    return sum(total[:, start : start + LANES] for start in range(0, columns, LANES))
+
+
+def add_products(sums, first, slots, vectors):
+    for slot, pair in slots:
+        kind, i, j = pair
+        left = vectors[kind[0]][i]
+        right = vectors["g"][0] if kind[1] == "g" else vectors[kind[1]][j]
+        value = folded(left * right)
+        sums[slot] = jnp.where(first, value, sums[slot] + value)
+
+
+def lane_row(sums, count):
+    rows = [jnp.sum(sums[slot], axis=0, keepdims=True) for slot in range(count)]
+    square = jnp.concatenate(rows + [jnp.zeros((LANES - count, LANES), F32)], axis=0)
+    return jnp.sum(square.T, axis=0, keepdims=True)
+
+
+def old_kernel(steps_ref, changes_ref, out_ref, sums):
+    step = pl.program_id(0)
+    vectors = {
+        "s": [steps_ref[index] for index in range(HIST)],
+        "y": [changes_ref[index] for index in range(HIST - 1)],
+    }
+    add_products(sums, step == 0, list(enumerate(PAIRS[:OLD_PAIRS])), vectors)
+
+    @pl.when(step == pl.num_programs(0) - 1)
+    def _():
+        out_ref[...] = lane_row(sums, OLD_PAIRS)
+
+
+def gradient_kernel(
+    pos_ref, data_ref, transmission_ref, old_ref, steps_ref, changes_ref, row_ref, gradient_ref, out_ref, sums
+):
+    step = pl.program_id(0)
+    table = shift_table(data_ref.shape[2], transmission_ref.shape[2], pos_ref[0, 0], 0)
+    parts = [
+        dot(data_ref[part], table) + TIKHONOV * transmission_ref[part] for part in range(2)
+    ]
+    gradient = jnp.stack(parts)
+    gradient_ref[...] = gradient
+    vectors = {
+        "s": [steps_ref[index] for index in range(HIST)],
+        "y": [changes_ref[index] for index in range(HIST - 1)] + [gradient - old_ref[...]],
+        "g": [gradient],
+    }
+    slots = [(index, pair) for index, pair in enumerate(PAIRS[OLD_PAIRS:])]
+    add_products(sums, step == 0, slots, vectors)
+
+    @pl.when(step == pl.num_programs(0) - 1)
+    def _():
+        fresh = pltpu.roll(lane_row(sums, len(PAIRS) - OLD_PAIRS), OLD_PAIRS, 1)
+        out_ref[...] = jnp.broadcast_to(fresh + row_ref[...], out_ref.shape)
+
+
+def update_kernel(
+    rows_ref, transmission_ref, gradient_ref, old_ref, steps_ref, changes_ref, out_ref, factors
+):
+    width = factors.shape[1]
+
+    @pl.when(pl.program_id(0) == 0)
+    def _():
+        row = jnp.sum(rows_ref[...], axis=0, keepdims=True)
+        lane = lax.broadcasted_iota(jnp.int32, row.shape, 1)
+
+        def get(kind, i, j):
+            if kind == "yy" and i > j:
+                i, j = j, i
+            picked = jnp.where(lane == SLOT[(kind, i, j)], row, 0.0)
+            return jnp.broadcast_to(jnp.sum(picked, axis=1, keepdims=True), row.shape)
+
+        last = HIST - 1
+        floors = [
+            jnp.maximum(get("sy", index, index), CURVE_FLOOR * get("ss", index, index)) for index in range(HIST)
+        ]
+        weights = [1.0 / floor for floor in floors]
+        alphas = [None] * HIST
+        for index in reversed(range(HIST)):
+            value = get("sg", index, index)
+            for later in range(index + 1, HIST):
+                value = value - alphas[later] * get("sy", index, later)
+            alphas[index] = weights[index] * value
+        scale = floors[last] / (get("yy", last, last) + EPSILON)
+        moves = []
+        for index in range(HIST):
+            value = get("yg", index, index)
+            for other in range(HIST):
+                value = value - alphas[other] * get("yy", index, other)
+            value = scale * value
+            for before in range(index):
+                value = value + moves[before] * get("sy", before, index)
+            moves.append(alphas[index] - weights[index] * value)
+        table = [scale] + [-scale * alpha for alpha in alphas] + moves
+        for index, value in enumerate(table):
+            factors[index : index + 1, :] = jnp.concatenate([value] * (width // LANES), axis=1)
+
+    def factor(index):
+        return factors[index : index + 1, :]
+
+    for part in range(2):
+        gradient = gradient_ref[part]
+        total = factor(0) * gradient + factor(HIST) * (gradient - old_ref[part])
+        for index in range(HIST - 1):
+            total = total + factor(1 + index) * changes_ref[index, part]
+        for index in range(HIST):
+            total = total + factor(1 + HIST + index) * steps_ref[index, part]
+        out_ref[part] = transmission_ref[part] - total
+
+
+def call(body, outs, scratch=(), limit=48, smem=(), count=0, cost=None):
+    specs = [
+        pl.BlockSpec(memory_space=pltpu.SMEM if index in smem else pltpu.VMEM) for index in range(count)
+    ]
+    return pl.pallas_call(
+        body,
+        out_shape=outs,
+        in_specs=specs,
+        out_specs=jax.tree.map(lambda _: pl.BlockSpec(memory_space=pltpu.VMEM), outs),
+        scratch_shapes=list(scratch),
+        compiler_params=pltpu.CompilerParams(vmem_limit_bytes=limit * MIB),
+        cost_estimate=cost,
+    )
+
+
+def cost(flops, moved):
+    return pl.CostEstimate(flops=int(flops), bytes_accessed=int(moved), transcendentals=0)
+
+
+def routes(mesh, target):
+    regions, members = mesh.shape["region"], mesh.shape["grp"]
+    pairs = []
+    for region in range(regions):
+        for member in range(members):
+            to_region, to_member = target(region, member)
+            pairs.append((region * members + member, to_region * members + to_member))
+    return pairs
+
+
+def home(region, member):
+    if region % 2 == member // 2:
+        return region, member
+    return region ^ 1, member ^ 2
+
+
+def fast(mesh, transmission, probe, measured, positions, past_steps, past_changes, old_gradient):
+    def send(value, target):
+        return lax.ppermute(value, AXES, routes(mesh, target))
+
+    near = lambda region, member: (region, member ^ 1)
+    far = lambda region, member: (region, member ^ 2)
+    cross = lambda region, member: (region, member ^ 3)
+    mate = lambda region, member: (region ^ 1, member)
+    along_x = lambda region, member: (region ^ 2, member)
+    along_y = lambda region, member: (region ^ 4, member)
+
+    region, member = lax.axis_index("region"), lax.axis_index("grp")
+    core, half, line = region % 2, member % 2, (region // 2) % 4
+    chunk, frame_len = probe.shape[2], probe.shape[3]
+    piece_len, tile_len = transmission.shape[1], transmission.shape[2]
+    size = jax.ShapeDtypeStruct
+
+    part, which = line % 2, line // 2
+    base = 4 * core + 2 * half
+    other_base = 4 * core + 2 * (1 - half)
+
+    def block(mode):
+        return lax.dynamic_slice(probe, (part, mode, 0, 0), (1, 1, chunk, frame_len)).reshape(chunk, frame_len)
+
+    same_block, flip_block = block(base + which), block(other_base + which)
+    fetched = [send(flip_block, near), send(same_block, far), send(flip_block, cross)]
+    mine = lax.dynamic_slice(probe, (0, base, 0, 0), (2, 2, chunk, frame_len))
+    q0 = jnp.concatenate(fetched, axis=0)
+    q1, q2 = send(q0, along_x), send(q0, along_y)
+    cut = q0.shape[0] // 2
+    q3a, q3b = send(q2[:cut], along_x), send(q1[cut:], along_y)
+
+    piece = call(cut_kernel, size((2, piece_len, frame_len), BF), count=2, smem=(0,), limit=16)(
+        positions, transmission
+    )
+    own = send(piece, home)
+    side = send(own, near)
+    mates = send(jnp.stack([own, side]), mate)
+    target = send(measured[0], home)
+    mate_positions = send(positions, mate)
+    column = jnp.where(core == member // 2, positions[0, 1], mate_positions[0, 1])
+    place = jnp.stack([column, core, member, line, half]).astype(jnp.int32)
+
+    right, left = (jnp.asarray(table) for table in propagators(frame_len))
+    half_len = frame_len // 2
+    flops = 2 * 2 * 2 * frame_len * 4 * frame_len * frame_len
+    field = size((2, 2, frame_len, frame_len), BF)
+    partial = size((half_len, frame_len), F32)
+    far_field, whole_probe, sent, kept = call(
+        forward_kernel,
+        (field, field, partial, partial),
+        [
+            pltpu.VMEM((2, tile_len, frame_len), BF),
+            pltpu.VMEM((2, frame_len, frame_len), BF),
+            pltpu.VMEM((2, 2 * frame_len, frame_len), BF),
+        ],
+        count=13,
+        smem=(0,),
+        cost=cost(flops, 16 * MIB),
+    )(place, own, side, mates, mine, q0, q1, q2, q3a, q3b, target, right, left)
+
+    chip = kept + send(sent, mate)
+    misfit = chip + send(chip.astype(BF), near).astype(F32)
+    mates_misfit = send(misfit, mate)
+
+    piece_shape = size((2, piece_len, frame_len), BF)
+    sent, kept_side, kept = call(
+        backward_kernel,
+        (size((2, 2, piece_len, frame_len), BF), piece_shape, piece_shape),
+        [
+            pltpu.VMEM((frame_len, frame_len), F32),
+            pltpu.VMEM((2, 2 * frame_len, frame_len), BF),
+            pltpu.VMEM((2, frame_len, 2 * frame_len), BF),
+            pltpu.VMEM((2, frame_len, frame_len), BF),
+        ],
+        count=7,
+        smem=(0,),
+        cost=cost(flops, 12 * MIB),
+    )(place, far_field, whole_probe, misfit, mates_misfit, right, left)
+    met = send(sent, mate)
+    add = lambda a, b: (a.astype(F32) + b.astype(F32)).astype(BF)
+    data = add(add(kept, met[1]), send(add(kept_side, met[0]), near))
+    data = send(data, home)
+
+    steps = 5
+    rows = piece_len // steps
+    whole = lambda *dims: pl.BlockSpec(dims, lambda index: (0,) * len(dims))
+    vector = pl.BlockSpec((2, rows, tile_len), lambda index: (0, index, 0))
+    window = pl.BlockSpec((2, rows, frame_len), lambda index: (0, index, 0))
+    history = lambda count: pl.BlockSpec((count, 2, rows, tile_len), lambda index: (0, 0, index, 0))
+    params = pltpu.CompilerParams(vmem_limit_bytes=32 * MIB)
+    moved = 4 * 2 * piece_len * tile_len
+    old_row = pl.pallas_call(
+        old_kernel,
+        out_shape=size((1, LANES), F32),
+        grid=(steps,),
+        in_specs=[history(HIST), history(HIST - 1)],
+        out_specs=whole(1, LANES),
+        scratch_shapes=[pltpu.VMEM((OLD_PAIRS, 8, LANES), F32)],
+        compiler_params=params,
+        cost_estimate=cost(22 * moved, 7 * moved),
+    )(past_steps, past_changes)
+    devices = mesh.shape["region"] * mesh.shape["grp"]
+    gradient, row = pl.pallas_call(
+        gradient_kernel,
+        out_shape=(size(transmission.shape, F32), size((devices, LANES), F32)),
+        grid=(steps,),
+        in_specs=[
+            pl.BlockSpec(memory_space=pltpu.SMEM),
+            window,
+            vector,
+            vector,
+            history(HIST),
+            history(HIST - 1),
+            whole(1, LANES),
+        ],
+        out_specs=(vector, whole(devices, LANES)),
+        scratch_shapes=[pltpu.VMEM((len(PAIRS) - OLD_PAIRS, 8, LANES), F32)],
+        compiler_params=params,
+        cost_estimate=cost(16 * moved, 10 * moved),
+    )(positions, data, transmission, old_gradient, past_steps, past_changes, old_row)
+    all_rows = lax.all_to_all(
+        row.reshape(devices, 1, LANES), AXES, split_axis=0, concat_axis=0, tiled=True
+    ).reshape(devices, LANES)
+    updated = pl.pallas_call(
+        update_kernel,
+        out_shape=size(transmission.shape, F32),
+        grid=(steps,),
+        in_specs=[whole(devices, LANES), vector, vector, vector, history(HIST), history(HIST - 1)],
+        out_specs=vector,
+        scratch_shapes=[pltpu.VMEM((16, tile_len), F32)],
+        compiler_params=params,
+        cost_estimate=cost(10 * moved, 11 * moved),
+    )(all_rows, transmission, gradient, old_gradient, past_steps, past_changes)
+    return (updated, gradient)
+
+
 def solution(mesh):
+    split = mesh.shape["grp"] == 4 and mesh.shape["region"] == 8
+
+    def shards(*args):
+        probe, positions, past_steps = args[1], args[3], args[4]
+        sized = probe.shape[1] == 8 and positions.shape[0] == 1 and past_steps.shape[0] == HIST
+        if split and sized:
+            return fast(mesh, *args)
+        return general(*args)
+
     return jax.shard_map(
         shards,
         mesh=mesh,

time: 921 us -> 131 us (0.14); the launches traced: 910 us -> 131 us
  blocking collectives: 477 us -> 21.3 us
  matrix products: 197 us -> 0 us
  waiting for transfers between devices: 116 us -> 34.3 us
  other arithmetic: 48.3 us -> 1.27 us
  local copies, waits for them, and re-layouts: 40.1 us -> 7.69 us
  Pallas kernels: 0 us -> 31.6 us
  starting transfers between devices: 3.69 us -> 32.7 us
  between operations: 28.5 us -> 2.1 us
    psum x8 -> x0, blocking collectives: 323 us -> none  [the longest x4 162 us: shards(): lax.psum(jnp.sum(changes[index] * direction), ('region', 'grp'))]
    dot_general x32 -> x0, matrix products: 197 us -> none  [the longest x16 102 us: single(): jnp.einsum('jk,...kc->...jc', left, right, preferred_element_type=jnp.flo...]
    all_to_all x3 -> x1, blocking collectives: 155 us -> 21.3 us  [fast(): lax.all_to_all(row.reshape(devices, 1, LANES), AXES, split_axis=0, concat...]
    all_to_all x1 -> x0, waiting for transfers between devices: 47.1 us -> none  [shards(): lax.all_to_all(weighted, 'grp', split_axis=3, concat_axis=2, tiled=True)]
    reduce_scatter x1 -> x0, waiting for transfers between devices: 35 us -> none  [shards(): lax.psum_scatter(scattered.astype(jnp.bfloat16), 'grp', scatter_dimension...]
    ppermute x0 -> x18, waiting for transfers between devices: none -> 34.3 us  [send(): return lax.ppermute(value, AXES, routes(mesh, target))]
    all_gather x1 -> x0, waiting for transfers between devices: 33.8 us -> none  [shards(): lax.all_gather(transmission.astype(jnp.bfloat16), 'grp', axis=1, tiled=True)]
    ppermute x0 -> x18, starting transfers between devices: none -> 32.7 us  [send(): return lax.ppermute(value, AXES, routes(mesh, target))]
  transfers between devices with their start and end apart: 3 -> 18, of which waited for: 3 -> 9; matrix products, arithmetic and copies ran while one was open for 1% -> 4% of each run, Pallas kernels for 0% -> 2%
where the time goes in v1:
time: 131 us
  waiting for transfers between devices  34.3 us (26%)
  starting transfers between devices  32.7 us (25%)
  Pallas kernels  31.6 us (24%)
  blocking collectives  21.3 us (16%)
  local copies, waits for them, and re-layouts  7.69 us (6%)
  between operations  2.1 us (2%)
    ppermute x18, waiting for transfers between devices, send(): return lax.ppermute(value, AXES, routes(mesh, target))  34.3 us
    ppermute x18, starting transfers between devices, send(): return lax.ppermute(value, AXES, routes(mesh, target))  32.7 us
    all_to_all x1, blocking collectives, fast(): lax.all_to_all(row.reshape(devices, 1, LANES), AXES, split_axis=0, concat...  21.3 us
    pallas_call x1, Pallas kernels, fast(): call(forward_kernel, (field, field, partial, partial), [pltpu.VMEM((2, ti...  10.8 us
    pallas_call x1, Pallas kernels, fast(): call(backward_kernel, (size((2, 2, piece_len, frame_len), BF), piece_shap...  10.3 us
    pallas_call x1, Pallas kernels, fast(): pl.pallas_call(gradient_kernel, out_shape=(size(transmission.shape, F32),...  4.58 us
    unnamed x20, local copies, waits for them, and re-layouts  2.99 us
    pallas_call x1, Pallas kernels, fast(): pl.pallas_call(update_kernel, out_shape=size(transmission.shape, F32), gr...  2.9 us
  transfers between devices with their start and end apart: 18, of which 9 were waited for; matrix products, arithmetic and copies ran while one was open for 4% of the time, Pallas kernels for 2%

profile of v1, /device:TPU:0, one launch (start us, length us, event | category | flops | bytes accessed | tf_op | source)
XLA Modules:
  0.0 130.9 jit_solution(9887609113443513881)
XLA Ops:
  0.6 0.0 copy-start.2
  0.6 1.1 copy-done.2
  1.8 0.7 copy-done.6
  2.4 1.0 shard_map.104
  3.5 0.7 collective-permute-start.1
  4.2 1.0 dynamic-slice_bitcast_fusion
  5.2 3.1 %collective-permute-start.4 = (bf16[128,512]{1,0:T(8,128)(2,1)S(1)}, bf16[128,512]{1,0:T(8,128)(2,1)S(1)}, u32[]{:S(2)}, u32[]{:S(2)}) collective-permute-start(bf16[128,512]{1,0:T(8,128)(2,1)S(1)} %get-tuple-element.23), channel_id=1, source_target_pairs={{0,1},{1,0},{2,3},{3,2},{4,5},{5,4},{6,7},{7,6},{8,9},{9,8},{10,11... | collective-permute-start | bytes 393224 | tf_op jit(solution)/shard_map/ppermute | solution.py:492
  8.3 0.0 collective-permute-done.1.own_ref
  8.3 0.1 collective-permute-start.2
  8.4 13.5 %collective-permute-start.5 = (bf16[128,512]{1,0:T(8,128)(2,1)S(1)}, bf16[128,512]{1,0:T(8,128)(2,1)S(1)}, u32[]{:S(2)}, u32[]{:S(2)}) collective-permute-start(bf16[128,512]{1,0:T(8,128)(2,1)S(1)} %get-tuple-element.22), channel_id=1, source_target_pairs={{0,2},{1,3},{2,0},{3,1},{4,6},{5,7},{6,4},{7,5},{8,10},{9,11},{10,... | collective-permute-start | bytes 393224 | tf_op jit(solution)/shard_map/ppermute | solution.py:492
  21.9 0.0 collective-permute-start.6
  21.9 0.0 collective-permute-done.4
  21.9 6.1 %collective-permute-done.5 = bf16[128,512]{1,0:T(8,128)(2,1)S(1)} collective-permute-done((bf16[128,512]{1,0:T(8,128)(2,1)S(1)}, bf16[128,512]{1,0:T(8,128)(2,1)S(1)}, u32[]{:S(2)}, u32[]{:S(2)}) %collective-permute-start.5) | collective-permute-done | bytes 131104 | tf_op jit(solution)/shard_map/ppermute | solution.py:492
  28.0 0.0 collective-permute-done.2.side_ref
  28.0 0.9 pad_maximum_fusion
  28.9 0.0 collective-permute-start.3
  28.9 2.6 %collective-permute-done.6 = bf16[128,512]{1,0:T(8,128)(2,1)S(1)} collective-permute-done((bf16[128,512]{1,0:T(8,128)(2,1)S(1)}, bf16[128,512]{1,0:T(8,128)(2,1)S(1)}, u32[]{:S(2)}, u32[]{:S(2)}) %collective-permute-start.6) | collective-permute-done | bytes 131104 | tf_op jit(solution)/shard_map/ppermute | solution.py:492
  31.5 1.6 %collective-permute-start.7 = (bf16[384,512]{1,0:T(8,128)(2,1)S(1)}, bf16[384,512]{1,0:T(8,128)(2,1)S(1)}, u32[]{:S(2)}, u32[]{:S(2)}) collective-permute-start(bf16[384,512]{1,0:T(8,128)(2,1)S(1)} %constant_dynamic-update-slice_fusion.q0_ref), channel_id=1, source_target_pairs={{0,8},{1,9},{2,10},{3,11},{4,12},{5,13},{6,14},{7,15},{8,0},{9,1},... | collective-permute-start | bytes 1179656 | tf_op jit(solution)/shard_map/ppermute | solution.py:492
  33.1 1.5 %collective-permute-start.8 = (bf16[384,512]{1,0:T(8,128)(2,1)S(1)}, bf16[384,512]{1,0:T(8,128)(2,1)S(1)}, u32[]{:S(2)}, u32[]{:S(2)}) collective-permute-start(bf16[384,512]{1,0:T(8,128)(2,1)S(1)} %constant_dynamic-update-slice_fusion.q0_ref), channel_id=1, source_target_pairs={{0,16},{1,17},{2,18},{3,19},{4,20},{5,21},{6,22},{7,23},{8,24},{9,... | collective-permute-start | bytes 1179656 | tf_op jit(solution)/shard_map/ppermute | solution.py:492
  34.6 1.6 %collective-permute-start.11 = (f32[128,512]{1,0:T(8,128)}, f32[128,512]{1,0:T(8,128)S(1)}, u32[]{:S(2)}, u32[]{:S(2)}) collective-permute-start(f32[128,512]{1,0:T(8,128)} %bitcast.11), channel_id=1, source_target_pairs={{0,0},{1,1},{2,4},{3,5},{4,2},{5,3},{6,6},{7,7},{8,8},{9,9},{10,12... | collective-permute-start | bytes 786440 | tf_op jit(solution)/shard_map/ppermute | solution.py:492
  36.2 4.3 %collective-permute-done.7.q1_ref = bf16[384,512]{1,0:T(8,128)(2,1)S(1)} collective-permute-done((bf16[384,512]{1,0:T(8,128)(2,1)S(1)}, bf16[384,512]{1,0:T(8,128)(2,1)S(1)}, u32[]{:S(2)}, u32[]{:S(2)}) %collective-permute-start.7) | collective-permute-done | bytes 393248 | tf_op jit(solution)/shard_map/ppermute | solution.py:492
  40.5 0.7 slice.25
  41.2 1.5 %collective-permute-start.10 = (bf16[192,512]{1,0:T(8,128)(2,1)}, bf16[192,512]{1,0:T(8,128)(2,1)S(1)}, u32[]{:S(2)}, u32[]{:S(2)}) collective-permute-start(bf16[192,512]{1,0:T(8,128)(2,1)} %slice.25), channel_id=1, source_target_pairs={{0,16},{1,17},{2,18},{3,19},{4,20},{5,21},{6,22},{7,23},{8,24},{9,... | collective-permute-start | bytes 589832 | tf_op jit(solution)/shard_map/ppermute | solution.py:492
  42.7 0.0 collective-permute-done.8.q2_ref
  42.7 0.7 slice.24
  43.4 1.5 %collective-permute-start.9 = (bf16[192,512]{1,0:T(8,128)(2,1)}, bf16[192,512]{1,0:T(8,128)(2,1)}, u32[]{:S(2)}, u32[]{:S(2)}) collective-permute-start(bf16[192,512]{1,0:T(8,128)(2,1)} %slice.24), channel_id=1, source_target_pairs={{0,8},{1,9},{2,10},{3,11},{4,12},{5,13},{6,14},{7,15},{8,0},{9,1},... | collective-permute-start | bytes 589832 | tf_op jit(solution)/shard_map/ppermute | solution.py:492
  44.9 0.0 copy-done.7
  44.9 0.0 collective-permute-start
  44.9 0.6 slice.18
  45.5 1.1 constant_dynamic-slice_fusion.mine_ref
  46.5 0.0 collective-permute-done
  46.5 0.6 slice.19
  48.3 0.1 stack.32.place_ref
  48.4 0.0 collective-permute-done.11.measured_ref
  48.4 0.0 collective-permute-done.10.q3b_ref
  48.4 1.0 collective-permute-done.9.q3a_ref
  49.4 0.0 collective-permute-done.3.mates_ref
  49.4 10.8 %shard_map.105 = (bf16[2,2,512,512]{3,2,1,0:T(8,128)(2,1)}, bf16[2,2,512,512]{3,2,1,0:T(8,128)(2,1)}, f32[256,512]{1,0:T(8,128)S(1)}, f32[256,512]{1,0:T(8,128)S(1)}) custom-call(s32[5]{0:T(128)S(1)} %stack.32.place_ref, bf16[2,160,512]{2,1,0:T(8,128)(2,1)S(1)} %collective-permute-done.1.own_ref, bf16[2,160,512]{2,1,0:T(8,128)(2,1)S(1)} %collective-permute-done.2.side_ref, ...), custom_call_target="tpu_custom_call" | custom-call | flops 4294967296 | bytes 16777216 | tf_op jit(solution)/shard_map/pallas_call | solution.py:538
  60.2 0.0 collective-permute-start.12
  60.2 1.9 %collective-permute-done.12 = f32[256,512]{1,0:T(8,128)S(1)} collective-permute-done((f32[256,512]{1,0:T(8,128)S(1)}, f32[256,512]{1,0:T(8,128)S(1)}, u32[]{:S(2)}, u32[]{:S(2)}) %collective-permute-start.12) | collective-permute-done | bytes 524320 | tf_op jit(solution)/shard_map/ppermute | solution.py:492
  62.1 0.1 fusion.2
  62.2 4.7 %collective-permute-start.13 = (bf16[256,512]{1,0:T(8,128)(2,1)S(1)}, bf16[256,512]{1,0:T(8,128)(2,1)S(1)}, u32[]{:S(2)}, u32[]{:S(2)}) collective-permute-start(bf16[256,512]{1,0:T(8,128)(2,1)S(1)} %get-tuple-element.20), channel_id=1, source_target_pairs={{0,1},{1,0},{2,3},{3,2},{4,5},{5,4},{6,7},{7,6},{8,9},{9,8},{10,11... | collective-permute-start | bytes 786440 | tf_op jit(solution)/shard_map/ppermute | solution.py:492
  66.9 6.6 %collective-permute-done.13 = bf16[256,512]{1,0:T(8,128)(2,1)S(1)} collective-permute-done((bf16[256,512]{1,0:T(8,128)(2,1)S(1)}, bf16[256,512]{1,0:T(8,128)(2,1)S(1)}, u32[]{:S(2)}, u32[]{:S(2)}) %collective-permute-start.13) | collective-permute-done | bytes 262176 | tf_op jit(solution)/shard_map/ppermute | solution.py:492
  73.5 0.1 convert_add_fusion.2.mine_ref
  73.6 0.1 collective-permute-start.14
  73.7 1.9 %collective-permute-done.14.mates_ref = f32[256,512]{1,0:T(8,128)S(1)} collective-permute-done((f32[256,512]{1,0:T(8,128)S(1)}, f32[256,512]{1,0:T(8,128)S(1)}, u32[]{:S(2)}, u32[]{:S(2)}) %collective-permute-start.14) | collective-permute-done | bytes 524320 | tf_op jit(solution)/shard_map/ppermute | solution.py:492
  75.6 0.0 copy-done.8
  75.6 10.3 %shard_map.106 = (bf16[2,2,160,512]{3,2,1,0:T(8,128)(2,1)S(1)}, bf16[2,160,512]{2,1,0:T(8,128)(2,1)S(1)}, bf16[2,160,512]{2,1,0:T(8,128)(2,1)S(1)}) custom-call(s32[5]{0:T(128)S(1)} %stack.32.place_ref, bf16[2,2,512,512]{3,2,1,0:T(8,128)(2,1)S(1)} %copy-done.8, bf16[2,2,512,512]{3,2,1,0:T(8,128)(2,1)} %get-tuple-element.12.probe_ref, ...), custom_call_target="tpu_custom_call" | custom-call | flops 4294967296 | bytes 12582912 | tf_op jit(solution)/shard_map/pallas_call | solution.py:556
  85.9 0.2 collective-permute-start.15
  86.1 2.0 %collective-permute-done.15 = bf16[2,2,160,512]{3,2,1,0:T(8,128)(2,1)S(1)} collective-permute-done((bf16[2,2,160,512]{3,2,1,0:T(8,128)(2,1)S(1)}, bf16[2,2,160,512]{3,2,1,0:T(8,128)(2,1)S(1)}, u32[]{:S(2)}, u32[]{:S(2)}) %collective-permute-start.15) | collective-permute-done | bytes 655392 | tf_op jit(solution)/shard_map/ppermute | solution.py:492
  88.0 0.1 fusion
  88.1 1.8 %collective-permute-start.16 = (bf16[2,160,512]{2,1,0:T(8,128)(2,1)S(1)}, bf16[2,160,512]{2,1,0:T(8,128)(2,1)S(1)}, u32[]{:S(2)}, u32[]{:S(2)}) collective-permute-start(bf16[2,160,512]{2,1,0:T(8,128)(2,1)S(1)} %fusion), channel_id=1, source_target_pairs={{0,1},{1,0},{2,3},{3,2},{4,5},{5,4},{6,7},{7,6},{8,9},{9,8},{10,11... | collective-permute-start | bytes 983048 | tf_op jit(solution)/shard_map/ppermute | solution.py:492
  89.9 8.0 %collective-permute-done.16 = bf16[2,160,512]{2,1,0:T(8,128)(2,1)S(1)} collective-permute-done((bf16[2,160,512]{2,1,0:T(8,128)(2,1)S(1)}, bf16[2,160,512]{2,1,0:T(8,128)(2,1)S(1)}, u32[]{:S(2)}, u32[]{:S(2)}) %collective-permute-start.16) | collective-permute-done | bytes 327712 | tf_op jit(solution)/shard_map/ppermute | solution.py:492
  97.9 0.1 add_convert_fusion
  98.1 0.0 copy-start.3
  98.1 0.0 copy-start.4
  98.1 0.8 collective-permute-start.17
  98.9 0.0 copy-done
  98.9 2.0 %shard_map.107.row_ref = f32[1,128]{1,0:T(1,128)S(1)} custom-call(f32[4,2,160,640]{3,2,1,0:T(8,128)S(1)} %copy-done, f32[3,2,160,640]{3,2,1,0:T(8,128)S(1)} %copy-done.1), custom_call_target="tpu_custom_call" | custom-call | flops 18022400 | bytes 5734400 | tf_op jit(solution)/shard_map/pallas_call | solution.py:582
  101.0 0.0 collective-permute-done.17.data_ref
  101.0 4.6 %shard_map.108 = (f32[2,160,640]{2,1,0:T(8,128)}, f32[32,128]{1,0:T(8,128)S(1)}) custom-call(s32[1,2]{1,0:T(1,128)S(1)} %copy-done.7, bf16[2,160,512]{2,1,0:T(8,128)(2,1)S(1)} %collective-permute-done.17.data_ref, f32[2,160,640]{2,1,0:T(8,128)S(1)} %copy-done.3, f32[2,160,640]{2,1,0:T(8,128)S(1)} %copy-done.4, f32[4,2,160,640]{3,2,1,0:T(8,128)S(1)} %copy-done, ...), custom_call_target="tpu_custom_call" | custom-call | flops 13107200 | bytes 8192000 | tf_op jit(solution)/shard_map/pallas_call | solution.py:593
  105.6 21.3 %all_to_all.5 = f32[32,1,128]{2,1,0:T(1,128)S(1)} all-to-all(f32[32,1,128]{2,1,0:T(1,128)S(1)} %bitcast.31), channel_id=1, replica_groups=mesh['region'=8,'grp'=4] {'region','grp'}, dimensions={0} | all-to-all | bytes 32768 | tf_op jit(solution)/shard_map/all_to_all | solution.py:611
  126.9 1.1 copy-done.5
  128.0 2.9 %shard_map.109 = f32[2,160,640]{2,1,0:T(8,128)} custom-call(f32[32,128]{1,0:T(8,128)S(1)} %bitcast.30, f32[2,160,640]{2,1,0:T(8,128)S(1)} %copy-done.3, f32[2,160,640]{2,1,0:T(8,128)S(1)} %copy-done.5, f32[2,160,640]{2,1,0:T(8,128)S(1)} %copy-done.4, f32[4,2,160,640]{3,2,1,0:T(8,128)S(1)} %copy-done, f32[3,2,160,640]{3,2,1,0:T(8,128)S(1)} %copy-done.1), custom_call_target="tpu_custom_call" | custom-call | flops 8192000 | bytes 9011200 | tf_op jit(solution)/shard_map/pallas_call | solution.py:614
  (12 shorter events, 0.0 us)
Async XLA Ops:
  0.6 1.1 copy-start.2
  1.8 0.7 copy-start.6
  2.4 42.5 %copy-start.7 = (s32[1,2]{1,0:T(1,128)S(1)}, s32[1,2]{1,0:T(1,128)}, u32[]{:S(2)}) copy-start(s32[1,2]{1,0:T(1,128)} %pos_ref.3) | copy-start | bytes 28
  3.5 4.9 %collective-permute-start.1 = (bf16[2,160,512]{2,1,0:T(8,128)(2,1)S(1)}, bf16[2,160,512]{2,1,0:T(8,128)(2,1)S(1)}, u32[]{:S(2)}, u32[]{:S(2)}) collective-permute-start(bf16[2,160,512]{2,1,0:T(8,128)(2,1)S(1)} %shard_map.104), channel_id=1, source_target_pairs={{0,0},{1,1},{2,4},{3,5},{4,2},{5,3},{6,6},{7,7},{8,8},{9,9},{10,12... | collective-permute-start | bytes 983048 | tf_op jit(solution)/shard_map/ppermute | solution.py:492
  5.2 16.7 %collective-permute-start.4 = (bf16[128,512]{1,0:T(8,128)(2,1)S(1)}, bf16[128,512]{1,0:T(8,128)(2,1)S(1)}, u32[]{:S(2)}, u32[]{:S(2)}) collective-permute-start(bf16[128,512]{1,0:T(8,128)(2,1)S(1)} %get-tuple-element.23), channel_id=1, source_target_pairs={{0,1},{1,0},{2,3},{3,2},{4,5},{5,4},{6,7},{7,6},{8,9},{9,8},{10,11... | collective-permute-start | bytes 393224 | tf_op jit(solution)/shard_map/ppermute | solution.py:492
  8.3 19.7 %collective-permute-start.2 = (bf16[2,160,512]{2,1,0:T(8,128)(2,1)S(1)}, bf16[2,160,512]{2,1,0:T(8,128)(2,1)S(1)}, u32[]{:S(2)}, u32[]{:S(2)}) collective-permute-start(bf16[2,160,512]{2,1,0:T(8,128)(2,1)S(1)} %collective-permute-done.1.own_ref), channel_id=1, source_target_pairs={{0,1},{1,0},{2,3},{3,2},{4,5},{5,4},{6,7},{7,6},{8,9},{9,8},{10,11... | collective-permute-start | bytes 983048 | tf_op jit(solution)/shard_map/ppermute | solution.py:492
  8.4 19.6 %collective-permute-start.5 = (bf16[128,512]{1,0:T(8,128)(2,1)S(1)}, bf16[128,512]{1,0:T(8,128)(2,1)S(1)}, u32[]{:S(2)}, u32[]{:S(2)}) collective-permute-start(bf16[128,512]{1,0:T(8,128)(2,1)S(1)} %get-tuple-element.22), channel_id=1, source_target_pairs={{0,2},{1,3},{2,0},{3,1},{4,6},{5,7},{6,4},{7,5},{8,10},{9,11},{10,... | collective-permute-start | bytes 393224 | tf_op jit(solution)/shard_map/ppermute | solution.py:492
  21.9 9.6 %collective-permute-start.6 = (bf16[128,512]{1,0:T(8,128)(2,1)S(1)}, bf16[128,512]{1,0:T(8,128)(2,1)S(1)}, u32[]{:S(2)}, u32[]{:S(2)}) collective-permute-start(bf16[128,512]{1,0:T(8,128)(2,1)S(1)} %get-tuple-element.23), channel_id=1, source_target_pairs={{0,3},{1,2},{2,1},{3,0},{4,7},{5,6},{6,5},{7,4},{8,11},{9,10},{10,... | collective-permute-start | bytes 393224 | tf_op jit(solution)/shard_map/ppermute | solution.py:492
  28.9 20.5 %collective-permute-start.3 = (bf16[2,2,160,512]{3,2,1,0:T(8,128)(2,1)}, bf16[2,2,160,512]{3,2,1,0:T(8,128)(2,1)S(1)}, u32[]{:S(2)}, u32[]{:S(2)}) collective-permute-start(bf16[2,2,160,512]{3,2,1,0:T(8,128)(2,1)} %pad_maximum_fusion), channel_id=1, source_target_pairs={{0,4},{1,5},{2,6},{3,7},{4,0},{5,1},{6,2},{7,3},{8,12},{9,13},{10,... | collective-permute-start | bytes 1966088 | tf_op jit(solution)/shard_map/ppermute | solution.py:492
  31.5 9.0 %collective-permute-start.7 = (bf16[384,512]{1,0:T(8,128)(2,1)S(1)}, bf16[384,512]{1,0:T(8,128)(2,1)S(1)}, u32[]{:S(2)}, u32[]{:S(2)}) collective-permute-start(bf16[384,512]{1,0:T(8,128)(2,1)S(1)} %constant_dynamic-update-slice_fusion.q0_ref), channel_id=1, source_target_pairs={{0,8},{1,9},{2,10},{3,11},{4,12},{5,13},{6,14},{7,15},{8,0},{9,1},... | collective-permute-start | bytes 1179656 | tf_op jit(solution)/shard_map/ppermute | solution.py:492
  33.1 9.7 %collective-permute-start.8 = (bf16[384,512]{1,0:T(8,128)(2,1)S(1)}, bf16[384,512]{1,0:T(8,128)(2,1)S(1)}, u32[]{:S(2)}, u32[]{:S(2)}) collective-permute-start(bf16[384,512]{1,0:T(8,128)(2,1)S(1)} %constant_dynamic-update-slice_fusion.q0_ref), channel_id=1, source_target_pairs={{0,16},{1,17},{2,18},{3,19},{4,20},{5,21},{6,22},{7,23},{8,24},{9,... | collective-permute-start | bytes 1179656 | tf_op jit(solution)/shard_map/ppermute | solution.py:492
  34.6 13.9 %collective-permute-start.11 = (f32[128,512]{1,0:T(8,128)}, f32[128,512]{1,0:T(8,128)S(1)}, u32[]{:S(2)}, u32[]{:S(2)}) collective-permute-start(f32[128,512]{1,0:T(8,128)} %bitcast.11), channel_id=1, source_target_pairs={{0,0},{1,1},{2,4},{3,5},{4,2},{5,3},{6,6},{7,7},{8,8},{9,9},{10,12... | collective-permute-start | bytes 786440 | tf_op jit(solution)/shard_map/ppermute | solution.py:492
  41.2 7.2 %collective-permute-start.10 = (bf16[192,512]{1,0:T(8,128)(2,1)}, bf16[192,512]{1,0:T(8,128)(2,1)S(1)}, u32[]{:S(2)}, u32[]{:S(2)}) collective-permute-start(bf16[192,512]{1,0:T(8,128)(2,1)} %slice.25), channel_id=1, source_target_pairs={{0,16},{1,17},{2,18},{3,19},{4,20},{5,21},{6,22},{7,23},{8,24},{9,... | collective-permute-start | bytes 589832 | tf_op jit(solution)/shard_map/ppermute | solution.py:492
  43.4 6.0 %collective-permute-start.9 = (bf16[192,512]{1,0:T(8,128)(2,1)}, bf16[192,512]{1,0:T(8,128)(2,1)}, u32[]{:S(2)}, u32[]{:S(2)}) collective-permute-start(bf16[192,512]{1,0:T(8,128)(2,1)} %slice.24), channel_id=1, source_target_pairs={{0,8},{1,9},{2,10},{3,11},{4,12},{5,13},{6,14},{7,15},{8,0},{9,1},... | collective-permute-start | bytes 589832 | tf_op jit(solution)/shard_map/ppermute | solution.py:492
  44.9 1.6 %collective-permute-start = (s32[1,2]{1,0:T(1,128)S(1)}, s32[1,2]{1,0:T(1,128)S(1)}, u32[]{:S(2)}, u32[]{:S(2)}) collective-permute-start(s32[1,2]{1,0:T(1,128)S(1)} %copy-done.7), channel_id=1, source_target_pairs={{0,4},{1,5},{2,6},{3,7},{4,0},{5,1},{6,2},{7,3},{8,12},{9,13},{10,... | collective-permute-start | bytes 32 | tf_op jit(solution)/shard_map/ppermute | solution.py:492
  60.1 15.4 %copy-start.8 = (bf16[2,2,512,512]{3,2,1,0:T(8,128)(2,1)S(1)}, bf16[2,2,512,512]{3,2,1,0:T(8,128)(2,1)}, u32[]{:S(2)}) copy-start(bf16[2,2,512,512]{3,2,1,0:T(8,128)(2,1)} %get-tuple-element.11.far_ref) | copy-start | bytes 6291460
  60.2 1.9 %collective-permute-start.12 = (f32[256,512]{1,0:T(8,128)S(1)}, f32[256,512]{1,0:T(8,128)S(1)}, u32[]{:S(2)}, u32[]{:S(2)}) collective-permute-start(f32[256,512]{1,0:T(8,128)S(1)} %get-tuple-element.14), channel_id=1, source_target_pairs={{0,4},{1,5},{2,6},{3,7},{4,0},{5,1},{6,2},{7,3},{8,12},{9,13},{10,... | collective-permute-start | bytes 1572872 | tf_op jit(solution)/shard_map/ppermute | solution.py:492
  62.2 11.3 %collective-permute-start.13 = (bf16[256,512]{1,0:T(8,128)(2,1)S(1)}, bf16[256,512]{1,0:T(8,128)(2,1)S(1)}, u32[]{:S(2)}, u32[]{:S(2)}) collective-permute-start(bf16[256,512]{1,0:T(8,128)(2,1)S(1)} %get-tuple-element.20), channel_id=1, source_target_pairs={{0,1},{1,0},{2,3},{3,2},{4,5},{5,4},{6,7},{7,6},{8,9},{9,8},{10,11... | collective-permute-start | bytes 786440 | tf_op jit(solution)/shard_map/ppermute | solution.py:492
  73.6 2.0 %collective-permute-start.14 = (f32[256,512]{1,0:T(8,128)S(1)}, f32[256,512]{1,0:T(8,128)S(1)}, u32[]{:S(2)}, u32[]{:S(2)}) collective-permute-start(f32[256,512]{1,0:T(8,128)S(1)} %convert_add_fusion.2.mine_ref), channel_id=1, source_target_pairs={{0,4},{1,5},{2,6},{3,7},{4,0},{5,1},{6,2},{7,3},{8,12},{9,13},{10,... | collective-permute-start | bytes 1572872 | tf_op jit(solution)/shard_map/ppermute | solution.py:492
  75.6 23.4 %copy-start = (f32[4,2,160,640]{3,2,1,0:T(8,128)S(1)}, f32[4,2,160,640]{3,2,1,0:T(8,128)}, u32[]{:S(2)}) copy-start(f32[4,2,160,640]{3,2,1,0:T(8,128)} %steps_ref.5) | copy-start | bytes 9830404
  75.6 23.4 %copy-start.1 = (f32[3,2,160,640]{3,2,1,0:T(8,128)S(1)}, f32[3,2,160,640]{3,2,1,0:T(8,128)}, u32[]{:S(2)}) copy-start(f32[3,2,160,640]{3,2,1,0:T(8,128)} %changes_ref.5) | copy-start | bytes 7372804
  85.9 2.2 %collective-permute-start.15 = (bf16[2,2,160,512]{3,2,1,0:T(8,128)(2,1)S(1)}, bf16[2,2,160,512]{3,2,1,0:T(8,128)(2,1)S(1)}, u32[]{:S(2)}, u32[]{:S(2)}) collective-permute-start(bf16[2,2,160,512]{3,2,1,0:T(8,128)(2,1)S(1)} %get-tuple-element.16), channel_id=1, source_target_pairs={{0,4},{1,5},{2,6},{3,7},{4,0},{5,1},{6,2},{7,3},{8,12},{9,13},{10,... | collective-permute-start | bytes 1966088 | tf_op jit(solution)/shard_map/ppermute | solution.py:492
  88.1 9.8 %collective-permute-start.16 = (bf16[2,160,512]{2,1,0:T(8,128)(2,1)S(1)}, bf16[2,160,512]{2,1,0:T(8,128)(2,1)S(1)}, u32[]{:S(2)}, u32[]{:S(2)}) collective-permute-start(bf16[2,160,512]{2,1,0:T(8,128)(2,1)S(1)} %fusion), channel_id=1, source_target_pairs={{0,1},{1,0},{2,3},{3,2},{4,5},{5,4},{6,7},{7,6},{8,9},{9,8},{10,11... | collective-permute-start | bytes 983048 | tf_op jit(solution)/shard_map/ppermute | solution.py:492
  98.1 2.9 %copy-start.3 = (f32[2,160,640]{2,1,0:T(8,128)S(1)}, f32[2,160,640]{2,1,0:T(8,128)}, u32[]{:S(2)}) copy-start(f32[2,160,640]{2,1,0:T(8,128)} %transmission_ref.3) | copy-start | bytes 2457604
  98.1 2.9 %copy-start.4 = (f32[2,160,640]{2,1,0:T(8,128)S(1)}, f32[2,160,640]{2,1,0:T(8,128)}, u32[]{:S(2)}) copy-start(f32[2,160,640]{2,1,0:T(8,128)} %old_ref.3) | copy-start | bytes 2457604
  98.1 2.9 %collective-permute-start.17 = (bf16[2,160,512]{2,1,0:T(8,128)(2,1)S(1)}, bf16[2,160,512]{2,1,0:T(8,128)(2,1)S(1)}, u32[]{:S(2)}, u32[]{:S(2)}) collective-permute-start(bf16[2,160,512]{2,1,0:T(8,128)(2,1)S(1)} %add_convert_fusion), channel_id=1, source_target_pairs={{0,0},{1,1},{2,4},{3,5},{4,2},{5,3},{6,6},{7,7},{8,8},{9,9},{10,12... | collective-permute-start | bytes 983048 | tf_op jit(solution)/shard_map/ppermute | solution.py:492
  126.9 1.1 copy-start.5

commit v2 on v0

--- a/solution.py
+++ b/solution.py
@@ -2,13 +2,23 @@
 
 import jax
 import jax.numpy as jnp
+import ml_dtypes
+import numpy as np
 from jax import lax
+from jax.experimental import pallas as pl
+from jax.experimental.pallas import tpu as pltpu
 from jax.sharding import PartitionSpec as P
 
 TWO_PI = 2.0 * math.pi
 CURVE_FLOOR = 0.25
 TIKHONOV = 0.5
 EPSILON = 1e-06
+BF = jnp.bfloat16
+F32 = jnp.float32
+AXES = ("region", "grp")
+LANES = 128
+MIB = 1 << 20
+HIST = 4
 
 
 def dft_tables(count):
@@ -61,7 +71,7 @@
     )
 
 
-def shards(transmission, probe, measured, positions, past_steps, past_changes, old_gradient):
+def general(transmission, probe, measured, positions, past_steps, past_changes, old_gradient):
     member = lax.axis_index("grp")
     frame_len = probe.shape[3]
     rows_here = probe.shape[2]
@@ -170,7 +180,490 @@
     return (transmission - direction, gradient)
 
 
+def propagator(count):
+    index = np.arange(count, dtype=np.int64)
+    phase = (index[:, None] * index[None, :] % count).astype(np.float32) * np.float32(TWO_PI / count)
+    factor = np.float32(1.0 / math.sqrt(count))
+    table = (np.cos(phase) * factor).astype(ml_dtypes.bfloat16).astype(np.float64) + 1j * (
+        -np.sin(phase) * factor
+    ).astype(ml_dtypes.bfloat16).astype(np.float64)
+    wavenumber = (index + count // 2) % count - count // 2
+    chirp = np.exp(-1j * (wavenumber * wavenumber % (4 * count)) * (TWO_PI / (4 * count)))
+    folded = (table * chirp[None, :]) @ np.conj(table)
+    folded = 0.5 * (folded + folded.T)
+    real, imag = folded.real, folded.imag
+    return np.block([[real, imag], [-imag, real]]).astype(ml_dtypes.bfloat16)
+
+
+def dot(left, right, dims=((1,), (0,))):
+    return lax.dot_general(left, right, (dims, ((), ())), preferred_element_type=F32)
+
+
+def shift_table(rows, columns, row_base, column_base):
+    row = lax.broadcasted_iota(jnp.int32, (rows, columns), 0) + row_base
+    column = lax.broadcasted_iota(jnp.int32, (rows, columns), 1) + column_base
+    return jnp.where(row == column, 1.0, 0.0).astype(BF)
+
+
+def cut_kernel(pos_ref, tile_ref, out_ref):
+    tile_len, frame_len = tile_ref.shape[2], out_ref.shape[2]
+    table = shift_table(tile_len, frame_len, 0, pos_ref[0, 0])
+    for part in range(2):
+        out_ref[part] = dot(tile_ref[part].astype(BF), table).astype(BF)
+
+
+def probe_kernel(place_ref, all_ref, q0_ref, q1_ref, q2_ref, q3a_ref, q3b_ref, probe_ref, sem):
+    core, place, line, half = (place_ref[index] for index in range(4))
+    chunk = all_ref.shape[2]
+
+    def rows_of(step):
+        return pl.ds(pl.multiple_of(lax.bitwise_xor(place, step) * chunk, chunk), chunk)
+
+    copies = [
+        pltpu.make_async_copy(
+            all_ref.at[part, 4 * core + 2 * half + mode], probe_ref.at[part, mode, rows_of(0), :], sem.at[part, mode]
+        )
+        for part in range(2)
+        for mode in range(2)
+    ]
+    for copy in copies:
+        copy.start()
+    cut = q3a_ref.shape[0]
+    for turn, ref in ((0, q0_ref), (1, q1_ref), (2, q2_ref), (3, None)):
+        combo = lax.bitwise_xor(line, turn)
+        part, mode = lax.rem(combo, 2), lax.div(combo, 2)
+        for step in range(1, 4):
+            start = (step - 1) * chunk
+            if ref is not None:
+                value = ref[start : start + chunk]
+            elif start + chunk <= cut:
+                value = q3a_ref[start : start + chunk]
+            elif start >= cut:
+                value = q3b_ref[start - cut : start - cut + chunk]
+            else:
+                value = jnp.concatenate([q3a_ref[start:cut], q3b_ref[: start + chunk - cut]], axis=0)
+            probe_ref[part, mode, rows_of(step), :] = value
+    for copy in copies:
+        copy.wait()
+
+
+def forward_kernel(
+    place_ref, pos_ref, mate_pos_ref, own_ref, side_ref, mate_own_ref, mate_side_ref, probe_ref, measured_ref,
+    right_ref, far_ref, send_ref, keep_ref, tile, window_ref, wave, turned, total,
+):
+    core, half = place_ref[0], place_ref[3]
+    chunk, frame_len = measured_ref.shape
+    piece_len = own_ref.shape[1]
+    piece = 2 * core + half
+    for step, ref in enumerate((own_ref, side_ref, mate_own_ref, mate_side_ref)):
+        base = pl.multiple_of(lax.bitwise_xor(piece, step) * piece_len, piece_len)
+        for part in range(2):
+            tile[part, pl.ds(base, piece_len), :] = ref[part]
+    column = jnp.where(place_ref[4] == 1, pos_ref[0, 1], mate_pos_ref[0, 1])
+    table = shift_table(tile.shape[1], frame_len, 0, column)
+    for part in range(2):
+        window_ref[part] = dot(tile[part], table, ((0,), (0,))).astype(BF)
+
+    block = frame_len // 2
+    for mode in range(2):
+        rows = slice(mode * frame_len, (mode + 1) * frame_len)
+        pr, pi = probe_ref[0, mode].astype(F32), probe_ref[1, mode].astype(F32)
+        wr, wi = window_ref[0].astype(F32), window_ref[1].astype(F32)
+        wave[rows, :frame_len] = (pr * wr - pi * wi).astype(BF)
+        wave[rows, frame_len:] = (pr * wi + pi * wr).astype(BF)
+    for part in range(2):
+        for cell in range(2):
+            start = part * frame_len + cell * block
+            result = dot(wave[...], right_ref[:, start : start + block])
+            result = (result if part == 0 else -result).astype(BF)
+            for mode in range(2):
+                columns = slice(mode * frame_len + cell * block, mode * frame_len + (cell + 1) * block)
+                turned[part * frame_len : (part + 1) * frame_len, columns] = result[
+                    mode * frame_len : (mode + 1) * frame_len
+                ]
+    for mode in range(2):
+        for cell in range(2):
+            start = mode * frame_len + cell * block
+            columns = slice(cell * block, (cell + 1) * block)
+            result = dot(right_ref[...], turned[:, start : start + block])
+            real, imag = result[:frame_len].astype(BF), (-result[frame_len:]).astype(BF)
+            far_ref[mode, 0, :, columns] = real
+            far_ref[mode, 1, :, columns] = imag
+            real, imag = real.astype(F32), imag.astype(F32)
+            power = real * real + imag * imag
+            if mode == 0:
+                total[:, columns] = power
+            else:
+                total[:, columns] = total[:, columns] + power
+    send_ref[...] = total[pl.ds(pl.multiple_of((1 - core) * block, block), block), :]
+    keep_ref[...] = total[pl.ds(pl.multiple_of(core * block, block), block), :]
+    own_rows = pl.ds(pl.multiple_of(half * chunk, chunk), chunk)
+    keep_ref[own_rows, :] = keep_ref[own_rows, :] - measured_ref[...].astype(F32)
+
+
+def backward_kernel(
+    place_ref, pos_ref, mate_pos_ref, far_ref, probe_ref, mine_ref, mates_ref, right_ref,
+    send_ref, side_ref, keep_ref, misfit, weighted, turned, grad, table,
+):
+    core, half = place_ref[0], place_ref[3]
+    column = jnp.where(place_ref[4] == 1, pos_ref[0, 1], mate_pos_ref[0, 1])
+    frame_len = far_ref.shape[3]
+    block = frame_len // 2
+    piece_len = keep_ref.shape[1]
+    misfit[pl.ds(pl.multiple_of(core * block, block), block), :] = mine_ref[...]
+    misfit[pl.ds(pl.multiple_of((1 - core) * block, block), block), :] = mates_ref[...]
+    for mode in range(2):
+        for part in range(2):
+            weighted[part * frame_len : (part + 1) * frame_len, mode * frame_len : (mode + 1) * frame_len] = (
+                misfit[...] * far_ref[mode, part].astype(F32)
+            ).astype(BF)
+    for mode in range(2):
+        for cell in range(2):
+            start = mode * frame_len + cell * block
+            result = dot(right_ref[...], weighted[:, start : start + block])
+            for part in range(2):
+                columns = slice(part * frame_len + cell * block, part * frame_len + (cell + 1) * block)
+                value = result[part * frame_len : (part + 1) * frame_len]
+                turned[mode * frame_len : (mode + 1) * frame_len, columns] = (
+                    value if part == 0 else -value
+                ).astype(BF)
+    for cell in range(2):
+        columns = slice(cell * block, (cell + 1) * block)
+        back = [
+            dot(turned[...], right_ref[:, part * frame_len + cell * block : part * frame_len + (cell + 1) * block])
+            for part in range(2)
+        ]
+        real, imag = 0.0, 0.0
+        for mode in range(2):
+            br, bi = (value[mode * frame_len : (mode + 1) * frame_len] for value in back)
+            pr, pi = probe_ref[0, mode, :, columns].astype(F32), probe_ref[1, mode, :, columns].astype(F32)
+            real = real + (pr * br - pi * bi)
+            imag = imag + (pr * bi + pi * br)
+        grad[0, :, columns] = (4.0 * real).astype(BF)
+        grad[1, :, columns] = (-4.0 * imag).astype(BF)
+
+    slots = [(1 - core, 1), (1 - core, 0), (core, 1), (core, 0)]
+    for index, (pair, flip) in enumerate(slots):
+        base = (2 * pair + lax.bitwise_xor(half, flip)) * piece_len
+        table[index * piece_len : (index + 1) * piece_len, :] = shift_table(piece_len, frame_len, base, column)
+    for part in range(2):
+        value = dot(table[...], grad[part], ((1,), (1,))).astype(BF)
+        send_ref[0, part] = value[:piece_len]
+        send_ref[1, part] = value[piece_len : 2 * piece_len]
+        side_ref[part] = value[2 * piece_len : 3 * piece_len]
+        keep_ref[part] = value[3 * piece_len :]
+
+
+PAIRS = [("sy", i, j) for j in range(HIST - 1) for i in range(HIST)]
+PAIRS += [("ss", i, i) for i in range(HIST)]
+PAIRS += [("yy", i, j) for j in range(HIST - 1) for i in range(j + 1)]
+OLD_PAIRS = len(PAIRS)
+PAIRS += [("sy", i, HIST - 1) for i in range(HIST)]
+PAIRS += [("yy", i, HIST - 1) for i in range(HIST)]
+PAIRS += [("sg", i, i) for i in range(HIST)]
+PAIRS += [("yg", i, i) for i in range(HIST)]
+SLOT = {pair: index for index, pair in enumerate(PAIRS)}
+
+
+def folded(value):
+    parts, rows, columns = value.shape
+    total = jnp.sum(value.reshape(parts * rows // 8, 8, columns), axis=0)
+    return sum(total[:, start : start + LANES] for start in range(0, columns, LANES))
+
+
+def add_products(sums, first, slots, vectors):
+    for slot, pair in slots:
+        kind, i, j = pair
+        left = vectors[kind[0]][i]
+        right = vectors["g"][0] if kind[1] == "g" else vectors[kind[1]][j]
+        value = folded(left * right)
+        sums[slot] = value if first else sums[slot] + value
+
+
+def lane_row(sums, count):
+    rows = [jnp.sum(sums[slot], axis=0, keepdims=True) for slot in range(count)]
+    square = jnp.concatenate(rows + [jnp.zeros((LANES - count, LANES), F32)], axis=0)
+    return jnp.sum(square.T, axis=0, keepdims=True)
+
+
+BLOCK = 32
+
+
+def column_blocks(ref):
+    return range(0, ref.shape[-2], BLOCK)
+
+
+def old_kernel(steps_ref, changes_ref, out_ref, sums):
+    for start in column_blocks(steps_ref):
+        columns = slice(start, start + BLOCK)
+        vectors = {
+            "s": [steps_ref[index, :, columns] for index in range(HIST)],
+            "y": [changes_ref[index, :, columns] for index in range(HIST - 1)],
+        }
+        add_products(sums, start == 0, enumerate(PAIRS[:OLD_PAIRS]), vectors)
+    out_ref[...] = lane_row(sums, OLD_PAIRS)
+
+
+def gradient_kernel(
+    pos_ref, data_ref, transmission_ref, old_ref, steps_ref, changes_ref, row_ref, gradient_ref, again_ref, out_ref, sums
+):
+    table = shift_table(data_ref.shape[2], transmission_ref.shape[2], pos_ref[0, 0], 0)
+    for start in column_blocks(transmission_ref):
+        columns = slice(start, start + BLOCK)
+        gradient = jnp.stack(
+            [
+                dot(data_ref[part, columns], table) + TIKHONOV * transmission_ref[part, columns]
+                for part in range(2)
+            ]
+        )
+        gradient_ref[:, columns] = gradient
+        again_ref[:, columns] = gradient
+        vectors = {
+            "s": [steps_ref[index, :, columns] for index in range(HIST)],
+            "y": [changes_ref[index, :, columns] for index in range(HIST - 1)]
+            + [gradient - old_ref[:, columns]],
+            "g": [gradient],
+        }
+        add_products(sums, start == 0, enumerate(PAIRS[OLD_PAIRS:]), vectors)
+    fresh = pltpu.roll(lane_row(sums, len(PAIRS) - OLD_PAIRS), OLD_PAIRS, 1)
+    out_ref[...] = jnp.broadcast_to(fresh + row_ref[...], out_ref.shape)
+
+
+def update_kernel(rows_ref, transmission_ref, gradient_ref, old_ref, steps_ref, changes_ref, out_ref):
+    row = jnp.sum(rows_ref[...], axis=0, keepdims=True)
+    lane = lax.broadcasted_iota(jnp.int32, row.shape, 1)
+
+    def get(kind, i, j):
+        if kind == "yy" and i > j:
+            i, j = j, i
+        picked = jnp.where(lane == SLOT[(kind, i, j)], row, 0.0)
+        return jnp.broadcast_to(jnp.sum(picked, axis=1, keepdims=True), row.shape)
+
+    last = HIST - 1
+    floors = [
+        jnp.maximum(get("sy", index, index), CURVE_FLOOR * get("ss", index, index)) for index in range(HIST)
+    ]
+    weights = [1.0 / floor for floor in floors]
+    alphas = [None] * HIST
+    for index in reversed(range(HIST)):
+        value = get("sg", index, index)
+        for later in range(index + 1, HIST):
+            value = value - alphas[later] * get("sy", index, later)
+        alphas[index] = weights[index] * value
+    scale = floors[last] / (get("yy", last, last) + EPSILON)
+    moves = []
+    for index in range(HIST):
+        value = get("yg", index, index)
+        for other in range(HIST):
+            value = value - alphas[other] * get("yy", index, other)
+        value = scale * value
+        for before in range(index):
+            value = value + moves[before] * get("sy", before, index)
+        moves.append(alphas[index] - weights[index] * value)
+    repeat = out_ref.shape[-1] // LANES
+    wide = lambda value: jnp.concatenate([value] * repeat, axis=1)
+    scale_row = wide(scale)
+    change_rows = [wide(-scale * alpha) for alpha in alphas]
+    step_rows = [wide(move) for move in moves]
+    for part in range(2):
+        for start in column_blocks(out_ref):
+            columns = slice(start, start + BLOCK)
+            gradient = gradient_ref[part, columns]
+            total = scale_row * gradient + change_rows[last] * (gradient - old_ref[part, columns])
+            for index in range(HIST - 1):
+                total = total + change_rows[index] * changes_ref[index, part, columns]
+            for index in range(HIST):
+                total = total + step_rows[index] * steps_ref[index, part, columns]
+            out_ref[part, columns] = transmission_ref[part, columns] - total
+
+
+def call(body, outs, scratch=(), limit=48, smem=(), far=(), count=0, cost=None):
+    space = lambda index: pltpu.SMEM if index in smem else pl.ANY if index in far else pltpu.VMEM
+    specs = [pl.BlockSpec(memory_space=space(index)) for index in range(count)]
+    return pl.pallas_call(
+        body,
+        out_shape=outs,
+        in_specs=specs,
+        out_specs=jax.tree.map(lambda _: pl.BlockSpec(memory_space=pltpu.VMEM), outs),
+        scratch_shapes=list(scratch),
+        compiler_params=pltpu.CompilerParams(vmem_limit_bytes=limit * MIB),
+        cost_estimate=cost,
+    )
+
+
+def cost(flops, moved):
+    return pl.CostEstimate(flops=int(flops), bytes_accessed=int(moved), transcendentals=0)
+
+
+def home(region, member):
+    return (region, member) if at_home(region, member) else (region ^ 1, member ^ 2)
+
+
+def at_home(region, member):
+    return region % 2 == member // 2
+
+
+def away(region, member):
+    return not at_home(region, member)
+
+
+def fast(mesh, transmission, probe, measured, positions, past_steps, past_changes, old_gradient):
+    regions, members = mesh.shape["region"], mesh.shape["grp"]
+    barrier = lax.optimization_barrier
+
+    def send(value, target, chosen=lambda region, member: True):
+        pairs = []
+        for region in range(regions):
+            for member in range(members):
+                if chosen(region, member):
+                    to_region, to_member = target(region, member)
+                    pairs.append((region * members + member, to_region * members + to_member))
+        return lax.ppermute(value, AXES, pairs)
+
+    near = lambda region, member: (region, member ^ 1)
+    far = lambda region, member: (region, member ^ 2)
+    cross = lambda region, member: (region, member ^ 3)
+    mate = lambda region, member: (region ^ 1, member)
+    along_x = lambda region, member: (region ^ 2, member)
+    along_y = lambda region, member: (region ^ 4, member)
+    diagonal = lambda region, member: (region ^ 6, member)
+    home_near = lambda region, member: (region ^ 1, member ^ 3)
+
+    region, member = lax.axis_index("region"), lax.axis_index("grp")
+    core, half, line = region & 1, member & 1, (region >> 1) & 3
+    is_home = core == (member >> 1)
+    chunk, frame_len = probe.shape[2], probe.shape[3]
+    piece_len, tile_len = transmission.shape[1], transmission.shape[2]
+    size = jax.ShapeDtypeStruct
+    place = jnp.stack([core, member, line, half, is_home.astype(jnp.int32)]).astype(jnp.int32)
+
+    part, which = line & 1, line >> 1
+    base = 4 * core + 2 * half
+    other_base = 4 * core + 2 * (1 - half)
+
+    def block(mode):
+        return lax.dynamic_slice(probe, (part, mode, 0, 0), (1, 1, chunk, frame_len)).reshape(chunk, frame_len)
+
+    same_block, flip_block = block(base + which), block(other_base + which)
+    from_far, from_near = send(same_block, far), send(flip_block, near)
+    from_cross = send(flip_block, cross)
+    mate_positions = send(positions, mate)
+    piece = call(cut_kernel, size((2, piece_len, frame_len), BF), count=2, smem=(0,), limit=16)(
+        positions, transmission
+    )
+    measured_low, from_near = barrier((measured[0].astype(BF), from_near))
+    target = send(measured_low, home)
+    q0 = jnp.concatenate([from_near, from_far, from_cross], axis=0)
+    piece, place, mate_positions, target, q0 = barrier((piece, place, mate_positions, target, q0))
+    q1, q2 = send(q0, along_x), send(q0, along_y)
+    own = send(piece, home)
+    beside = send(piece, near, at_home)
+    further = send(piece, home_near, away)
+    cut = q0.shape[0] // 2
+    q3a, q3b = send(q2[:cut], along_x), send(q1[cut:], along_y)
+    own, beside, further, q3a, q3b = barrier((own, beside, further, q3a, q3b))
+    side = jnp.where(is_home, beside, further)
+    mate_own, mate_side = send(own, mate), send(side, mate)
+    whole_probe = call(
+        probe_kernel,
+        size((2, 2, frame_len, frame_len), BF),
+        [pltpu.SemaphoreType.DMA((2, 2))],
+        count=7,
+        smem=(0,),
+        far=(1,),
+        limit=16,
+    )(place, probe, q0, q1, q2, q3a, q3b)
+
+    right = jnp.asarray(propagator(frame_len))
+    double = 2 * frame_len
+    flops = 2 * 2 * double**3
+    field = size((2, 2, frame_len, frame_len), BF)
+    partial = size((frame_len // 2, frame_len), F32)
+    far_field, sent, kept = call(
+        forward_kernel,
+        (field, partial, partial),
+        [
+            pltpu.VMEM((2, tile_len, frame_len), BF),
+            pltpu.VMEM((2, frame_len, frame_len), BF),
+            pltpu.VMEM((double, double), BF),
+            pltpu.VMEM((double, double), BF),
+            pltpu.VMEM((frame_len, frame_len), F32),
+        ],
+        count=10,
+        smem=(0, 1, 2),
+        limit=24,
+        cost=cost(flops, 16 * MIB),
+    )(place, positions, mate_positions, own, side, mate_own, mate_side, whole_probe, target, right)
+
+    chip = kept + send(sent, mate)
+    misfit = chip + send(chip.astype(BF), near).astype(F32)
+    mates_misfit = send(misfit, mate)
+
+    piece_shape = size((2, piece_len, frame_len), BF)
+    sent, kept_side, kept = call(
+        backward_kernel,
+        (size((2, 2, piece_len, frame_len), BF), piece_shape, piece_shape),
+        [
+            pltpu.VMEM((frame_len, frame_len), F32),
+            pltpu.VMEM((double, double), BF),
+            pltpu.VMEM((double, double), BF),
+            pltpu.VMEM((2, frame_len, frame_len), BF),
+            pltpu.VMEM((4 * piece_len, frame_len), BF),
+        ],
+        count=8,
+        smem=(0, 1, 2),
+        limit=24,
+        cost=cost(flops, 12 * MIB),
+    )(place, positions, mate_positions, far_field, whole_probe, misfit, mates_misfit, right)
+    met = send(sent, mate)
+    add = lambda a, b: (a.astype(F32) + b.astype(F32)).astype(BF)
+    kept_side, kept = add(kept_side, met[0]), add(kept, met[1])
+    first, second = send(kept, home, away), send(kept_side, home_near, away)
+    beside = send(kept_side, near, at_home)
+    data = jnp.where(is_home, add(kept, beside), add(first, second))
+
+    devices = regions * members
+    moved = 4 * 2 * piece_len * tile_len
+    old_row = call(
+        old_kernel,
+        size((1, LANES), F32),
+        [pltpu.VMEM((OLD_PAIRS, 8, LANES), F32)],
+        count=2,
+        limit=16,
+        cost=cost(22 * moved, 7 * moved),
+    )(past_steps, past_changes)
+    gradient, again, row = call(
+        gradient_kernel,
+        (size(transmission.shape, F32), size(transmission.shape, F32), size((devices, LANES), F32)),
+        [pltpu.VMEM((len(PAIRS) - OLD_PAIRS, 8, LANES), F32)],
+        count=7,
+        smem=(0,),
+        limit=16,
+        cost=cost(16 * moved, 10 * moved),
+    )(positions, data, transmission, old_gradient, past_steps, past_changes, old_row)
+    all_rows = lax.all_to_all(
+        row.reshape(devices, 1, LANES), AXES, split_axis=0, concat_axis=0, tiled=True
+    ).reshape(devices, LANES)
+    updated = call(
+        update_kernel,
+        size(transmission.shape, F32),
+        count=6,
+        limit=16,
+        cost=cost(10 * moved, 11 * moved),
+    )(all_rows, transmission, again, old_gradient, past_steps, past_changes)
+    return (updated, gradient)
+
+
 def solution(mesh):
+    split = mesh.shape["grp"] == 4 and mesh.shape["region"] == 8
+
+    def shards(*args):
+        probe, positions, past_steps = args[1], args[3], args[4]
+        sized = probe.shape[1] == 8 and positions.shape[0] == 1 and past_steps.shape[0] == HIST
+        if split and sized:
+            return fast(mesh, *args)
+        return general(*args)
+
     return jax.shard_map(
         shards,
         mesh=mesh,

time: 921 us -> 107 us (0.12); the launches traced: 910 us -> 106 us
  blocking collectives: 477 us -> 16.9 us
  matrix products: 197 us -> 0 us
  waiting for transfers between devices: 116 us -> 30.5 us
  other arithmetic: 48.3 us -> 1.55 us
  local copies, waits for them, and re-layouts: 40.1 us -> 2.94 us
  starting transfers between devices: 3.69 us -> 31.6 us
  between operations: 28.5 us -> 0.91 us
  Pallas kernels: 0 us -> 21.8 us
    psum x8 -> x0, blocking collectives: 323 us -> none  [the longest x4 162 us: shards(): lax.psum(jnp.sum(changes[index] * direction), ('region', 'grp'))]
    dot_general x32 -> x0, matrix products: 197 us -> none  [the longest x16 102 us: single(): jnp.einsum('jk,...kc->...jc', left, right, preferred_element_type=jnp.flo...]
    all_to_all x3 -> x1, blocking collectives: 155 us -> 16.9 us  [fast(): lax.all_to_all(row.reshape(devices, 1, LANES), AXES, split_axis=0, concat...]
    all_to_all x1 -> x0, waiting for transfers between devices: 47.1 us -> none  [shards(): lax.all_to_all(weighted, 'grp', split_axis=3, concat_axis=2, tiled=True)]
    reduce_scatter x1 -> x0, waiting for transfers between devices: 35 us -> none  [shards(): lax.psum_scatter(scattered.astype(jnp.bfloat16), 'grp', scatter_dimension...]
    all_gather x1 -> x0, waiting for transfers between devices: 33.8 us -> none  [shards(): lax.all_gather(transmission.astype(jnp.bfloat16), 'grp', axis=1, tiled=True)]
    ppermute x0 -> x21, starting transfers between devices: none -> 31.6 us  [send(): return lax.ppermute(value, AXES, pairs)]
    ppermute x0 -> x21, waiting for transfers between devices: none -> 30.5 us  [send(): return lax.ppermute(value, AXES, pairs)]
  transfers between devices with their start and end apart: 3 -> 21, of which waited for: 3 -> 10; matrix products, arithmetic and copies ran while one was open for 1% -> 1% of each run, Pallas kernels for 0% -> 4%
where the time goes in v2:
time: 107 us; the launch traced here: 106 us
  starting transfers between devices  31.6 us (30%)
  waiting for transfers between devices  30.5 us (29%)
  Pallas kernels  21.8 us (20%)
  blocking collectives  16.9 us (16%)
  local copies, waits for them, and re-layouts  2.94 us (3%)
  other arithmetic  1.55 us (1%)
    ppermute x21, starting transfers between devices, send(): return lax.ppermute(value, AXES, pairs)  31.6 us
    ppermute x21, waiting for transfers between devices, send(): return lax.ppermute(value, AXES, pairs)  30.5 us
    all_to_all x1, blocking collectives, fast(): lax.all_to_all(row.reshape(devices, 1, LANES), AXES, split_axis=0, concat...  16.9 us
    pallas_call x1, Pallas kernels, fast(): call(forward_kernel, (field, partial, partial), [pltpu.VMEM((2, tile_len,...  6.34 us
    pallas_call x1, Pallas kernels, fast(): call(backward_kernel, (size((2, 2, piece_len, frame_len), BF), piece_shap...  6.25 us
    pallas_call x1, Pallas kernels, fast(): call(gradient_kernel, (size(transmission.shape, F32), size(transmission.s...  3.53 us
  transfers between devices with their start and end apart: 21, of which 10 were waited for; matrix products, arithmetic and copies ran while one was open for 1% of the time, Pallas kernels for 4%

profile of v2, /device:TPU:0, one launch (start us, length us, event | category | flops | bytes accessed | tf_op | source)
XLA Modules:
  0.0 106.3 jit_solution(9518474638883569266)
XLA Ops:
  0.6 1.0 dynamic-slice_bitcast_fusion
  1.6 3.1 %collective-permute-start.1 = (bf16[128,512]{1,0:T(8,128)(2,1)S(1)}, bf16[128,512]{1,0:T(8,128)(2,1)S(1)}, u32[]{:S(2)}, u32[]{:S(2)}) collective-permute-start(bf16[128,512]{1,0:T(8,128)(2,1)S(1)} %get-tuple-element.47), channel_id=1, source_target_pairs={{0,1},{1,0},{2,3},{3,2},{4,5},{5,4},{6,7},{7,6},{8,9},{9,8},{10,11... | collective-permute-start | bytes 393224 | tf_op jit(solution)/shard_map/ppermute | solution.py:521
  4.7 2.5 %collective-permute-start.4 = (bf16[128,512]{1,0:T(8,128)(2,1)S(1)}, bf16[128,512]{1,0:T(8,128)(2,1)S(1)}, u32[]{:S(2)}, u32[]{:S(2)}) collective-permute-start(bf16[128,512]{1,0:T(8,128)(2,1)S(1)} %get-tuple-element.47), channel_id=1, source_target_pairs={{0,3},{1,2},{2,1},{3,0},{4,7},{5,6},{6,5},{7,4},{8,11},{9,10},{10,... | collective-permute-start | bytes 393224 | tf_op jit(solution)/shard_map/ppermute | solution.py:521
  7.2 0.1 collective-permute-start.3
  7.3 1.0 convert_bitcast_fusion
  8.3 0.0 collective-permute-done.1
  8.3 0.7 collective-permute-start.2
  9.0 5.2 %collective-permute-start = (s32[1,2]{1,0:T(1,128)}, s32[1,2]{1,0:T(1,128)S(1)}, u32[]{:S(2)}, u32[]{:S(2)}) collective-permute-start(s32[1,2]{1,0:T(1,128)} %pos_ref.7), channel_id=1, source_target_pairs={{0,4},{1,5},{2,6},{3,7},{4,0},{5,1},{6,2},{7,3},{8,12},{9,13},{10,... | collective-permute-start | bytes 32 | tf_op jit(solution)/shard_map/ppermute | solution.py:521
  14.2 1.1 %copy-done.2 = f32[2,160,640]{2,1,0:T(8,128)S(1)} copy-done((f32[2,160,640]{2,1,0:T(8,128)S(1)}, f32[2,160,640]{2,1,0:T(8,128)}, u32[]{:S(2)}) %copy-start.2) | copy-done | bytes 819224
  15.4 0.7 copy-done.6
  16.0 1.0 shard_map.95
  17.0 0.1 stack.27.place_ref
  17.1 0.0 collective-permute-done.4
  17.1 3.2 %collective-permute-done.3 = bf16[128,512]{1,0:T(8,128)(2,1)S(1)} collective-permute-done((bf16[128,512]{1,0:T(8,128)(2,1)S(1)}, bf16[128,512]{1,0:T(8,128)(2,1)S(1)}, u32[]{:S(2)}, u32[]{:S(2)}) %collective-permute-start.3) | collective-permute-done | bytes 131104 | tf_op jit(solution)/shard_map/ppermute | solution.py:521
  20.4 0.0 collective-permute-done.mate_pos_ref
  20.4 0.0 collective-permute-done.2.measured_ref
  20.4 1.6 %collective-permute-start.10 = (bf16[384,512]{1,0:T(8,128)(2,1)S(1)}, bf16[384,512]{1,0:T(8,128)(2,1)S(1)}, u32[]{:S(2)}, u32[]{:S(2)}) collective-permute-start(bf16[384,512]{1,0:T(8,128)(2,1)S(1)} %pad_maximum_fusion.q0_ref), channel_id=1, source_target_pairs={{0,8},{1,9},{2,10},{3,11},{4,12},{5,13},{6,14},{7,15},{8,0},{9,1},... | collective-permute-start | bytes 1179656 | tf_op jit(solution)/shard_map/ppermute | solution.py:521
  22.0 1.5 %collective-permute-start.8 = (bf16[384,512]{1,0:T(8,128)(2,1)S(1)}, bf16[384,512]{1,0:T(8,128)(2,1)S(1)}, u32[]{:S(2)}, u32[]{:S(2)}) collective-permute-start(bf16[384,512]{1,0:T(8,128)(2,1)S(1)} %pad_maximum_fusion.q0_ref), channel_id=1, source_target_pairs={{0,16},{1,17},{2,18},{3,19},{4,20},{5,21},{6,22},{7,23},{8,24},{9,... | collective-permute-start | bytes 1179656 | tf_op jit(solution)/shard_map/ppermute | solution.py:521
  23.5 0.7 collective-permute-start.5
  24.2 2.9 %collective-permute-start.6 = (bf16[2,160,512]{2,1,0:T(8,128)(2,1)S(1)}, bf16[2,160,512]{2,1,0:T(8,128)(2,1)S(1)}, u32[]{:S(2)}, u32[]{:S(2)}) collective-permute-start(bf16[2,160,512]{2,1,0:T(8,128)(2,1)S(1)} %shard_map.95), channel_id=1, source_target_pairs={{0,1},{1,0},{6,7},{7,6},{8,9},{9,8},{14,15},{15,14},{16,17},{17,16... | collective-permute-start | bytes 983048 | tf_op jit(solution)/shard_map/ppermute | solution.py:521
  27.1 0.7 collective-permute-start.7
  27.8 4.6 %collective-permute-done.10.q1_ref = bf16[384,512]{1,0:T(8,128)(2,1)S(1)} collective-permute-done((bf16[384,512]{1,0:T(8,128)(2,1)S(1)}, bf16[384,512]{1,0:T(8,128)(2,1)S(1)}, u32[]{:S(2)}, u32[]{:S(2)}) %collective-permute-start.10) | collective-permute-done | bytes 393248 | tf_op jit(solution)/shard_map/ppermute | solution.py:521
  32.3 1.6 %collective-permute-start.11 = (bf16[192,512]{1,0:T(8,128)(2,1)S(1)}, bf16[192,512]{1,0:T(8,128)(2,1)S(1)}, u32[]{:S(2)}, u32[]{:S(2)}) collective-permute-start(bf16[192,512]{1,0:T(8,128)(2,1)S(1)} %slice.17), channel_id=1, source_target_pairs={{0,16},{1,17},{2,18},{3,19},{4,20},{5,21},{6,22},{7,23},{8,24},{9,... | collective-permute-start | bytes 589832 | tf_op jit(solution)/shard_map/ppermute | solution.py:521
  33.9 0.0 collective-permute-done.8.q2_ref
  34.0 1.6 %collective-permute-start.9 = (bf16[192,512]{1,0:T(8,128)(2,1)S(1)}, bf16[192,512]{1,0:T(8,128)(2,1)S(1)}, u32[]{:S(2)}, u32[]{:S(2)}) collective-permute-start(bf16[192,512]{1,0:T(8,128)(2,1)S(1)} %slice.16), channel_id=1, source_target_pairs={{0,8},{1,9},{2,10},{3,11},{4,12},{5,13},{6,14},{7,15},{8,0},{9,1},... | collective-permute-start | bytes 589832 | tf_op jit(solution)/shard_map/ppermute | solution.py:521
  35.5 0.0 collective-permute-done.5.own_ref
  35.5 0.0 collective-permute-done.6
  35.5 0.0 collective-permute-done.7
  35.5 4.0 %collective-permute-done.11.q3b_ref = bf16[192,512]{1,0:T(8,128)(2,1)S(1)} collective-permute-done((bf16[192,512]{1,0:T(8,128)(2,1)S(1)}, bf16[192,512]{1,0:T(8,128)(2,1)S(1)}, u32[]{:S(2)}, u32[]{:S(2)}) %collective-permute-start.11) | collective-permute-done | bytes 196640 | tf_op jit(solution)/shard_map/ppermute | solution.py:521
  39.5 1.3 %collective-permute-done.9.q3a_ref = bf16[192,512]{1,0:T(8,128)(2,1)S(1)} collective-permute-done((bf16[192,512]{1,0:T(8,128)(2,1)S(1)}, bf16[192,512]{1,0:T(8,128)(2,1)S(1)}, u32[]{:S(2)}, u32[]{:S(2)}) %collective-permute-start.9) | collective-permute-done | bytes 196640 | tf_op jit(solution)/shard_map/ppermute | solution.py:521
  40.8 0.0 copy-start.7
  40.9 0.0 copy-start.8
  40.9 0.1 collective-permute-start.13
  40.9 0.5 collective-permute-start.12
  41.4 1.4 %shard_map.96.probe_ref = bf16[2,2,512,512]{3,2,1,0:T(8,128)(2,1)S(1)} custom-call(s32[5]{0:T(128)S(1)} %stack.27.place_ref, bf16[2,8,128,512]{3,2,1,0:T(8,128)(2,1)S(1)} %copy-done.5, bf16[384,512]{1,0:T(8,128)(2,1)S(1)} %pad_maximum_fusion.q0_ref, bf16[384,512]{1,0:T(8,128)(2,1)S(1)} %collective-permute-done.10.q1_ref, ...), custom_call_target="tpu_custom_call" | custom-call | tf_op jit(solution)/shard_map/pallas_call | solution.py:567
  42.8 0.0 collective-permute-done.13.mate_side_ref
  42.8 0.2 collective-permute-done.12.mate_own_ref
  43.0 0.0 copy-done.7
  43.0 6.3 %shard_map.97 = (bf16[2,2,512,512]{3,2,1,0:T(8,128)(2,1)S(1)}, f32[256,512]{1,0:T(8,128)S(1)}, f32[256,512]{1,0:T(8,128)S(1)}) custom-call(s32[5]{0:T(128)S(1)} %stack.27.place_ref, s32[1,2]{1,0:T(1,128)S(1)} %copy-done.7, s32[1,2]{1,0:T(1,128)S(1)} %collective-permute-done.mate_pos_ref, bf16[2,160,512]{2,1,0:T(8,128)(2,1)S(1)} %collective-permute-done.5.own_ref, ...), custom_call_target="tpu_custom_call" | custom-call | flops 4294967296 | bytes 16777216 | tf_op jit(solution)/shard_map/pallas_call | solution.py:582
  49.4 0.2 collective-permute-start.14
  49.6 1.8 %collective-permute-done.14 = f32[256,512]{1,0:T(8,128)S(1)} collective-permute-done((f32[256,512]{1,0:T(8,128)S(1)}, f32[256,512]{1,0:T(8,128)S(1)}, u32[]{:S(2)}, u32[]{:S(2)}) %collective-permute-start.14) | collective-permute-done | bytes 524320 | tf_op jit(solution)/shard_map/ppermute | solution.py:521
  51.4 0.1 fusion.3
  51.5 3.3 %collective-permute-start.15 = (bf16[256,512]{1,0:T(8,128)(2,1)S(1)}, bf16[256,512]{1,0:T(8,128)(2,1)S(1)}, u32[]{:S(2)}, u32[]{:S(2)}) collective-permute-start(bf16[256,512]{1,0:T(8,128)(2,1)S(1)} %get-tuple-element.44), channel_id=1, source_target_pairs={{0,1},{1,0},{2,3},{3,2},{4,5},{5,4},{6,7},{7,6},{8,9},{9,8},{10,11... | collective-permute-start | bytes 786440 | tf_op jit(solution)/shard_map/ppermute | solution.py:521
  54.8 6.8 %collective-permute-done.15 = bf16[256,512]{1,0:T(8,128)(2,1)S(1)} collective-permute-done((bf16[256,512]{1,0:T(8,128)(2,1)S(1)}, bf16[256,512]{1,0:T(8,128)(2,1)S(1)}, u32[]{:S(2)}, u32[]{:S(2)}) %collective-permute-start.15) | collective-permute-done | bytes 262176 | tf_op jit(solution)/shard_map/ppermute | solution.py:521
  61.6 0.1 convert_add_fusion.2.mine_ref
  61.7 0.1 collective-permute-start.16
  61.8 1.9 %collective-permute-done.16.mates_ref = f32[256,512]{1,0:T(8,128)S(1)} collective-permute-done((f32[256,512]{1,0:T(8,128)S(1)}, f32[256,512]{1,0:T(8,128)S(1)}, u32[]{:S(2)}, u32[]{:S(2)}) %collective-permute-start.16) | collective-permute-done | bytes 524320 | tf_op jit(solution)/shard_map/ppermute | solution.py:521
  63.7 6.3 %shard_map.98 = (bf16[2,2,160,512]{3,2,1,0:T(8,128)(2,1)S(1)}, bf16[2,160,512]{2,1,0:T(8,128)(2,1)S(1)}, bf16[2,160,512]{2,1,0:T(8,128)(2,1)S(1)}) custom-call(s32[5]{0:T(128)S(1)} %stack.27.place_ref, s32[1,2]{1,0:T(1,128)S(1)} %copy-done.7, s32[1,2]{1,0:T(1,128)S(1)} %collective-permute-done.mate_pos_ref, ...), custom_call_target="tpu_custom_call" | custom-call | flops 4294967296 | bytes 12582912 | tf_op jit(solution)/shard_map/pallas_call | solution.py:603
  69.9 0.2 collective-permute-start.17
  70.1 2.0 %collective-permute-done.17 = bf16[2,2,160,512]{3,2,1,0:T(8,128)(2,1)S(1)} collective-permute-done((bf16[2,2,160,512]{3,2,1,0:T(8,128)(2,1)S(1)}, bf16[2,2,160,512]{3,2,1,0:T(8,128)(2,1)S(1)}, u32[]{:S(2)}, u32[]{:S(2)}) %collective-permute-start.17) | collective-permute-done | bytes 655392 | tf_op jit(solution)/shard_map/ppermute | solution.py:521
  72.1 0.2 fusion.1
  72.3 3.6 %collective-permute-start.18 = (bf16[2,160,512]{2,1,0:T(8,128)(2,1)S(1)}, bf16[2,160,512]{2,1,0:T(8,128)(2,1)S(1)}, u32[]{:S(2)}, u32[]{:S(2)}) collective-permute-start(bf16[2,160,512]{2,1,0:T(8,128)(2,1)S(1)} %get-tuple-element.49), channel_id=1, source_target_pairs={{0,1},{1,0},{6,7},{7,6},{8,9},{9,8},{14,15},{15,14},{16,17},{17,16... | collective-permute-start | bytes 983048 | tf_op jit(solution)/shard_map/ppermute | solution.py:521
  75.9 0.7 collective-permute-start.19
  76.6 0.9 collective-permute-start.20
  77.5 1.8 %shard_map.99.row_ref = f32[1,128]{1,0:T(1,128)S(1)} custom-call(f32[4,2,160,640]{3,2,1,0:T(8,128)S(1)} %copy-done, f32[3,2,160,640]{3,2,1,0:T(8,128)S(1)} %copy-done.1), custom_call_target="tpu_custom_call" | custom-call | flops 18022400 | bytes 5734400 | tf_op jit(solution)/shard_map/pallas_call | solution.py:627
  79.3 0.0 copy-start.3
  79.3 0.0 copy-start.4
  79.3 4.8 %collective-permute-done.18 = bf16[2,160,512]{2,1,0:T(8,128)(2,1)S(1)} collective-permute-done((bf16[2,160,512]{2,1,0:T(8,128)(2,1)S(1)}, bf16[2,160,512]{2,1,0:T(8,128)(2,1)S(1)}, u32[]{:S(2)}, u32[]{:S(2)}) %collective-permute-start.18) | collective-permute-done | bytes 327712 | tf_op jit(solution)/shard_map/ppermute | solution.py:521
  84.1 0.0 collective-permute-done.19
  84.1 0.0 collective-permute-done.20
  84.1 0.2 fusion.2.data_ref
  84.3 3.5 %shard_map.100 = (f32[2,160,640]{2,1,0:T(8,128)}, f32[2,160,640]{2,1,0:T(8,128)S(1)}, f32[32,128]{1,0:T(8,128)S(1)}) custom-call(s32[1,2]{1,0:T(1,128)S(1)} %copy-done.7, bf16[2,160,512]{2,1,0:T(8,128)(2,1)S(1)} %fusion.2.data_ref, f32[2,160,640]{2,1,0:T(8,128)S(1)} %copy-done.3, f32[2,160,640]{2,1,0:T(8,128)S(1)} %copy-done.4, ...), custom_call_target="tpu_custom_call" | custom-call | flops 13107200 | bytes 8192000 | tf_op jit(solution)/shard_map/pallas_call | solution.py:635
  87.8 16.9 %all_to_all.5 = f32[32,1,128]{2,1,0:T(1,128)S(1)} all-to-all(f32[32,1,128]{2,1,0:T(1,128)S(1)} %bitcast.26), channel_id=1, replica_groups=mesh['region'=8,'grp'=4] {'region','grp'}, dimensions={0} | all-to-all | bytes 32768 | tf_op jit(solution)/shard_map/all_to_all | solution.py:644
  104.7 1.6 %shard_map.101 = f32[2,160,640]{2,1,0:T(8,128)} custom-call(f32[32,128]{1,0:T(8,128)S(1)} %bitcast.25, f32[2,160,640]{2,1,0:T(8,128)S(1)} %copy-done.3, f32[2,160,640]{2,1,0:T(8,128)S(1)} %get-tuple-element.42.gradient_ref, f32[2,160,640]{2,1,0:T(8,128)S(1)} %copy-done.4, f32[4,2,160,640]{3,2,1,0:T(8,128)S(1)} %copy-done, f32[3,2,160,640]{3,2,1,0:T(8,128)S(1)} %copy-done.1), custom_call_target="tpu_custom_call" | custom-call | flops 8192000 | bytes 9011200 | tf_op jit(solution)/shard_map/pallas_call | solution.py:647
  (15 shorter events, 0.1 us)
Async XLA Ops:
  1.6 6.7 %collective-permute-start.1 = (bf16[128,512]{1,0:T(8,128)(2,1)S(1)}, bf16[128,512]{1,0:T(8,128)(2,1)S(1)}, u32[]{:S(2)}, u32[]{:S(2)}) collective-permute-start(bf16[128,512]{1,0:T(8,128)(2,1)S(1)} %get-tuple-element.47), channel_id=1, source_target_pairs={{0,1},{1,0},{2,3},{3,2},{4,5},{5,4},{6,7},{7,6},{8,9},{9,8},{10,11... | collective-permute-start | bytes 393224 | tf_op jit(solution)/shard_map/ppermute | solution.py:521
  4.7 12.4 %collective-permute-start.4 = (bf16[128,512]{1,0:T(8,128)(2,1)S(1)}, bf16[128,512]{1,0:T(8,128)(2,1)S(1)}, u32[]{:S(2)}, u32[]{:S(2)}) collective-permute-start(bf16[128,512]{1,0:T(8,128)(2,1)S(1)} %get-tuple-element.47), channel_id=1, source_target_pairs={{0,3},{1,2},{2,1},{3,0},{4,7},{5,6},{6,5},{7,4},{8,11},{9,10},{10,... | collective-permute-start | bytes 393224 | tf_op jit(solution)/shard_map/ppermute | solution.py:521
  7.2 13.2 %collective-permute-start.3 = (bf16[128,512]{1,0:T(8,128)(2,1)S(1)}, bf16[128,512]{1,0:T(8,128)(2,1)S(1)}, u32[]{:S(2)}, u32[]{:S(2)}) collective-permute-start(bf16[128,512]{1,0:T(8,128)(2,1)S(1)} %get-tuple-element.46), channel_id=1, source_target_pairs={{0,2},{1,3},{2,0},{3,1},{4,6},{5,7},{6,4},{7,5},{8,10},{9,11},{10,... | collective-permute-start | bytes 393224 | tf_op jit(solution)/shard_map/ppermute | solution.py:521
  8.3 12.1 %collective-permute-start.2 = (bf16[128,512]{1,0:T(8,128)(2,1)S(1)}, bf16[128,512]{1,0:T(8,128)(2,1)S(1)}, u32[]{:S(2)}, u32[]{:S(2)}) collective-permute-start(bf16[128,512]{1,0:T(8,128)(2,1)S(1)} %convert_bitcast_fusion), channel_id=1, source_target_pairs={{0,0},{1,1},{2,4},{3,5},{4,2},{5,3},{6,6},{7,7},{8,8},{9,9},{10,12... | collective-permute-start | bytes 393224 | tf_op jit(solution)/shard_map/ppermute | solution.py:521
  9.0 11.4 %collective-permute-start = (s32[1,2]{1,0:T(1,128)}, s32[1,2]{1,0:T(1,128)S(1)}, u32[]{:S(2)}, u32[]{:S(2)}) collective-permute-start(s32[1,2]{1,0:T(1,128)} %pos_ref.7), channel_id=1, source_target_pairs={{0,4},{1,5},{2,6},{3,7},{4,0},{5,1},{6,2},{7,3},{8,12},{9,13},{10,... | collective-permute-start | bytes 32 | tf_op jit(solution)/shard_map/ppermute | solution.py:521
  14.2 1.1 %copy-start.2 = (f32[2,160,640]{2,1,0:T(8,128)S(1)}, f32[2,160,640]{2,1,0:T(8,128)}, u32[]{:S(2)}) copy-start(f32[2,160,640]{2,1,0:T(8,128)} %transmission_ref.3) | copy-start | bytes 2457604
  15.4 0.7 copy-start.6
  16.0 25.4 %copy-start.5 = (bf16[2,8,128,512]{3,2,1,0:T(8,128)(2,1)S(1)}, bf16[2,8,128,512]{3,2,1,0:T(8,128)(2,1)}, u32[]{:S(2)}) copy-start(bf16[2,8,128,512]{3,2,1,0:T(8,128)(2,1)} %all_ref.1) | copy-start | bytes 6291460
  20.4 11.9 %collective-permute-start.10 = (bf16[384,512]{1,0:T(8,128)(2,1)S(1)}, bf16[384,512]{1,0:T(8,128)(2,1)S(1)}, u32[]{:S(2)}, u32[]{:S(2)}) collective-permute-start(bf16[384,512]{1,0:T(8,128)(2,1)S(1)} %pad_maximum_fusion.q0_ref), channel_id=1, source_target_pairs={{0,8},{1,9},{2,10},{3,11},{4,12},{5,13},{6,14},{7,15},{8,0},{9,1},... | collective-permute-start | bytes 1179656 | tf_op jit(solution)/shard_map/ppermute | solution.py:521
  22.0 12.0 %collective-permute-start.8 = (bf16[384,512]{1,0:T(8,128)(2,1)S(1)}, bf16[384,512]{1,0:T(8,128)(2,1)S(1)}, u32[]{:S(2)}, u32[]{:S(2)}) collective-permute-start(bf16[384,512]{1,0:T(8,128)(2,1)S(1)} %pad_maximum_fusion.q0_ref), channel_id=1, source_target_pairs={{0,16},{1,17},{2,18},{3,19},{4,20},{5,21},{6,22},{7,23},{8,24},{9,... | collective-permute-start | bytes 1179656 | tf_op jit(solution)/shard_map/ppermute | solution.py:521
  23.5 12.0 %collective-permute-start.5 = (bf16[2,160,512]{2,1,0:T(8,128)(2,1)S(1)}, bf16[2,160,512]{2,1,0:T(8,128)(2,1)S(1)}, u32[]{:S(2)}, u32[]{:S(2)}) collective-permute-start(bf16[2,160,512]{2,1,0:T(8,128)(2,1)S(1)} %shard_map.95), channel_id=1, source_target_pairs={{0,0},{1,1},{2,4},{3,5},{4,2},{5,3},{6,6},{7,7},{8,8},{9,9},{10,12... | collective-permute-start | bytes 983048 | tf_op jit(solution)/shard_map/ppermute | solution.py:521
  24.2 11.3 %collective-permute-start.6 = (bf16[2,160,512]{2,1,0:T(8,128)(2,1)S(1)}, bf16[2,160,512]{2,1,0:T(8,128)(2,1)S(1)}, u32[]{:S(2)}, u32[]{:S(2)}) collective-permute-start(bf16[2,160,512]{2,1,0:T(8,128)(2,1)S(1)} %shard_map.95), channel_id=1, source_target_pairs={{0,1},{1,0},{6,7},{7,6},{8,9},{9,8},{14,15},{15,14},{16,17},{17,16... | collective-permute-start | bytes 983048 | tf_op jit(solution)/shard_map/ppermute | solution.py:521
  27.1 8.5 %collective-permute-start.7 = (bf16[2,160,512]{2,1,0:T(8,128)(2,1)S(1)}, bf16[2,160,512]{2,1,0:T(8,128)(2,1)S(1)}, u32[]{:S(2)}, u32[]{:S(2)}) collective-permute-start(bf16[2,160,512]{2,1,0:T(8,128)(2,1)S(1)} %shard_map.95), channel_id=1, source_target_pairs={{2,5},{3,4},{4,3},{5,2},{10,13},{11,12},{12,11},{13,10},{18,21},{1... | collective-permute-start | bytes 983048 | tf_op jit(solution)/shard_map/ppermute | solution.py:521
  32.3 7.1 %collective-permute-start.11 = (bf16[192,512]{1,0:T(8,128)(2,1)S(1)}, bf16[192,512]{1,0:T(8,128)(2,1)S(1)}, u32[]{:S(2)}, u32[]{:S(2)}) collective-permute-start(bf16[192,512]{1,0:T(8,128)(2,1)S(1)} %slice.17), channel_id=1, source_target_pairs={{0,16},{1,17},{2,18},{3,19},{4,20},{5,21},{6,22},{7,23},{8,24},{9,... | collective-permute-start | bytes 589832 | tf_op jit(solution)/shard_map/ppermute | solution.py:521
  34.0 6.8 %collective-permute-start.9 = (bf16[192,512]{1,0:T(8,128)(2,1)S(1)}, bf16[192,512]{1,0:T(8,128)(2,1)S(1)}, u32[]{:S(2)}, u32[]{:S(2)}) collective-permute-start(bf16[192,512]{1,0:T(8,128)(2,1)S(1)} %slice.16), channel_id=1, source_target_pairs={{0,8},{1,9},{2,10},{3,11},{4,12},{5,13},{6,14},{7,15},{8,0},{9,1},... | collective-permute-start | bytes 589832 | tf_op jit(solution)/shard_map/ppermute | solution.py:521
  40.8 2.2 %copy-start.7 = (s32[1,2]{1,0:T(1,128)S(1)}, s32[1,2]{1,0:T(1,128)}, u32[]{:S(2)}) copy-start(s32[1,2]{1,0:T(1,128)} %pos_ref.7) | copy-start | bytes 28
  40.9 2.2 %copy-start.8 = (bf16[1024,1024]{1,0:T(8,128)(2,1)S(1)}, bf16[1024,1024]{1,0:T(8,128)(2,1)}, u32[]{:S(2)}) copy-start(bf16[1024,1024]{1,0:T(8,128)(2,1)} %constant.23.clone.right_ref) | copy-start | bytes 6291460
  40.9 2.0 %collective-permute-start.13 = (bf16[2,160,512]{2,1,0:T(8,128)(2,1)S(1)}, bf16[2,160,512]{2,1,0:T(8,128)(2,1)S(1)}, u32[]{:S(2)}, u32[]{:S(2)}) collective-permute-start(bf16[2,160,512]{2,1,0:T(8,128)(2,1)S(1)} %broadcast_select_fusion.side_ref), channel_id=1, source_target_pairs={{0,4},{1,5},{2,6},{3,7},{4,0},{5,1},{6,2},{7,3},{8,12},{9,13},{10,... | collective-permute-start | bytes 983048 | tf_op jit(solution)/shard_map/ppermute | solution.py:521
  40.9 2.1 %collective-permute-start.12 = (bf16[2,160,512]{2,1,0:T(8,128)(2,1)S(1)}, bf16[2,160,512]{2,1,0:T(8,128)(2,1)S(1)}, u32[]{:S(2)}, u32[]{:S(2)}) collective-permute-start(bf16[2,160,512]{2,1,0:T(8,128)(2,1)S(1)} %collective-permute-done.5.own_ref), channel_id=1, source_target_pairs={{0,4},{1,5},{2,6},{3,7},{4,0},{5,1},{6,2},{7,3},{8,12},{9,13},{10,... | collective-permute-start | bytes 983048 | tf_op jit(solution)/shard_map/ppermute | solution.py:521
  49.4 2.0 %collective-permute-start.14 = (f32[256,512]{1,0:T(8,128)S(1)}, f32[256,512]{1,0:T(8,128)S(1)}, u32[]{:S(2)}, u32[]{:S(2)}) collective-permute-start(f32[256,512]{1,0:T(8,128)S(1)} %get-tuple-element.37), channel_id=1, source_target_pairs={{0,4},{1,5},{2,6},{3,7},{4,0},{5,1},{6,2},{7,3},{8,12},{9,13},{10,... | collective-permute-start | bytes 1572872 | tf_op jit(solution)/shard_map/ppermute | solution.py:521
  51.5 10.2 %collective-permute-start.15 = (bf16[256,512]{1,0:T(8,128)(2,1)S(1)}, bf16[256,512]{1,0:T(8,128)(2,1)S(1)}, u32[]{:S(2)}, u32[]{:S(2)}) collective-permute-start(bf16[256,512]{1,0:T(8,128)(2,1)S(1)} %get-tuple-element.44), channel_id=1, source_target_pairs={{0,1},{1,0},{2,3},{3,2},{4,5},{5,4},{6,7},{7,6},{8,9},{9,8},{10,11... | collective-permute-start | bytes 786440 | tf_op jit(solution)/shard_map/ppermute | solution.py:521
  61.7 2.0 %collective-permute-start.16 = (f32[256,512]{1,0:T(8,128)S(1)}, f32[256,512]{1,0:T(8,128)S(1)}, u32[]{:S(2)}, u32[]{:S(2)}) collective-permute-start(f32[256,512]{1,0:T(8,128)S(1)} %convert_add_fusion.2.mine_ref), channel_id=1, source_target_pairs={{0,4},{1,5},{2,6},{3,7},{4,0},{5,1},{6,2},{7,3},{8,12},{9,13},{10,... | collective-permute-start | bytes 1572872 | tf_op jit(solution)/shard_map/ppermute | solution.py:521
  63.7 13.8 %copy-start = (f32[4,2,160,640]{3,2,1,0:T(8,128)S(1)}, f32[4,2,160,640]{3,2,1,0:T(8,128)}, u32[]{:S(2)}) copy-start(f32[4,2,160,640]{3,2,1,0:T(8,128)} %steps_ref.5) | copy-start | bytes 9830404
  63.7 13.8 %copy-start.1 = (f32[3,2,160,640]{3,2,1,0:T(8,128)S(1)}, f32[3,2,160,640]{3,2,1,0:T(8,128)}, u32[]{:S(2)}) copy-start(f32[3,2,160,640]{3,2,1,0:T(8,128)} %changes_ref.5) | copy-start | bytes 7372804
  69.9 2.2 %collective-permute-start.17 = (bf16[2,2,160,512]{3,2,1,0:T(8,128)(2,1)S(1)}, bf16[2,2,160,512]{3,2,1,0:T(8,128)(2,1)S(1)}, u32[]{:S(2)}, u32[]{:S(2)}) collective-permute-start(bf16[2,2,160,512]{3,2,1,0:T(8,128)(2,1)S(1)} %get-tuple-element.39), channel_id=1, source_target_pairs={{0,4},{1,5},{2,6},{3,7},{4,0},{5,1},{6,2},{7,3},{8,12},{9,13},{10,... | collective-permute-start | bytes 1966088 | tf_op jit(solution)/shard_map/ppermute | solution.py:521
  72.3 11.8 %collective-permute-start.18 = (bf16[2,160,512]{2,1,0:T(8,128)(2,1)S(1)}, bf16[2,160,512]{2,1,0:T(8,128)(2,1)S(1)}, u32[]{:S(2)}, u32[]{:S(2)}) collective-permute-start(bf16[2,160,512]{2,1,0:T(8,128)(2,1)S(1)} %get-tuple-element.49), channel_id=1, source_target_pairs={{0,1},{1,0},{6,7},{7,6},{8,9},{9,8},{14,15},{15,14},{16,17},{17,16... | collective-permute-start | bytes 983048 | tf_op jit(solution)/shard_map/ppermute | solution.py:521
  75.9 8.1 %collective-permute-start.19 = (bf16[2,160,512]{2,1,0:T(8,128)(2,1)S(1)}, bf16[2,160,512]{2,1,0:T(8,128)(2,1)S(1)}, u32[]{:S(2)}, u32[]{:S(2)}) collective-permute-start(bf16[2,160,512]{2,1,0:T(8,128)(2,1)S(1)} %get-tuple-element.48), channel_id=1, source_target_pairs={{2,4},{3,5},{4,2},{5,3},{10,12},{11,13},{12,10},{13,11},{18,20},{1... | collective-permute-start | bytes 983048 | tf_op jit(solution)/shard_map/ppermute | solution.py:521
  76.6 7.4 %collective-permute-start.20 = (bf16[2,160,512]{2,1,0:T(8,128)(2,1)S(1)}, bf16[2,160,512]{2,1,0:T(8,128)(2,1)S(1)}, u32[]{:S(2)}, u32[]{:S(2)}) collective-permute-start(bf16[2,160,512]{2,1,0:T(8,128)(2,1)S(1)} %get-tuple-element.49), channel_id=1, source_target_pairs={{2,5},{3,4},{4,3},{5,2},{10,13},{11,12},{12,11},{13,10},{18,21},{1... | collective-permute-start | bytes 983048 | tf_op jit(solution)/shard_map/ppermute | solution.py:521
  79.3 5.0 %copy-start.3 = (f32[2,160,640]{2,1,0:T(8,128)S(1)}, f32[2,160,640]{2,1,0:T(8,128)}, u32[]{:S(2)}) copy-start(f32[2,160,640]{2,1,0:T(8,128)} %transmission_ref.3) | copy-start | bytes 2457604
  79.3 5.0 %copy-start.4 = (f32[2,160,640]{2,1,0:T(8,128)S(1)}, f32[2,160,640]{2,1,0:T(8,128)}, u32[]{:S(2)}) copy-start(f32[2,160,640]{2,1,0:T(8,128)} %old_ref.3) | copy-start | bytes 2457604

commit v3 on v2

--- a/solution.py
+++ b/solution.py
@@ -248,8 +248,8 @@
 
 
 def forward_kernel(
-    place_ref, pos_ref, mate_pos_ref, own_ref, side_ref, mate_own_ref, mate_side_ref, probe_ref, measured_ref,
-    right_ref, far_ref, send_ref, keep_ref, tile, window_ref, wave, turned, total,
+    place_ref, own_ref, side_ref, mate_own_ref, mate_side_ref, probe_ref, measured_ref,
+    right_ref, turned_ref, far_ref, send_ref, tile, window_ref, wave, total,
 ):
     core, half = place_ref[0], place_ref[3]
     chunk, frame_len = measured_ref.shape
@@ -259,7 +259,7 @@
         base = pl.multiple_of(lax.bitwise_xor(piece, step) * piece_len, piece_len)
         for part in range(2):
             tile[part, pl.ds(base, piece_len), :] = ref[part]
-    column = jnp.where(place_ref[4] == 1, pos_ref[0, 1], mate_pos_ref[0, 1])
+    column = place_ref[4]
     table = shift_table(tile.shape[1], frame_len, 0, column)
     for part in range(2):
         window_ref[part] = dot(tile[part], table, ((0,), (0,))).astype(BF)
@@ -277,56 +277,79 @@
             result = dot(wave[...], right_ref[:, start : start + block])
             result = (result if part == 0 else -result).astype(BF)
             for mode in range(2):
-                columns = slice(mode * frame_len + cell * block, mode * frame_len + (cell + 1) * block)
-                turned[part * frame_len : (part + 1) * frame_len, columns] = result[
+                turned_ref[mode, cell, part * frame_len : (part + 1) * frame_len, :] = result[
                     mode * frame_len : (mode + 1) * frame_len
                 ]
+    far_columns(1 - core, turned_ref, right_ref, far_ref, total)
+    subtract(core, half, 1 - core, measured_ref, total)
+    send_ref[...] = total[...].astype(BF)
+
+
+def far_columns(cell, turned_ref, right_ref, far_ref, total):
+    frame_len = total.shape[0]
+    power = 0.0
     for mode in range(2):
-        for cell in range(2):
-            start = mode * frame_len + cell * block
-            columns = slice(cell * block, (cell + 1) * block)
-            result = dot(right_ref[...], turned[:, start : start + block])
-            real, imag = result[:frame_len].astype(BF), (-result[frame_len:]).astype(BF)
-            far_ref[mode, 0, :, columns] = real
-            far_ref[mode, 1, :, columns] = imag
-            real, imag = real.astype(F32), imag.astype(F32)
-            power = real * real + imag * imag
-            if mode == 0:
-                total[:, columns] = power
-            else:
-                total[:, columns] = total[:, columns] + power
-    send_ref[...] = total[pl.ds(pl.multiple_of((1 - core) * block, block), block), :]
-    keep_ref[...] = total[pl.ds(pl.multiple_of(core * block, block), block), :]
-    own_rows = pl.ds(pl.multiple_of(half * chunk, chunk), chunk)
-    keep_ref[own_rows, :] = keep_ref[own_rows, :] - measured_ref[...].astype(F32)
+        result = dot(right_ref[...], turned_ref[mode, cell])
+        real, imag = result[:frame_len].astype(BF), (-result[frame_len:]).astype(BF)
+        far_ref[mode, 0] = real
+        far_ref[mode, 1] = imag
+        real, imag = real.astype(F32), imag.astype(F32)
+        power = power + (real * real + imag * imag)
+    total[...] = power
+
+
+def subtract(core, half, cell, measured_ref, total):
+    chunk, block = measured_ref.shape[0], total.shape[1]
+    rows = pl.ds(pl.multiple_of((2 * core + half) * chunk, chunk), chunk)
+    wanted = jnp.where(cell == 0, measured_ref[:, :block], measured_ref[:, block:])
+    total[rows, :] = total[rows, :] - wanted.astype(F32)
+
+
+def rest_kernel(place_ref, turned_ref, measured_ref, right_ref, far_ref, total):
+    core, half = place_ref[0], place_ref[3]
+    far_columns(core, turned_ref, right_ref, far_ref, total)
+    subtract(core, half, core, measured_ref, total)
+
+
+def left_columns(misfit, far_ref, right_ref, weighted, store):
+    frame_len, block = misfit.shape
+    for mode in range(2):
+        for part in range(2):
+            weighted[part * frame_len : (part + 1) * frame_len, mode * block : (mode + 1) * block] = (
+                misfit * far_ref[mode, part].astype(F32)
+            ).astype(BF)
+        result = dot(right_ref[...], weighted[:, mode * block : (mode + 1) * block])
+        store(mode, 0, result[:frame_len].astype(BF))
+        store(mode, 1, (-result[frame_len:]).astype(BF))
+
+
+def own_kernel(far_ref, mine_ref, right_ref, out_ref, weighted):
+    frame_len = mine_ref.shape[0]
+
+    def store(mode, part, value):
+        out_ref[part, mode * frame_len : (mode + 1) * frame_len, :] = value
+
+    left_columns(mine_ref[...], far_ref, right_ref, weighted, store)
 
 
 def backward_kernel(
-    place_ref, pos_ref, mate_pos_ref, far_ref, probe_ref, mine_ref, mates_ref, right_ref,
-    send_ref, side_ref, keep_ref, misfit, weighted, turned, grad, table,
+    place_ref, far_ref, probe_ref, mates_ref, own_ref, right_ref,
+    send_ref, side_ref, keep_ref, weighted, turned, grad, table,
 ):
     core, half = place_ref[0], place_ref[3]
-    column = jnp.where(place_ref[4] == 1, pos_ref[0, 1], mate_pos_ref[0, 1])
-    frame_len = far_ref.shape[3]
-    block = frame_len // 2
+    column = place_ref[4]
+    frame_len, block = mates_ref.shape
     piece_len = keep_ref.shape[1]
-    misfit[pl.ds(pl.multiple_of(core * block, block), block), :] = mine_ref[...]
-    misfit[pl.ds(pl.multiple_of((1 - core) * block, block), block), :] = mates_ref[...]
-    for mode in range(2):
-        for part in range(2):
-            weighted[part * frame_len : (part + 1) * frame_len, mode * frame_len : (mode + 1) * frame_len] = (
-                misfit[...] * far_ref[mode, part].astype(F32)
-            ).astype(BF)
-    for mode in range(2):
-        for cell in range(2):
-            start = mode * frame_len + cell * block
-            result = dot(right_ref[...], weighted[:, start : start + block])
-            for part in range(2):
-                columns = slice(part * frame_len + cell * block, part * frame_len + (cell + 1) * block)
-                value = result[part * frame_len : (part + 1) * frame_len]
-                turned[mode * frame_len : (mode + 1) * frame_len, columns] = (
-                    value if part == 0 else -value
-                ).astype(BF)
+
+    def lanes(part, cell):
+        return pl.ds(pl.multiple_of(part * frame_len + cell * block, block), block)
+
+    def store(mode, part, value):
+        turned[mode * frame_len : (mode + 1) * frame_len, lanes(part, 1 - core)] = value
+
+    left_columns(mates_ref[...].astype(F32), far_ref, right_ref, weighted, store)
+    for part in range(2):
+        turned[:, lanes(part, core)] = own_ref[part]
     for cell in range(2):
         columns = slice(cell * block, (cell + 1) * block)
         back = [
@@ -405,7 +428,7 @@
 
 
 def gradient_kernel(
-    pos_ref, data_ref, transmission_ref, old_ref, steps_ref, changes_ref, row_ref, gradient_ref, again_ref, out_ref, sums
+    pos_ref, data_ref, transmission_ref, old_ref, steps_ref, changes_ref, row_ref, gradient_ref, out_ref, sums
 ):
     table = shift_table(data_ref.shape[2], transmission_ref.shape[2], pos_ref[0, 0], 0)
     for start in column_blocks(transmission_ref):
@@ -417,7 +440,6 @@
             ]
         )
         gradient_ref[:, columns] = gradient
-        again_ref[:, columns] = gradient
         vectors = {
             "s": [steps_ref[index, :, columns] for index in range(HIST)],
             "y": [changes_ref[index, :, columns] for index in range(HIST - 1)]
@@ -429,7 +451,7 @@
     out_ref[...] = jnp.broadcast_to(fresh + row_ref[...], out_ref.shape)
 
 
-def update_kernel(rows_ref, transmission_ref, gradient_ref, old_ref, steps_ref, changes_ref, out_ref):
+def update_kernel(rows_ref, transmission_ref, gradient_ref, old_ref, steps_ref, changes_ref, out_ref, copy_ref):
     row = jnp.sum(rows_ref[...], axis=0, keepdims=True)
     lane = lax.broadcasted_iota(jnp.int32, row.shape, 1)
 
@@ -469,6 +491,7 @@
         for start in column_blocks(out_ref):
             columns = slice(start, start + BLOCK)
             gradient = gradient_ref[part, columns]
+            copy_ref[part, columns] = gradient
             total = scale_row * gradient + change_rows[last] * (gradient - old_ref[part, columns])
             for index in range(HIST - 1):
                 total = total + change_rows[index] * changes_ref[index, part, columns]
@@ -535,7 +558,6 @@
     chunk, frame_len = probe.shape[2], probe.shape[3]
     piece_len, tile_len = transmission.shape[1], transmission.shape[2]
     size = jax.ShapeDtypeStruct
-    place = jnp.stack([core, member, line, half, is_home.astype(jnp.int32)]).astype(jnp.int32)
 
     part, which = line & 1, line >> 1
     base = 4 * core + 2 * half
@@ -554,7 +576,9 @@
     measured_low, from_near = barrier((measured[0].astype(BF), from_near))
     target = send(measured_low, home)
     q0 = jnp.concatenate([from_near, from_far, from_cross], axis=0)
-    piece, place, mate_positions, target, q0 = barrier((piece, place, mate_positions, target, q0))
+    column = jnp.where(is_home, positions[0, 1], mate_positions[0, 1])
+    place = jnp.stack([core, member, line, half, column]).astype(jnp.int32)
+    piece, place, target, q0 = barrier((piece, place, target, q0))
     q1, q2 = send(q0, along_x), send(q0, along_y)
     own = send(piece, home)
     beside = send(piece, near, at_home)
@@ -577,44 +601,59 @@
     right = jnp.asarray(propagator(frame_len))
     double = 2 * frame_len
     flops = 2 * 2 * double**3
-    field = size((2, 2, frame_len, frame_len), BF)
-    partial = size((frame_len // 2, frame_len), F32)
-    far_field, sent, kept = call(
+    half_len = frame_len // 2
+    half_field = size((2, 2, frame_len, half_len), BF)
+    turned, mates_far, sent = call(
         forward_kernel,
-        (field, partial, partial),
+        (size((2, 2, double, half_len), BF), half_field, size((frame_len, half_len), BF)),
         [
             pltpu.VMEM((2, tile_len, frame_len), BF),
             pltpu.VMEM((2, frame_len, frame_len), BF),
             pltpu.VMEM((double, double), BF),
-            pltpu.VMEM((double, double), BF),
-            pltpu.VMEM((frame_len, frame_len), F32),
+            pltpu.VMEM((frame_len, half_len), F32),
         ],
-        count=10,
-        smem=(0, 1, 2),
+        count=8,
+        smem=(0,),
         limit=24,
-        cost=cost(flops, 16 * MIB),
-    )(place, positions, mate_positions, own, side, mate_own, mate_side, whole_probe, target, right)
-
-    chip = kept + send(sent, mate)
+        cost=cost(3 * flops // 4, 16 * MIB),
+    )(place, own, side, mate_own, mate_side, whole_probe, target, right)
+    met = send(sent, mate)
+    own_far, kept = call(
+        rest_kernel,
+        (half_field, size((frame_len, half_len), F32)),
+        count=4,
+        smem=(0,),
+        limit=24,
+        cost=cost(flops // 4, 4 * MIB),
+    )(place, turned, target, right)
+
+    chip = kept + met.astype(F32)
     misfit = chip + send(chip.astype(BF), near).astype(F32)
-    mates_misfit = send(misfit, mate)
+    mates_misfit = send(misfit.astype(BF), mate)
+    own_left = call(
+        own_kernel,
+        size((2, double, half_len), BF),
+        [pltpu.VMEM((double, frame_len), BF)],
+        count=3,
+        limit=24,
+        cost=cost(flops // 4, 4 * MIB),
+    )(own_far, misfit, right)
 
     piece_shape = size((2, piece_len, frame_len), BF)
     sent, kept_side, kept = call(
         backward_kernel,
         (size((2, 2, piece_len, frame_len), BF), piece_shape, piece_shape),
         [
-            pltpu.VMEM((frame_len, frame_len), F32),
-            pltpu.VMEM((double, double), BF),
+            pltpu.VMEM((double, frame_len), BF),
             pltpu.VMEM((double, double), BF),
             pltpu.VMEM((2, frame_len, frame_len), BF),
             pltpu.VMEM((4 * piece_len, frame_len), BF),
         ],
-        count=8,
-        smem=(0, 1, 2),
+        count=6,
+        smem=(0,),
         limit=24,
-        cost=cost(flops, 12 * MIB),
-    )(place, positions, mate_positions, far_field, whole_probe, misfit, mates_misfit, right)
+        cost=cost(3 * flops // 4, 12 * MIB),
+    )(place, mates_far, whole_probe, mates_misfit, own_left, right)
     met = send(sent, mate)
     add = lambda a, b: (a.astype(F32) + b.astype(F32)).astype(BF)
     kept_side, kept = add(kept_side, met[0]), add(kept, met[1])
@@ -632,9 +671,9 @@
         limit=16,
         cost=cost(22 * moved, 7 * moved),
     )(past_steps, past_changes)
-    gradient, again, row = call(
+    gradient, row = call(
         gradient_kernel,
-        (size(transmission.shape, F32), size(transmission.shape, F32), size((devices, LANES), F32)),
+        (size(transmission.shape, F32), size((devices, LANES), F32)),
         [pltpu.VMEM((len(PAIRS) - OLD_PAIRS, 8, LANES), F32)],
         count=7,
         smem=(0,),
@@ -644,14 +683,13 @@
     all_rows = lax.all_to_all(
         row.reshape(devices, 1, LANES), AXES, split_axis=0, concat_axis=0, tiled=True
     ).reshape(devices, LANES)
-    updated = call(
+    return call(
         update_kernel,
-        size(transmission.shape, F32),
+        (size(transmission.shape, F32), size(transmission.shape, F32)),
         count=6,
         limit=16,
         cost=cost(10 * moved, 11 * moved),
-    )(all_rows, transmission, again, old_gradient, past_steps, past_changes)
-    return (updated, gradient)
+    )(all_rows, transmission, gradient, old_gradient, past_steps, past_changes)
 
 
 def solution(mesh):

time: 107 us -> 104 us (0.972)
  waiting for transfers between devices: 30.5 us -> 22 us
  local copies, waits for them, and re-layouts: 2.94 us -> 4.82 us
  starting transfers between devices: 31.6 us -> 33.4 us
  between operations: 0.91 us -> 2.18 us
    ppermute x21, waiting for transfers between devices: 30.5 us -> 22 us  [send(): return lax.ppermute(value, AXES, pairs)]
    slice x0 -> x2, local copies, waits for them, and re-layouts: none -> 1.88 us  [fast(): column = jnp.where(is_home, positions[0, 1], mate_positions[0, 1])]
    ppermute x21, starting transfers between devices: 31.6 us -> 33.4 us  [send(): return lax.ppermute(value, AXES, pairs)]
    pallas_call x3 -> x5, Pallas kernels: 11.4 us -> 13.2 us  [the longest x1 5.32 us: fast(): call(forward_kernel, (size((2, 2, double, half_len), BF), half_field, siz...]
  transfers between devices with their start and end apart: 21 -> 21, of which waited for: 10 -> 10; matrix products, arithmetic and copies ran while one was open for 1% -> 3% of each run, Pallas kernels for 4% -> 7%
where the time goes in v3:
time: 104 us
  starting transfers between devices  33.4 us (32%)
  Pallas kernels  22.8 us (22%)
  waiting for transfers between devices  22 us (21%)
  blocking collectives  16.9 us (16%)
  local copies, waits for them, and re-layouts  4.82 us (5%)
  between operations  2.18 us (2%)
  other arithmetic  1.54 us (1%)
    ppermute x21, starting transfers between devices, send(): return lax.ppermute(value, AXES, pairs)  33.4 us
    ppermute x21, waiting for transfers between devices, send(): return lax.ppermute(value, AXES, pairs)  22 us
    all_to_all x1, blocking collectives, fast(): lax.all_to_all(row.reshape(devices, 1, LANES), AXES, split_axis=0, concat...  16.9 us
    pallas_call x1, Pallas kernels, fast(): call(backward_kernel, (size((2, 2, piece_len, frame_len), BF), piece_shap...  5.54 us
    pallas_call x1, Pallas kernels, fast(): call(forward_kernel, (size((2, 2, double, half_len), BF), half_field, siz...  5.32 us
    pallas_call x1, Pallas kernels, fast(): call(gradient_kernel, (size(transmission.shape, F32), size((devices, LANE...  2.94 us
  transfers between devices with their start and end apart: 21, of which 10 were waited for; matrix products, arithmetic and copies ran while one was open for 3% of the time, Pallas kernels for 7%

profile of v3, /device:TPU:0, one launch (start us, length us, event | category | flops | bytes accessed | tf_op | source)
XLA Modules:
  0.0 103.7 jit_solution(4602883866798698842)
XLA Ops:
  0.6 1.0 dynamic-slice_bitcast_fusion
  1.6 3.1 %collective-permute-start.1 = (bf16[128,512]{1,0:T(8,128)(2,1)S(1)}, bf16[128,512]{1,0:T(8,128)(2,1)S(1)}, u32[]{:S(2)}, u32[]{:S(2)}) collective-permute-start(bf16[128,512]{1,0:T(8,128)(2,1)S(1)} %get-tuple-element.47), channel_id=1, source_target_pairs={{0,1},{1,0},{2,3},{3,2},{4,5},{5,4},{6,7},{7,6},{8,9},{9,8},{10,11... | collective-permute-start | bytes 393224 | tf_op jit(solution)/shard_map/ppermute | solution.py:544
  4.7 2.5 %collective-permute-start.4 = (bf16[128,512]{1,0:T(8,128)(2,1)S(1)}, bf16[128,512]{1,0:T(8,128)(2,1)S(1)}, u32[]{:S(2)}, u32[]{:S(2)}) collective-permute-start(bf16[128,512]{1,0:T(8,128)(2,1)S(1)} %get-tuple-element.47), channel_id=1, source_target_pairs={{0,3},{1,2},{2,1},{3,0},{4,7},{5,6},{6,5},{7,4},{8,11},{9,10},{10,... | collective-permute-start | bytes 393224 | tf_op jit(solution)/shard_map/ppermute | solution.py:544
  7.2 0.1 collective-permute-start.3
  7.3 1.0 convert_bitcast_fusion
  8.3 0.7 collective-permute-start.2
  9.0 5.2 %collective-permute-start = (s32[1,2]{1,0:T(1,128)}, s32[1,2]{1,0:T(1,128)S(1)}, u32[]{:S(2)}, u32[]{:S(2)}) collective-permute-start(s32[1,2]{1,0:T(1,128)} %pos_ref.3), channel_id=1, source_target_pairs={{0,4},{1,5},{2,6},{3,7},{4,0},{5,1},{6,2},{7,3},{8,12},{9,13},{10,... | collective-permute-start | bytes 32 | tf_op jit(solution)/shard_map/ppermute | solution.py:544
  14.2 1.2 %slice.18 = s32[1,1]{1,0:T(1,128)} slice(s32[1,2]{1,0:T(1,128)} %pos_ref.3), slice={[0:1], [1:2]} | slice | bytes 8 | tf_op jit(solution)/shard_map/slice | solution.py:579
  15.5 1.1 %copy-done.3 = f32[2,160,640]{2,1,0:T(8,128)S(1)} copy-done((f32[2,160,640]{2,1,0:T(8,128)S(1)}, f32[2,160,640]{2,1,0:T(8,128)}, u32[]{:S(2)}) %copy-start.3) | copy-done | bytes 819224
  16.6 0.7 copy-done.7
  17.3 1.0 shard_map.95
  18.3 0.0 collective-permute-done
  18.3 0.6 slice.19
  20.2 0.1 stack.23.place_ref
  20.3 0.1 collective-permute-done.3
  20.4 0.0 collective-permute-done.2.measured_ref
  20.4 1.6 %collective-permute-start.10 = (bf16[384,512]{1,0:T(8,128)(2,1)S(1)}, bf16[384,512]{1,0:T(8,128)(2,1)S(1)}, u32[]{:S(2)}, u32[]{:S(2)}) collective-permute-start(bf16[384,512]{1,0:T(8,128)(2,1)S(1)} %pad_maximum_fusion.q0_ref), channel_id=1, source_target_pairs={{0,8},{1,9},{2,10},{3,11},{4,12},{5,13},{6,14},{7,15},{8,0},{9,1},... | collective-permute-start | bytes 1179656 | tf_op jit(solution)/shard_map/ppermute | solution.py:544
  22.0 1.5 %collective-permute-start.8 = (bf16[384,512]{1,0:T(8,128)(2,1)S(1)}, bf16[384,512]{1,0:T(8,128)(2,1)S(1)}, u32[]{:S(2)}, u32[]{:S(2)}) collective-permute-start(bf16[384,512]{1,0:T(8,128)(2,1)S(1)} %pad_maximum_fusion.q0_ref), channel_id=1, source_target_pairs={{0,16},{1,17},{2,18},{3,19},{4,20},{5,21},{6,22},{7,23},{8,24},{9,... | collective-permute-start | bytes 1179656 | tf_op jit(solution)/shard_map/ppermute | solution.py:544
  23.5 0.7 collective-permute-start.5
  24.2 4.3 %collective-permute-start.6 = (bf16[2,160,512]{2,1,0:T(8,128)(2,1)S(1)}, bf16[2,160,512]{2,1,0:T(8,128)(2,1)S(1)}, u32[]{:S(2)}, u32[]{:S(2)}) collective-permute-start(bf16[2,160,512]{2,1,0:T(8,128)(2,1)S(1)} %shard_map.95), channel_id=1, source_target_pairs={{0,1},{1,0},{6,7},{7,6},{8,9},{9,8},{14,15},{15,14},{16,17},{17,16... | collective-permute-start | bytes 983048 | tf_op jit(solution)/shard_map/ppermute | solution.py:544
  28.5 0.7 collective-permute-start.7
  29.2 3.1 %collective-permute-done.10.q1_ref = bf16[384,512]{1,0:T(8,128)(2,1)S(1)} collective-permute-done((bf16[384,512]{1,0:T(8,128)(2,1)S(1)}, bf16[384,512]{1,0:T(8,128)(2,1)S(1)}, u32[]{:S(2)}, u32[]{:S(2)}) %collective-permute-start.10) | collective-permute-done | bytes 393248 | tf_op jit(solution)/shard_map/ppermute | solution.py:544
  32.3 1.6 %collective-permute-start.11 = (bf16[192,512]{1,0:T(8,128)(2,1)S(1)}, bf16[192,512]{1,0:T(8,128)(2,1)S(1)}, u32[]{:S(2)}, u32[]{:S(2)}) collective-permute-start(bf16[192,512]{1,0:T(8,128)(2,1)S(1)} %slice.25), channel_id=1, source_target_pairs={{0,16},{1,17},{2,18},{3,19},{4,20},{5,21},{6,22},{7,23},{8,24},{9,... | collective-permute-start | bytes 589832 | tf_op jit(solution)/shard_map/ppermute | solution.py:544
  33.9 0.0 collective-permute-done.8.q2_ref
  33.9 1.6 %collective-permute-start.9 = (bf16[192,512]{1,0:T(8,128)(2,1)S(1)}, bf16[192,512]{1,0:T(8,128)(2,1)S(1)}, u32[]{:S(2)}, u32[]{:S(2)}) collective-permute-start(bf16[192,512]{1,0:T(8,128)(2,1)S(1)} %slice.24), channel_id=1, source_target_pairs={{0,8},{1,9},{2,10},{3,11},{4,12},{5,13},{6,14},{7,15},{8,0},{9,1},... | collective-permute-start | bytes 589832 | tf_op jit(solution)/shard_map/ppermute | solution.py:544
  35.5 0.0 collective-permute-done.5.own_ref
  35.5 0.2 collective-permute-done.6
  35.7 3.7 %collective-permute-done.11.q3b_ref = bf16[192,512]{1,0:T(8,128)(2,1)S(1)} collective-permute-done((bf16[192,512]{1,0:T(8,128)(2,1)S(1)}, bf16[192,512]{1,0:T(8,128)(2,1)S(1)}, u32[]{:S(2)}, u32[]{:S(2)}) %collective-permute-start.11) | collective-permute-done | bytes 196640 | tf_op jit(solution)/shard_map/ppermute | solution.py:544
  39.5 1.3 %collective-permute-done.9.q3a_ref = bf16[192,512]{1,0:T(8,128)(2,1)S(1)} collective-permute-done((bf16[192,512]{1,0:T(8,128)(2,1)S(1)}, bf16[192,512]{1,0:T(8,128)(2,1)S(1)}, u32[]{:S(2)}, u32[]{:S(2)}) %collective-permute-start.9) | collective-permute-done | bytes 196640 | tf_op jit(solution)/shard_map/ppermute | solution.py:544
  40.8 0.0 copy-start.2
  40.8 0.1 collective-permute-start.13
  40.9 0.5 collective-permute-start.12
  41.4 1.4 %shard_map.96.probe_ref = bf16[2,2,512,512]{3,2,1,0:T(8,128)(2,1)S(1)} custom-call(s32[5]{0:T(128)S(1)} %stack.23.place_ref, bf16[2,8,128,512]{3,2,1,0:T(8,128)(2,1)S(1)} %copy-done.6, bf16[384,512]{1,0:T(8,128)(2,1)S(1)} %pad_maximum_fusion.q0_ref, bf16[384,512]{1,0:T(8,128)(2,1)S(1)} %collective-permute-done.10.q1_ref, ...), custom_call_target="tpu_custom_call" | custom-call | tf_op jit(solution)/shard_map/pallas_call | solution.py:591
  42.8 0.0 collective-permute-done.13.mate_side_ref
  42.8 0.2 collective-permute-done.12.mate_own_ref
  43.0 5.3 %shard_map.97 = (bf16[2,2,1024,256]{3,2,1,0:T(8,128)(2,1)S(1)}, bf16[2,2,512,256]{3,2,1,0:T(8,128)(2,1)S(1)}, bf16[512,256]{1,0:T(8,128)(2,1)S(1)}) custom-call(s32[5]{0:T(128)S(1)} %stack.23.place_ref, bf16[2,160,512]{2,1,0:T(8,128)(2,1)S(1)} %collective-permute-done.5.own_ref, bf16[2,160,512]{2,1,0:T(8,128)(2,1)S(1)} %broadcast_select_fusion.side_ref, ...), custom_call_target="tpu_custom_call" | custom-call | flops 3221225472 | bytes 16777216 | tf_op jit(solution)/shard_map/pallas_call | solution.py:606
  48.3 0.2 collective-permute-start.14
  48.5 1.9 %shard_map.98 = (bf16[2,2,512,256]{3,2,1,0:T(8,128)(2,1)S(1)}, f32[512,256]{1,0:T(8,128)S(1)}) custom-call(s32[5]{0:T(128)S(1)} %stack.23.place_ref, bf16[2,2,1024,256]{3,2,1,0:T(8,128)(2,1)S(1)} %get-tuple-element.35.turned_ref, bf16[128,512]{1,0:T(8,128)(2,1)S(1)} %collective-permute-done.2.measured_ref, bf16[1024,1024]{1,0:T(8,128)(2,1)S(1)} %copy-done.2), custom_call_target="tpu_custom_call" | custom-call | flops 1073741824 | bytes 4194304 | tf_op jit(solution)/shard_map/pallas_call | solution.py:621
  50.4 0.0 collective-permute-done.14
  50.4 0.1 fusion.2
  50.5 3.6 %collective-permute-start.15 = (bf16[512,256]{1,0:T(8,128)(2,1)S(1)}, bf16[512,256]{1,0:T(8,128)(2,1)S(1)}, u32[]{:S(2)}, u32[]{:S(2)}) collective-permute-start(bf16[512,256]{1,0:T(8,128)(2,1)S(1)} %fusion.2), channel_id=1, source_target_pairs={{0,1},{1,0},{2,3},{3,2},{4,5},{5,4},{6,7},{7,6},{8,9},{9,8},{10,11... | collective-permute-start | bytes 786440 | tf_op jit(solution)/shard_map/ppermute | solution.py:544
  54.1 6.6 %collective-permute-done.15 = bf16[512,256]{1,0:T(8,128)(2,1)S(1)} collective-permute-done((bf16[512,256]{1,0:T(8,128)(2,1)S(1)}, bf16[512,256]{1,0:T(8,128)(2,1)S(1)}, u32[]{:S(2)}, u32[]{:S(2)}) %collective-permute-start.15) | collective-permute-done | bytes 262176 | tf_op jit(solution)/shard_map/ppermute | solution.py:544
  60.7 0.1 fusion.4
  60.8 0.1 collective-permute-start.16
  60.8 1.3 %shard_map.99.own_ref = bf16[2,1024,256]{2,1,0:T(8,128)(2,1)S(1)} custom-call(bf16[2,2,512,256]{3,2,1,0:T(8,128)(2,1)S(1)} %get-tuple-element.38.far_ref, f32[512,256]{1,0:T(8,128)S(1)} %get-tuple-element.45.mine_ref, bf16[1024,1024]{1,0:T(8,128)(2,1)S(1)} %copy-done.2), custom_call_target="tpu_custom_call" | custom-call | flops 1073741824 | bytes 4194304 | tf_op jit(solution)/shard_map/pallas_call | solution.py:633
  62.1 0.2 collective-permute-done.16.mates_ref
  62.4 5.5 %shard_map.100 = (bf16[2,2,160,512]{3,2,1,0:T(8,128)(2,1)S(1)}, bf16[2,160,512]{2,1,0:T(8,128)(2,1)S(1)}, bf16[2,160,512]{2,1,0:T(8,128)(2,1)S(1)}) custom-call(s32[5]{0:T(128)S(1)} %stack.23.place_ref, bf16[2,2,512,256]{3,2,1,0:T(8,128)(2,1)S(1)} %get-tuple-element.34.far_ref, bf16[2,2,512,512]{3,2,1,0:T(8,128)(2,1)S(1)} %shard_map.96.probe_ref, ...), custom_call_target="tpu_custom_call" | custom-call | flops 3221225472 | bytes 12582912 | tf_op jit(solution)/shard_map/pallas_call | solution.py:643
  67.9 0.4 collective-permute-start.17
  68.3 1.8 %collective-permute-done.17 = bf16[2,2,160,512]{3,2,1,0:T(8,128)(2,1)S(1)} collective-permute-done((bf16[2,2,160,512]{3,2,1,0:T(8,128)(2,1)S(1)}, bf16[2,2,160,512]{3,2,1,0:T(8,128)(2,1)S(1)}, u32[]{:S(2)}, u32[]{:S(2)}) %collective-permute-start.17) | collective-permute-done | bytes 655392 | tf_op jit(solution)/shard_map/ppermute | solution.py:544
  70.1 0.2 fusion.1
  70.3 3.6 %collective-permute-start.18 = (bf16[2,160,512]{2,1,0:T(8,128)(2,1)S(1)}, bf16[2,160,512]{2,1,0:T(8,128)(2,1)S(1)}, u32[]{:S(2)}, u32[]{:S(2)}) collective-permute-start(bf16[2,160,512]{2,1,0:T(8,128)(2,1)S(1)} %get-tuple-element.49), channel_id=1, source_target_pairs={{0,1},{1,0},{6,7},{7,6},{8,9},{9,8},{14,15},{15,14},{16,17},{17,16... | collective-permute-start | bytes 983048 | tf_op jit(solution)/shard_map/ppermute | solution.py:544
  73.9 0.0 copy-start.8
  73.9 0.9 collective-permute-start.19
  74.8 0.7 collective-permute-start.20
  75.5 1.8 %shard_map.101.row_ref = f32[1,128]{1,0:T(1,128)S(1)} custom-call(f32[4,2,160,640]{3,2,1,0:T(8,128)S(1)} %copy-done, f32[3,2,160,640]{3,2,1,0:T(8,128)S(1)} %copy-done.1), custom_call_target="tpu_custom_call" | custom-call | flops 18022400 | bytes 5734400 | tf_op jit(solution)/shard_map/pallas_call | solution.py:666
  77.3 0.0 copy-start.4
  77.3 0.0 copy-start.5
  77.3 4.6 %collective-permute-done.18 = bf16[2,160,512]{2,1,0:T(8,128)(2,1)S(1)} collective-permute-done((bf16[2,160,512]{2,1,0:T(8,128)(2,1)S(1)}, bf16[2,160,512]{2,1,0:T(8,128)(2,1)S(1)}, u32[]{:S(2)}, u32[]{:S(2)}) %collective-permute-start.18) | collective-permute-done | bytes 327712 | tf_op jit(solution)/shard_map/ppermute | solution.py:544
  81.9 0.0 collective-permute-done.19
  81.9 0.0 collective-permute-done.20
  81.9 0.2 fusion.3.data_ref
  82.1 2.9 %shard_map.102 = (f32[2,160,640]{2,1,0:T(8,128)S(1)}, f32[32,128]{1,0:T(8,128)S(1)}) custom-call(s32[1,2]{1,0:T(1,128)S(1)} %copy-done.8, bf16[2,160,512]{2,1,0:T(8,128)(2,1)S(1)} %fusion.3.data_ref, f32[2,160,640]{2,1,0:T(8,128)S(1)} %copy-done.4, f32[2,160,640]{2,1,0:T(8,128)S(1)} %copy-done.5, f32[4,2,160,640]{3,2,1,0:T(8,128)S(1)} %copy-done, ...), custom_call_target="tpu_custom_call" | custom-call | flops 13107200 | bytes 8192000 | tf_op jit(solution)/shard_map/pallas_call | solution.py:674
  85.0 16.9 %all_to_all.5 = f32[32,1,128]{2,1,0:T(1,128)S(1)} all-to-all(f32[32,1,128]{2,1,0:T(1,128)S(1)} %bitcast.28), channel_id=1, replica_groups=mesh['region'=8,'grp'=4] {'region','grp'}, dimensions={0} | all-to-all | bytes 32768 | tf_op jit(solution)/shard_map/all_to_all | solution.py:683
  102.0 1.7 %shard_map.103 = (f32[2,160,640]{2,1,0:T(8,128)}, f32[2,160,640]{2,1,0:T(8,128)}) custom-call(f32[32,128]{1,0:T(8,128)S(1)} %bitcast.27, f32[2,160,640]{2,1,0:T(8,128)S(1)} %copy-done.4, f32[2,160,640]{2,1,0:T(8,128)S(1)} %get-tuple-element.43.gradient_ref, f32[2,160,640]{2,1,0:T(8,128)S(1)} %copy-done.5, f32[4,2,160,640]{3,2,1,0:T(8,128)S(1)} %copy-done, ...), custom_call_target="tpu_custom_call" | custom-call | flops 8192000 | bytes 9011200 | tf_op jit(solution)/shard_map/pallas_call | solution.py:686
  (19 shorter events, 0.1 us)
Async XLA Ops:
  1.6 6.7 %collective-permute-start.1 = (bf16[128,512]{1,0:T(8,128)(2,1)S(1)}, bf16[128,512]{1,0:T(8,128)(2,1)S(1)}, u32[]{:S(2)}, u32[]{:S(2)}) collective-permute-start(bf16[128,512]{1,0:T(8,128)(2,1)S(1)} %get-tuple-element.47), channel_id=1, source_target_pairs={{0,1},{1,0},{2,3},{3,2},{4,5},{5,4},{6,7},{7,6},{8,9},{9,8},{10,11... | collective-permute-start | bytes 393224 | tf_op jit(solution)/shard_map/ppermute | solution.py:544
  4.7 15.5 %collective-permute-start.4 = (bf16[128,512]{1,0:T(8,128)(2,1)S(1)}, bf16[128,512]{1,0:T(8,128)(2,1)S(1)}, u32[]{:S(2)}, u32[]{:S(2)}) collective-permute-start(bf16[128,512]{1,0:T(8,128)(2,1)S(1)} %get-tuple-element.47), channel_id=1, source_target_pairs={{0,3},{1,2},{2,1},{3,0},{4,7},{5,6},{6,5},{7,4},{8,11},{9,10},{10,... | collective-permute-start | bytes 393224 | tf_op jit(solution)/shard_map/ppermute | solution.py:544
  7.2 13.2 %collective-permute-start.3 = (bf16[128,512]{1,0:T(8,128)(2,1)S(1)}, bf16[128,512]{1,0:T(8,128)(2,1)S(1)}, u32[]{:S(2)}, u32[]{:S(2)}) collective-permute-start(bf16[128,512]{1,0:T(8,128)(2,1)S(1)} %get-tuple-element.46), channel_id=1, source_target_pairs={{0,2},{1,3},{2,0},{3,1},{4,6},{5,7},{6,4},{7,5},{8,10},{9,11},{10,... | collective-permute-start | bytes 393224 | tf_op jit(solution)/shard_map/ppermute | solution.py:544
  8.3 12.1 %collective-permute-start.2 = (bf16[128,512]{1,0:T(8,128)(2,1)S(1)}, bf16[128,512]{1,0:T(8,128)(2,1)S(1)}, u32[]{:S(2)}, u32[]{:S(2)}) collective-permute-start(bf16[128,512]{1,0:T(8,128)(2,1)S(1)} %convert_bitcast_fusion), channel_id=1, source_target_pairs={{0,0},{1,1},{2,4},{3,5},{4,2},{5,3},{6,6},{7,7},{8,8},{9,9},{10,12... | collective-permute-start | bytes 393224 | tf_op jit(solution)/shard_map/ppermute | solution.py:544
  9.0 9.3 %collective-permute-start = (s32[1,2]{1,0:T(1,128)}, s32[1,2]{1,0:T(1,128)S(1)}, u32[]{:S(2)}, u32[]{:S(2)}) collective-permute-start(s32[1,2]{1,0:T(1,128)} %pos_ref.3), channel_id=1, source_target_pairs={{0,4},{1,5},{2,6},{3,7},{4,0},{5,1},{6,2},{7,3},{8,12},{9,13},{10,... | collective-permute-start | bytes 32 | tf_op jit(solution)/shard_map/ppermute | solution.py:544
  15.5 1.1 %copy-start.3 = (f32[2,160,640]{2,1,0:T(8,128)S(1)}, f32[2,160,640]{2,1,0:T(8,128)}, u32[]{:S(2)}) copy-start(f32[2,160,640]{2,1,0:T(8,128)} %transmission_ref.3) | copy-start | bytes 2457604
  16.6 0.7 copy-start.7
  17.3 24.2 %copy-start.6 = (bf16[2,8,128,512]{3,2,1,0:T(8,128)(2,1)S(1)}, bf16[2,8,128,512]{3,2,1,0:T(8,128)(2,1)}, u32[]{:S(2)}) copy-start(bf16[2,8,128,512]{3,2,1,0:T(8,128)(2,1)} %all_ref.1) | copy-start | bytes 6291460
  20.4 11.9 %collective-permute-start.10 = (bf16[384,512]{1,0:T(8,128)(2,1)S(1)}, bf16[384,512]{1,0:T(8,128)(2,1)S(1)}, u32[]{:S(2)}, u32[]{:S(2)}) collective-permute-start(bf16[384,512]{1,0:T(8,128)(2,1)S(1)} %pad_maximum_fusion.q0_ref), channel_id=1, source_target_pairs={{0,8},{1,9},{2,10},{3,11},{4,12},{5,13},{6,14},{7,15},{8,0},{9,1},... | collective-permute-start | bytes 1179656 | tf_op jit(solution)/shard_map/ppermute | solution.py:544
  22.0 12.0 %collective-permute-start.8 = (bf16[384,512]{1,0:T(8,128)(2,1)S(1)}, bf16[384,512]{1,0:T(8,128)(2,1)S(1)}, u32[]{:S(2)}, u32[]{:S(2)}) collective-permute-start(bf16[384,512]{1,0:T(8,128)(2,1)S(1)} %pad_maximum_fusion.q0_ref), channel_id=1, source_target_pairs={{0,16},{1,17},{2,18},{3,19},{4,20},{5,21},{6,22},{7,23},{8,24},{9,... | collective-permute-start | bytes 1179656 | tf_op jit(solution)/shard_map/ppermute | solution.py:544
  23.5 12.0 %collective-permute-start.5 = (bf16[2,160,512]{2,1,0:T(8,128)(2,1)S(1)}, bf16[2,160,512]{2,1,0:T(8,128)(2,1)S(1)}, u32[]{:S(2)}, u32[]{:S(2)}) collective-permute-start(bf16[2,160,512]{2,1,0:T(8,128)(2,1)S(1)} %shard_map.95), channel_id=1, source_target_pairs={{0,0},{1,1},{2,4},{3,5},{4,2},{5,3},{6,6},{7,7},{8,8},{9,9},{10,12... | collective-permute-start | bytes 983048 | tf_op jit(solution)/shard_map/ppermute | solution.py:544
  24.2 11.6 %collective-permute-start.6 = (bf16[2,160,512]{2,1,0:T(8,128)(2,1)S(1)}, bf16[2,160,512]{2,1,0:T(8,128)(2,1)S(1)}, u32[]{:S(2)}, u32[]{:S(2)}) collective-permute-start(bf16[2,160,512]{2,1,0:T(8,128)(2,1)S(1)} %shard_map.95), channel_id=1, source_target_pairs={{0,1},{1,0},{6,7},{7,6},{8,9},{9,8},{14,15},{15,14},{16,17},{17,16... | collective-permute-start | bytes 983048 | tf_op jit(solution)/shard_map/ppermute | solution.py:544
  28.5 7.2 %collective-permute-start.7 = (bf16[2,160,512]{2,1,0:T(8,128)(2,1)S(1)}, bf16[2,160,512]{2,1,0:T(8,128)(2,1)S(1)}, u32[]{:S(2)}, u32[]{:S(2)}) collective-permute-start(bf16[2,160,512]{2,1,0:T(8,128)(2,1)S(1)} %shard_map.95), channel_id=1, source_target_pairs={{2,5},{3,4},{4,3},{5,2},{10,13},{11,12},{12,11},{13,10},{18,21},{1... | collective-permute-start | bytes 983048 | tf_op jit(solution)/shard_map/ppermute | solution.py:544
  32.3 7.1 %collective-permute-start.11 = (bf16[192,512]{1,0:T(8,128)(2,1)S(1)}, bf16[192,512]{1,0:T(8,128)(2,1)S(1)}, u32[]{:S(2)}, u32[]{:S(2)}) collective-permute-start(bf16[192,512]{1,0:T(8,128)(2,1)S(1)} %slice.25), channel_id=1, source_target_pairs={{0,16},{1,17},{2,18},{3,19},{4,20},{5,21},{6,22},{7,23},{8,24},{9,... | collective-permute-start | bytes 589832 | tf_op jit(solution)/shard_map/ppermute | solution.py:544
  33.9 6.9 %collective-permute-start.9 = (bf16[192,512]{1,0:T(8,128)(2,1)S(1)}, bf16[192,512]{1,0:T(8,128)(2,1)S(1)}, u32[]{:S(2)}, u32[]{:S(2)}) collective-permute-start(bf16[192,512]{1,0:T(8,128)(2,1)S(1)} %slice.24), channel_id=1, source_target_pairs={{0,8},{1,9},{2,10},{3,11},{4,12},{5,13},{6,14},{7,15},{8,0},{9,1},... | collective-permute-start | bytes 589832 | tf_op jit(solution)/shard_map/ppermute | solution.py:544
  40.8 2.2 %copy-start.2 = (bf16[1024,1024]{1,0:T(8,128)(2,1)S(1)}, bf16[1024,1024]{1,0:T(8,128)(2,1)}, u32[]{:S(2)}) copy-start(bf16[1024,1024]{1,0:T(8,128)(2,1)} %constant.23.clone.right_ref) | copy-start | bytes 6291460
  40.8 2.0 %collective-permute-start.13 = (bf16[2,160,512]{2,1,0:T(8,128)(2,1)S(1)}, bf16[2,160,512]{2,1,0:T(8,128)(2,1)S(1)}, u32[]{:S(2)}, u32[]{:S(2)}) collective-permute-start(bf16[2,160,512]{2,1,0:T(8,128)(2,1)S(1)} %broadcast_select_fusion.side_ref), channel_id=1, source_target_pairs={{0,4},{1,5},{2,6},{3,7},{4,0},{5,1},{6,2},{7,3},{8,12},{9,13},{10,... | collective-permute-start | bytes 983048 | tf_op jit(solution)/shard_map/ppermute | solution.py:544
  40.9 2.1 %collective-permute-start.12 = (bf16[2,160,512]{2,1,0:T(8,128)(2,1)S(1)}, bf16[2,160,512]{2,1,0:T(8,128)(2,1)S(1)}, u32[]{:S(2)}, u32[]{:S(2)}) collective-permute-start(bf16[2,160,512]{2,1,0:T(8,128)(2,1)S(1)} %collective-permute-done.5.own_ref), channel_id=1, source_target_pairs={{0,4},{1,5},{2,6},{3,7},{4,0},{5,1},{6,2},{7,3},{8,12},{9,13},{10,... | collective-permute-start | bytes 983048 | tf_op jit(solution)/shard_map/ppermute | solution.py:544
  48.3 2.1 %collective-permute-start.14 = (bf16[512,256]{1,0:T(8,128)(2,1)S(1)}, bf16[512,256]{1,0:T(8,128)(2,1)S(1)}, u32[]{:S(2)}, u32[]{:S(2)}) collective-permute-start(bf16[512,256]{1,0:T(8,128)(2,1)S(1)} %get-tuple-element.37), channel_id=1, source_target_pairs={{0,4},{1,5},{2,6},{3,7},{4,0},{5,1},{6,2},{7,3},{8,12},{9,13},{10,... | collective-permute-start | bytes 786440 | tf_op jit(solution)/shard_map/ppermute | solution.py:544
  50.5 10.2 %collective-permute-start.15 = (bf16[512,256]{1,0:T(8,128)(2,1)S(1)}, bf16[512,256]{1,0:T(8,128)(2,1)S(1)}, u32[]{:S(2)}, u32[]{:S(2)}) collective-permute-start(bf16[512,256]{1,0:T(8,128)(2,1)S(1)} %fusion.2), channel_id=1, source_target_pairs={{0,1},{1,0},{2,3},{3,2},{4,5},{5,4},{6,7},{7,6},{8,9},{9,8},{10,11... | collective-permute-start | bytes 786440 | tf_op jit(solution)/shard_map/ppermute | solution.py:544
  60.8 1.6 %collective-permute-start.16 = (bf16[512,256]{1,0:T(8,128)(2,1)S(1)}, bf16[512,256]{1,0:T(8,128)(2,1)S(1)}, u32[]{:S(2)}, u32[]{:S(2)}) collective-permute-start(bf16[512,256]{1,0:T(8,128)(2,1)S(1)} %get-tuple-element.44), channel_id=1, source_target_pairs={{0,4},{1,5},{2,6},{3,7},{4,0},{5,1},{6,2},{7,3},{8,12},{9,13},{10,... | collective-permute-start | bytes 786440 | tf_op jit(solution)/shard_map/ppermute | solution.py:544
  62.4 13.1 %copy-start = (f32[4,2,160,640]{3,2,1,0:T(8,128)S(1)}, f32[4,2,160,640]{3,2,1,0:T(8,128)}, u32[]{:S(2)}) copy-start(f32[4,2,160,640]{3,2,1,0:T(8,128)} %steps_ref.5) | copy-start | bytes 9830404
  62.4 13.1 %copy-start.1 = (f32[3,2,160,640]{3,2,1,0:T(8,128)S(1)}, f32[3,2,160,640]{3,2,1,0:T(8,128)}, u32[]{:S(2)}) copy-start(f32[3,2,160,640]{3,2,1,0:T(8,128)} %changes_ref.5) | copy-start | bytes 7372804
  67.9 2.2 %collective-permute-start.17 = (bf16[2,2,160,512]{3,2,1,0:T(8,128)(2,1)S(1)}, bf16[2,2,160,512]{3,2,1,0:T(8,128)(2,1)S(1)}, u32[]{:S(2)}, u32[]{:S(2)}) collective-permute-start(bf16[2,2,160,512]{3,2,1,0:T(8,128)(2,1)S(1)} %get-tuple-element.40), channel_id=1, source_target_pairs={{0,4},{1,5},{2,6},{3,7},{4,0},{5,1},{6,2},{7,3},{8,12},{9,13},{10,... | collective-permute-start | bytes 1966088 | tf_op jit(solution)/shard_map/ppermute | solution.py:544
  70.3 11.6 %collective-permute-start.18 = (bf16[2,160,512]{2,1,0:T(8,128)(2,1)S(1)}, bf16[2,160,512]{2,1,0:T(8,128)(2,1)S(1)}, u32[]{:S(2)}, u32[]{:S(2)}) collective-permute-start(bf16[2,160,512]{2,1,0:T(8,128)(2,1)S(1)} %get-tuple-element.49), channel_id=1, source_target_pairs={{0,1},{1,0},{6,7},{7,6},{8,9},{9,8},{14,15},{15,14},{16,17},{17,16... | collective-permute-start | bytes 983048 | tf_op jit(solution)/shard_map/ppermute | solution.py:544
  73.9 8.2 %copy-start.8 = (s32[1,2]{1,0:T(1,128)S(1)}, s32[1,2]{1,0:T(1,128)}, u32[]{:S(2)}) copy-start(s32[1,2]{1,0:T(1,128)} %pos_ref.3) | copy-start | bytes 28
  73.9 8.0 %collective-permute-start.19 = (bf16[2,160,512]{2,1,0:T(8,128)(2,1)S(1)}, bf16[2,160,512]{2,1,0:T(8,128)(2,1)S(1)}, u32[]{:S(2)}, u32[]{:S(2)}) collective-permute-start(bf16[2,160,512]{2,1,0:T(8,128)(2,1)S(1)} %get-tuple-element.48), channel_id=1, source_target_pairs={{2,4},{3,5},{4,2},{5,3},{10,12},{11,13},{12,10},{13,11},{18,20},{1... | collective-permute-start | bytes 983048 | tf_op jit(solution)/shard_map/ppermute | solution.py:544
  74.8 7.1 %collective-permute-start.20 = (bf16[2,160,512]{2,1,0:T(8,128)(2,1)S(1)}, bf16[2,160,512]{2,1,0:T(8,128)(2,1)S(1)}, u32[]{:S(2)}, u32[]{:S(2)}) collective-permute-start(bf16[2,160,512]{2,1,0:T(8,128)(2,1)S(1)} %get-tuple-element.49), channel_id=1, source_target_pairs={{2,5},{3,4},{4,3},{5,2},{10,13},{11,12},{12,11},{13,10},{18,21},{1... | collective-permute-start | bytes 983048 | tf_op jit(solution)/shard_map/ppermute | solution.py:544
  77.3 4.8 %copy-start.4 = (f32[2,160,640]{2,1,0:T(8,128)S(1)}, f32[2,160,640]{2,1,0:T(8,128)}, u32[]{:S(2)}) copy-start(f32[2,160,640]{2,1,0:T(8,128)} %transmission_ref.3) | copy-start | bytes 2457604
  77.3 4.8 %copy-start.5 = (f32[2,160,640]{2,1,0:T(8,128)S(1)}, f32[2,160,640]{2,1,0:T(8,128)}, u32[]{:S(2)}) copy-start(f32[2,160,640]{2,1,0:T(8,128)} %old_ref.3) | copy-start | bytes 2457604

commit v4 on v3

--- a/solution.py
+++ b/solution.py
@@ -192,11 +192,19 @@
     folded = (table * chirp[None, :]) @ np.conj(table)
     folded = 0.5 * (folded + folded.T)
     real, imag = folded.real, folded.imag
-    return np.block([[real, imag], [-imag, real]]).astype(ml_dtypes.bfloat16)
+    return np.stack([real, imag - real, real + imag]).astype(ml_dtypes.bfloat16)
 
 
 def dot(left, right, dims=((1,), (0,))):
     return lax.dot_general(left, right, (dims, ((), ())), preferred_element_type=F32)
+
+
+def join(sums, reals, imags):
+    return sums - imags, sums + reals
+
+
+def summed(real, imag):
+    return (real.astype(F32) + imag.astype(F32)).astype(BF)
 
 
 def shift_table(rows, columns, row_base, column_base):
@@ -269,17 +277,17 @@
         rows = slice(mode * frame_len, (mode + 1) * frame_len)
         pr, pi = probe_ref[0, mode].astype(F32), probe_ref[1, mode].astype(F32)
         wr, wi = window_ref[0].astype(F32), window_ref[1].astype(F32)
-        wave[rows, :frame_len] = (pr * wr - pi * wi).astype(BF)
-        wave[rows, frame_len:] = (pr * wi + pi * wr).astype(BF)
-    for part in range(2):
-        for cell in range(2):
-            start = part * frame_len + cell * block
-            result = dot(wave[...], right_ref[:, start : start + block])
-            result = (result if part == 0 else -result).astype(BF)
-            for mode in range(2):
-                turned_ref[mode, cell, part * frame_len : (part + 1) * frame_len, :] = result[
-                    mode * frame_len : (mode + 1) * frame_len
-                ]
+        real, imag = (pr * wr - pi * wi).astype(BF), (pr * wi + pi * wr).astype(BF)
+        wave[0, rows], wave[1, rows], wave[2, rows] = summed(real, imag), real, imag
+    for cell in range(2):
+        columns = slice(cell * block, (cell + 1) * block)
+        real, imag = join(*(dot(wave[index], right_ref[index, :, columns]) for index in range(3)))
+        real, imag = real.astype(BF), imag.astype(BF)
+        total_part = summed(real, imag)
+        for mode in range(2):
+            rows = slice(mode * frame_len, (mode + 1) * frame_len)
+            for index, value in enumerate((total_part, real, imag)):
+                turned_ref[mode, cell, index] = value[rows]
     far_columns(1 - core, turned_ref, right_ref, far_ref, total)
     subtract(core, half, 1 - core, measured_ref, total)
     send_ref[...] = total[...].astype(BF)
@@ -289,8 +297,8 @@
     frame_len = total.shape[0]
     power = 0.0
     for mode in range(2):
-        result = dot(right_ref[...], turned_ref[mode, cell])
-        real, imag = result[:frame_len].astype(BF), (-result[frame_len:]).astype(BF)
+        real, imag = join(*(dot(right_ref[index], turned_ref[mode, cell, index]) for index in range(3)))
+        real, imag = real.astype(BF), imag.astype(BF)
         far_ref[mode, 0] = real
         far_ref[mode, 1] = imag
         real, imag = real.astype(F32), imag.astype(F32)
@@ -311,51 +319,47 @@
     subtract(core, half, core, measured_ref, total)
 
 
-def left_columns(misfit, far_ref, right_ref, weighted, store):
-    frame_len, block = misfit.shape
+def left_columns(misfit, far_ref, right_ref, store):
     for mode in range(2):
-        for part in range(2):
-            weighted[part * frame_len : (part + 1) * frame_len, mode * block : (mode + 1) * block] = (
-                misfit * far_ref[mode, part].astype(F32)
-            ).astype(BF)
-        result = dot(right_ref[...], weighted[:, mode * block : (mode + 1) * block])
-        store(mode, 0, result[:frame_len].astype(BF))
-        store(mode, 1, (-result[frame_len:]).astype(BF))
-
-
-def own_kernel(far_ref, mine_ref, right_ref, out_ref, weighted):
+        real = (misfit * far_ref[mode, 0].astype(F32)).astype(BF)
+        imag = (-misfit * far_ref[mode, 1].astype(F32)).astype(BF)
+        pieces = (summed(real, imag), real, imag)
+        real, imag = join(*(dot(right_ref[index], value) for index, value in enumerate(pieces)))
+        real, imag = real.astype(BF), imag.astype(BF)
+        for index, value in enumerate((summed(real, imag), real, imag)):
+            store(mode, index, value)
+
+
+def own_kernel(far_ref, mine_ref, right_ref, out_ref):
     frame_len = mine_ref.shape[0]
 
     def store(mode, part, value):
         out_ref[part, mode * frame_len : (mode + 1) * frame_len, :] = value
 
-    left_columns(mine_ref[...], far_ref, right_ref, weighted, store)
+    left_columns(mine_ref[...], far_ref, right_ref, store)
 
 
 def backward_kernel(
     place_ref, far_ref, probe_ref, mates_ref, own_ref, right_ref,
-    send_ref, side_ref, keep_ref, weighted, turned, grad, table,
+    send_ref, side_ref, keep_ref, turned, grad, table,
 ):
     core, half = place_ref[0], place_ref[3]
     column = place_ref[4]
     frame_len, block = mates_ref.shape
     piece_len = keep_ref.shape[1]
 
-    def lanes(part, cell):
-        return pl.ds(pl.multiple_of(part * frame_len + cell * block, block), block)
-
-    def store(mode, part, value):
-        turned[mode * frame_len : (mode + 1) * frame_len, lanes(part, 1 - core)] = value
-
-    left_columns(mates_ref[...].astype(F32), far_ref, right_ref, weighted, store)
-    for part in range(2):
-        turned[:, lanes(part, core)] = own_ref[part]
+    def lanes(cell):
+        return pl.ds(pl.multiple_of(cell * block, block), block)
+
+    def store(mode, index, value):
+        turned[index, mode * frame_len : (mode + 1) * frame_len, lanes(1 - core)] = value
+
+    left_columns(mates_ref[...].astype(F32), far_ref, right_ref, store)
+    for index in range(3):
+        turned[index, :, lanes(core)] = own_ref[index]
     for cell in range(2):
         columns = slice(cell * block, (cell + 1) * block)
-        back = [
-            dot(turned[...], right_ref[:, part * frame_len + cell * block : part * frame_len + (cell + 1) * block])
-            for part in range(2)
-        ]
+        back = join(*(dot(turned[index], right_ref[index, :, columns]) for index in range(3)))
         real, imag = 0.0, 0.0
         for mode in range(2):
             br, bi = (value[mode * frame_len : (mode + 1) * frame_len] for value in back)
@@ -431,15 +435,12 @@
     pos_ref, data_ref, transmission_ref, old_ref, steps_ref, changes_ref, row_ref, gradient_ref, out_ref, sums
 ):
     table = shift_table(data_ref.shape[2], transmission_ref.shape[2], pos_ref[0, 0], 0)
+    parts, piece_len, frame_len = data_ref.shape
+    placed = dot(data_ref[...].reshape(parts * piece_len, frame_len), table)
+    gradient_ref[...] = placed.reshape(transmission_ref.shape) + TIKHONOV * transmission_ref[...]
     for start in column_blocks(transmission_ref):
         columns = slice(start, start + BLOCK)
-        gradient = jnp.stack(
-            [
-                dot(data_ref[part, columns], table) + TIKHONOV * transmission_ref[part, columns]
-                for part in range(2)
-            ]
-        )
-        gradient_ref[:, columns] = gradient
+        gradient = gradient_ref[:, columns]
         vectors = {
             "s": [steps_ref[index, :, columns] for index in range(HIST)],
             "y": [changes_ref[index, :, columns] for index in range(HIST - 1)]
@@ -451,7 +452,11 @@
     out_ref[...] = jnp.broadcast_to(fresh + row_ref[...], out_ref.shape)
 
 
-def update_kernel(rows_ref, transmission_ref, gradient_ref, old_ref, steps_ref, changes_ref, out_ref, copy_ref):
+def update_kernel(
+    rows_ref, transmission_ref, gradient_ref, old_ref, steps_ref, changes_ref, updated_ref, copy_ref, out_ref, sem
+):
+    copies = [pltpu.make_async_copy(gradient_ref, copy_ref, sem.at[2])]
+    copies[0].start()
     row = jnp.sum(rows_ref[...], axis=0, keepdims=True)
     lane = lax.broadcasted_iota(jnp.int32, row.shape, 1)
 
@@ -491,23 +496,26 @@
         for start in column_blocks(out_ref):
             columns = slice(start, start + BLOCK)
             gradient = gradient_ref[part, columns]
-            copy_ref[part, columns] = gradient
             total = scale_row * gradient + change_rows[last] * (gradient - old_ref[part, columns])
             for index in range(HIST - 1):
                 total = total + change_rows[index] * changes_ref[index, part, columns]
             for index in range(HIST):
                 total = total + step_rows[index] * steps_ref[index, part, columns]
             out_ref[part, columns] = transmission_ref[part, columns] - total
-
-
-def call(body, outs, scratch=(), limit=48, smem=(), far=(), count=0, cost=None):
+        copies.append(pltpu.make_async_copy(out_ref.at[part], updated_ref.at[part], sem.at[part]))
+        copies[-1].start()
+    for copy in copies:
+        copy.wait()
+
+
+def call(body, outs, scratch=(), limit=48, smem=(), far=(), count=0, cost=None, out_space=pltpu.VMEM):
     space = lambda index: pltpu.SMEM if index in smem else pl.ANY if index in far else pltpu.VMEM
     specs = [pl.BlockSpec(memory_space=space(index)) for index in range(count)]
     return pl.pallas_call(
         body,
         out_shape=outs,
         in_specs=specs,
-        out_specs=jax.tree.map(lambda _: pl.BlockSpec(memory_space=pltpu.VMEM), outs),
+        out_specs=jax.tree.map(lambda _: pl.BlockSpec(memory_space=out_space), outs),
         scratch_shapes=list(scratch),
         compiler_params=pltpu.CompilerParams(vmem_limit_bytes=limit * MIB),
         cost_estimate=cost,
@@ -605,11 +613,11 @@
     half_field = size((2, 2, frame_len, half_len), BF)
     turned, mates_far, sent = call(
         forward_kernel,
-        (size((2, 2, double, half_len), BF), half_field, size((frame_len, half_len), BF)),
+        (size((2, 2, 3, frame_len, half_len), BF), half_field, size((frame_len, half_len), BF)),
         [
             pltpu.VMEM((2, tile_len, frame_len), BF),
             pltpu.VMEM((2, frame_len, frame_len), BF),
-            pltpu.VMEM((double, double), BF),
+            pltpu.VMEM((3, double, frame_len), BF),
             pltpu.VMEM((frame_len, half_len), F32),
         ],
         count=8,
@@ -632,8 +640,7 @@
     mates_misfit = send(misfit.astype(BF), mate)
     own_left = call(
         own_kernel,
-        size((2, double, half_len), BF),
-        [pltpu.VMEM((double, frame_len), BF)],
+        size((3, double, half_len), BF),
         count=3,
         limit=24,
         cost=cost(flops // 4, 4 * MIB),
@@ -644,8 +651,7 @@
         backward_kernel,
         (size((2, 2, piece_len, frame_len), BF), piece_shape, piece_shape),
         [
-            pltpu.VMEM((double, frame_len), BF),
-            pltpu.VMEM((double, double), BF),
+            pltpu.VMEM((3, double, frame_len), BF),
             pltpu.VMEM((2, frame_len, frame_len), BF),
             pltpu.VMEM((4 * piece_len, frame_len), BF),
         ],
@@ -686,9 +692,11 @@
     return call(
         update_kernel,
         (size(transmission.shape, F32), size(transmission.shape, F32)),
+        [pltpu.VMEM(transmission.shape, F32), pltpu.SemaphoreType.DMA((3,))],
         count=6,
         limit=16,
         cost=cost(10 * moved, 11 * moved),
+        out_space=pl.ANY,
     )(all_rows, transmission, gradient, old_gradient, past_steps, past_changes)
 
 

time: 104 us -> 102 us (0.981)
  Pallas kernels: 22.8 us -> 20.8 us
where the time goes in v4:
time: 102 us
  starting transfers between devices  33.3 us (33%)
  waiting for transfers between devices  22.3 us (22%)
  Pallas kernels  20.8 us (20%)
  blocking collectives  16.9 us (17%)
  local copies, waits for them, and re-layouts  4.82 us (5%)
  between operations  2.34 us (2%)
  other arithmetic  1.54 us (2%)
    ppermute x21, starting transfers between devices, send(): return lax.ppermute(value, AXES, pairs)  33.3 us
    ppermute x21, waiting for transfers between devices, send(): return lax.ppermute(value, AXES, pairs)  22.3 us
    all_to_all x1, blocking collectives, fast(): lax.all_to_all(row.reshape(devices, 1, LANES), AXES, split_axis=0, concat...  16.9 us
    pallas_call x1, Pallas kernels, fast(): call(forward_kernel, (size((2, 2, 3, frame_len, half_len), BF), half_fiel...  5.14 us
    pallas_call x1, Pallas kernels, fast(): call(backward_kernel, (size((2, 2, piece_len, frame_len), BF), piece_shap...  4.86 us
    pallas_call x1, Pallas kernels, fast(): call(gradient_kernel, (size(transmission.shape, F32), size((devices, LANE...  2.49 us
  transfers between devices with their start and end apart: 21, of which 10 were waited for; matrix products, arithmetic and copies ran while one was open for 3% of the time, Pallas kernels for 7%

profile of v4, /device:TPU:0, one launch (start us, length us, event | category | flops | bytes accessed | tf_op | source)
XLA Modules:
  0.0 102.0 jit_solution(12898636592336413074)
XLA Ops:
  0.6 1.0 dynamic-slice_bitcast_fusion
  1.6 3.1 %collective-permute-start.1 = (bf16[128,512]{1,0:T(8,128)(2,1)S(1)}, bf16[128,512]{1,0:T(8,128)(2,1)S(1)}, u32[]{:S(2)}, u32[]{:S(2)}) collective-permute-start(bf16[128,512]{1,0:T(8,128)(2,1)S(1)} %get-tuple-element.47), channel_id=1, source_target_pairs={{0,1},{1,0},{2,3},{3,2},{4,5},{5,4},{6,7},{7,6},{8,9},{9,8},{10,11... | collective-permute-start | bytes 393224 | tf_op jit(solution)/shard_map/ppermute | solution.py:552
  4.7 2.5 %collective-permute-start.4 = (bf16[128,512]{1,0:T(8,128)(2,1)S(1)}, bf16[128,512]{1,0:T(8,128)(2,1)S(1)}, u32[]{:S(2)}, u32[]{:S(2)}) collective-permute-start(bf16[128,512]{1,0:T(8,128)(2,1)S(1)} %get-tuple-element.47), channel_id=1, source_target_pairs={{0,3},{1,2},{2,1},{3,0},{4,7},{5,6},{6,5},{7,4},{8,11},{9,10},{10,... | collective-permute-start | bytes 393224 | tf_op jit(solution)/shard_map/ppermute | solution.py:552
  7.2 0.1 collective-permute-start.3
  7.3 1.0 convert_bitcast_fusion
  8.3 0.0 collective-permute-done.1
  8.3 0.7 collective-permute-start.2
  9.0 5.2 %collective-permute-start = (s32[1,2]{1,0:T(1,128)}, s32[1,2]{1,0:T(1,128)S(1)}, u32[]{:S(2)}, u32[]{:S(2)}) collective-permute-start(s32[1,2]{1,0:T(1,128)} %pos_ref.3), channel_id=1, source_target_pairs={{0,4},{1,5},{2,6},{3,7},{4,0},{5,1},{6,2},{7,3},{8,12},{9,13},{10,... | collective-permute-start | bytes 32 | tf_op jit(solution)/shard_map/ppermute | solution.py:552
  14.2 1.2 %slice.18 = s32[1,1]{1,0:T(1,128)} slice(s32[1,2]{1,0:T(1,128)} %pos_ref.3), slice={[0:1], [1:2]} | slice | bytes 8 | tf_op jit(solution)/shard_map/slice | solution.py:587
  15.5 1.1 %copy-done.2 = f32[2,160,640]{2,1,0:T(8,128)S(1)} copy-done((f32[2,160,640]{2,1,0:T(8,128)S(1)}, f32[2,160,640]{2,1,0:T(8,128)}, u32[]{:S(2)}) %copy-start.2) | copy-done | bytes 819224
  16.6 0.7 copy-done.7
  17.3 1.0 shard_map.95
  18.3 0.0 collective-permute-done
  18.3 0.6 slice.19
  20.2 0.1 stack.23.place_ref
  20.3 0.0 collective-permute-done.4
  20.3 0.1 collective-permute-done.3
  20.4 1.6 %collective-permute-start.10 = (bf16[384,512]{1,0:T(8,128)(2,1)S(1)}, bf16[384,512]{1,0:T(8,128)(2,1)S(1)}, u32[]{:S(2)}, u32[]{:S(2)}) collective-permute-start(bf16[384,512]{1,0:T(8,128)(2,1)S(1)} %pad_maximum_fusion.q0_ref), channel_id=1, source_target_pairs={{0,8},{1,9},{2,10},{3,11},{4,12},{5,13},{6,14},{7,15},{8,0},{9,1},... | collective-permute-start | bytes 1179656 | tf_op jit(solution)/shard_map/ppermute | solution.py:552
  22.0 1.5 %collective-permute-start.8 = (bf16[384,512]{1,0:T(8,128)(2,1)S(1)}, bf16[384,512]{1,0:T(8,128)(2,1)S(1)}, u32[]{:S(2)}, u32[]{:S(2)}) collective-permute-start(bf16[384,512]{1,0:T(8,128)(2,1)S(1)} %pad_maximum_fusion.q0_ref), channel_id=1, source_target_pairs={{0,16},{1,17},{2,18},{3,19},{4,20},{5,21},{6,22},{7,23},{8,24},{9,... | collective-permute-start | bytes 1179656 | tf_op jit(solution)/shard_map/ppermute | solution.py:552
  23.5 0.7 collective-permute-start.5
  24.2 4.3 %collective-permute-start.6 = (bf16[2,160,512]{2,1,0:T(8,128)(2,1)S(1)}, bf16[2,160,512]{2,1,0:T(8,128)(2,1)S(1)}, u32[]{:S(2)}, u32[]{:S(2)}) collective-permute-start(bf16[2,160,512]{2,1,0:T(8,128)(2,1)S(1)} %shard_map.95), channel_id=1, source_target_pairs={{0,1},{1,0},{6,7},{7,6},{8,9},{9,8},{14,15},{15,14},{16,17},{17,16... | collective-permute-start | bytes 983048 | tf_op jit(solution)/shard_map/ppermute | solution.py:552
  28.5 0.7 collective-permute-start.7
  29.2 3.1 %collective-permute-done.10.q1_ref = bf16[384,512]{1,0:T(8,128)(2,1)S(1)} collective-permute-done((bf16[384,512]{1,0:T(8,128)(2,1)S(1)}, bf16[384,512]{1,0:T(8,128)(2,1)S(1)}, u32[]{:S(2)}, u32[]{:S(2)}) %collective-permute-start.10) | collective-permute-done | bytes 393248 | tf_op jit(solution)/shard_map/ppermute | solution.py:552
  32.3 1.6 %collective-permute-start.11 = (bf16[192,512]{1,0:T(8,128)(2,1)S(1)}, bf16[192,512]{1,0:T(8,128)(2,1)S(1)}, u32[]{:S(2)}, u32[]{:S(2)}) collective-permute-start(bf16[192,512]{1,0:T(8,128)(2,1)S(1)} %slice.25), channel_id=1, source_target_pairs={{0,16},{1,17},{2,18},{3,19},{4,20},{5,21},{6,22},{7,23},{8,24},{9,... | collective-permute-start | bytes 589832 | tf_op jit(solution)/shard_map/ppermute | solution.py:552
  33.9 1.6 %collective-permute-start.9 = (bf16[192,512]{1,0:T(8,128)(2,1)S(1)}, bf16[192,512]{1,0:T(8,128)(2,1)S(1)}, u32[]{:S(2)}, u32[]{:S(2)}) collective-permute-start(bf16[192,512]{1,0:T(8,128)(2,1)S(1)} %slice.24), channel_id=1, source_target_pairs={{0,8},{1,9},{2,10},{3,11},{4,12},{5,13},{6,14},{7,15},{8,0},{9,1},... | collective-permute-start | bytes 589832 | tf_op jit(solution)/shard_map/ppermute | solution.py:552
  35.5 0.0 collective-permute-done.5.own_ref
  35.5 0.2 collective-permute-done.6
  35.7 0.0 collective-permute-done.7
  35.7 3.7 %collective-permute-done.11.q3b_ref = bf16[192,512]{1,0:T(8,128)(2,1)S(1)} collective-permute-done((bf16[192,512]{1,0:T(8,128)(2,1)S(1)}, bf16[192,512]{1,0:T(8,128)(2,1)S(1)}, u32[]{:S(2)}, u32[]{:S(2)}) %collective-permute-start.11) | collective-permute-done | bytes 196640 | tf_op jit(solution)/shard_map/ppermute | solution.py:552
  39.5 1.3 %collective-permute-done.9.q3a_ref = bf16[192,512]{1,0:T(8,128)(2,1)S(1)} collective-permute-done((bf16[192,512]{1,0:T(8,128)(2,1)S(1)}, bf16[192,512]{1,0:T(8,128)(2,1)S(1)}, u32[]{:S(2)}, u32[]{:S(2)}) %collective-permute-start.9) | collective-permute-done | bytes 196640 | tf_op jit(solution)/shard_map/ppermute | solution.py:552
  40.8 0.0 copy-start.4
  40.8 0.1 collective-permute-start.13
  40.9 0.5 collective-permute-start.12
  41.4 1.4 %shard_map.96.probe_ref = bf16[2,2,512,512]{3,2,1,0:T(8,128)(2,1)S(1)} custom-call(s32[5]{0:T(128)S(1)} %stack.23.place_ref, bf16[2,8,128,512]{3,2,1,0:T(8,128)(2,1)S(1)} %copy-done.6, bf16[384,512]{1,0:T(8,128)(2,1)S(1)} %pad_maximum_fusion.q0_ref, bf16[384,512]{1,0:T(8,128)(2,1)S(1)} %collective-permute-done.10.q1_ref, ...), custom_call_target="tpu_custom_call" | custom-call | tf_op jit(solution)/shard_map/pallas_call | solution.py:599
  42.8 0.0 collective-permute-done.13.mate_side_ref
  42.8 0.2 collective-permute-done.12.mate_own_ref
  43.0 5.1 %shard_map.97 = (bf16[2,2,3,512,256]{4,3,2,1,0:T(8,128)(2,1)S(1)}, bf16[2,2,512,256]{3,2,1,0:T(8,128)(2,1)S(1)}, bf16[512,256]{1,0:T(8,128)(2,1)S(1)}) custom-call(s32[5]{0:T(128)S(1)} %stack.23.place_ref, bf16[2,160,512]{2,1,0:T(8,128)(2,1)S(1)} %collective-permute-done.5.own_ref, bf16[2,160,512]{2,1,0:T(8,128)(2,1)S(1)} %broadcast_select_fusion.side_ref, ...), custom_call_target="tpu_custom_call" | custom-call | flops 3221225472 | bytes 16777216 | tf_op jit(solution)/shard_map/pallas_call | solution.py:614
  48.2 0.2 collective-permute-start.14
  48.4 1.6 %shard_map.98 = (bf16[2,2,512,256]{3,2,1,0:T(8,128)(2,1)S(1)}, f32[512,256]{1,0:T(8,128)S(1)}) custom-call(s32[5]{0:T(128)S(1)} %stack.23.place_ref, bf16[2,2,3,512,256]{4,3,2,1,0:T(8,128)(2,1)S(1)} %get-tuple-element.35.turned_ref, bf16[128,512]{1,0:T(8,128)(2,1)S(1)} %collective-permute-done.2.measured_ref, bf16[3,512,512]{2,1,0:T(8,128)(2,1)S(1)} %copy-done.4), custom_call_target="tpu_custom_call" | custom-call | flops 1073741824 | bytes 4194304 | tf_op jit(solution)/shard_map/pallas_call | solution.py:629
  50.0 0.0 collective-permute-done.14
  50.0 0.1 fusion.2
  50.1 3.6 %collective-permute-start.15 = (bf16[512,256]{1,0:T(8,128)(2,1)S(1)}, bf16[512,256]{1,0:T(8,128)(2,1)S(1)}, u32[]{:S(2)}, u32[]{:S(2)}) collective-permute-start(bf16[512,256]{1,0:T(8,128)(2,1)S(1)} %fusion.2), channel_id=1, source_target_pairs={{0,1},{1,0},{2,3},{3,2},{4,5},{5,4},{6,7},{7,6},{8,9},{9,8},{10,11... | collective-permute-start | bytes 786440 | tf_op jit(solution)/shard_map/ppermute | solution.py:552
  53.6 6.6 %collective-permute-done.15 = bf16[512,256]{1,0:T(8,128)(2,1)S(1)} collective-permute-done((bf16[512,256]{1,0:T(8,128)(2,1)S(1)}, bf16[512,256]{1,0:T(8,128)(2,1)S(1)}, u32[]{:S(2)}, u32[]{:S(2)}) %collective-permute-start.15) | collective-permute-done | bytes 262176 | tf_op jit(solution)/shard_map/ppermute | solution.py:552
  60.2 0.1 fusion.4
  60.3 0.1 collective-permute-start.16
  60.4 1.1 %shard_map.99.own_ref = bf16[3,1024,256]{2,1,0:T(8,128)(2,1)S(1)} custom-call(bf16[2,2,512,256]{3,2,1,0:T(8,128)(2,1)S(1)} %get-tuple-element.38.far_ref, f32[512,256]{1,0:T(8,128)S(1)} %get-tuple-element.45.mine_ref, bf16[3,512,512]{2,1,0:T(8,128)(2,1)S(1)} %copy-done.4), custom_call_target="tpu_custom_call" | custom-call | flops 1073741824 | bytes 4194304 | tf_op jit(solution)/shard_map/pallas_call | solution.py:641
  61.6 0.4 collective-permute-done.16.mates_ref
  61.9 4.9 %shard_map.100 = (bf16[2,2,160,512]{3,2,1,0:T(8,128)(2,1)S(1)}, bf16[2,160,512]{2,1,0:T(8,128)(2,1)S(1)}, bf16[2,160,512]{2,1,0:T(8,128)(2,1)S(1)}) custom-call(s32[5]{0:T(128)S(1)} %stack.23.place_ref, bf16[2,2,512,256]{3,2,1,0:T(8,128)(2,1)S(1)} %get-tuple-element.34.far_ref, bf16[2,2,512,512]{3,2,1,0:T(8,128)(2,1)S(1)} %shard_map.96.probe_ref, ...), custom_call_target="tpu_custom_call" | custom-call | flops 3221225472 | bytes 12582912 | tf_op jit(solution)/shard_map/pallas_call | solution.py:650
  66.8 0.2 collective-permute-start.17
  67.0 1.9 %collective-permute-done.17 = bf16[2,2,160,512]{3,2,1,0:T(8,128)(2,1)S(1)} collective-permute-done((bf16[2,2,160,512]{3,2,1,0:T(8,128)(2,1)S(1)}, bf16[2,2,160,512]{3,2,1,0:T(8,128)(2,1)S(1)}, u32[]{:S(2)}, u32[]{:S(2)}) %collective-permute-start.17) | collective-permute-done | bytes 655392 | tf_op jit(solution)/shard_map/ppermute | solution.py:552
  69.0 0.2 fusion.1
  69.1 3.6 %collective-permute-start.18 = (bf16[2,160,512]{2,1,0:T(8,128)(2,1)S(1)}, bf16[2,160,512]{2,1,0:T(8,128)(2,1)S(1)}, u32[]{:S(2)}, u32[]{:S(2)}) collective-permute-start(bf16[2,160,512]{2,1,0:T(8,128)(2,1)S(1)} %get-tuple-element.49), channel_id=1, source_target_pairs={{0,1},{1,0},{6,7},{7,6},{8,9},{9,8},{14,15},{15,14},{16,17},{17,16... | collective-permute-start | bytes 983048 | tf_op jit(solution)/shard_map/ppermute | solution.py:552
  72.8 0.0 copy-start.8
  72.8 0.7 collective-permute-start.19
  73.5 0.9 collective-permute-start.20
  74.4 1.8 %shard_map.101.row_ref = f32[1,128]{1,0:T(1,128)S(1)} custom-call(f32[4,2,160,640]{3,2,1,0:T(8,128)S(1)} %copy-done, f32[3,2,160,640]{3,2,1,0:T(8,128)S(1)} %copy-done.1), custom_call_target="tpu_custom_call" | custom-call | flops 18022400 | bytes 5734400 | tf_op jit(solution)/shard_map/pallas_call | solution.py:672
  76.1 0.0 copy-start.3
  76.1 0.0 copy-start.5
  76.2 4.6 %collective-permute-done.18 = bf16[2,160,512]{2,1,0:T(8,128)(2,1)S(1)} collective-permute-done((bf16[2,160,512]{2,1,0:T(8,128)(2,1)S(1)}, bf16[2,160,512]{2,1,0:T(8,128)(2,1)S(1)}, u32[]{:S(2)}, u32[]{:S(2)}) %collective-permute-start.18) | collective-permute-done | bytes 327712 | tf_op jit(solution)/shard_map/ppermute | solution.py:552
  80.8 0.0 collective-permute-done.20
  80.8 0.2 fusion.3.data_ref
  81.0 2.5 %shard_map.102 = (f32[2,160,640]{2,1,0:T(8,128)S(1)}, f32[32,128]{1,0:T(8,128)S(1)}) custom-call(s32[1,2]{1,0:T(1,128)S(1)} %copy-done.8, bf16[2,160,512]{2,1,0:T(8,128)(2,1)S(1)} %fusion.3.data_ref, f32[2,160,640]{2,1,0:T(8,128)S(1)} %copy-done.3, f32[2,160,640]{2,1,0:T(8,128)S(1)} %copy-done.5, f32[4,2,160,640]{3,2,1,0:T(8,128)S(1)} %copy-done, ...), custom_call_target="tpu_custom_call" | custom-call | flops 13107200 | bytes 8192000 | tf_op jit(solution)/shard_map/pallas_call | solution.py:680
  83.5 16.9 %all_to_all.5 = f32[32,1,128]{2,1,0:T(1,128)S(1)} all-to-all(f32[32,1,128]{2,1,0:T(1,128)S(1)} %bitcast.28), channel_id=1, replica_groups=mesh['region'=8,'grp'=4] {'region','grp'}, dimensions={0} | all-to-all | bytes 32768 | tf_op jit(solution)/shard_map/all_to_all | solution.py:689
  100.4 1.5 %shard_map.103 = (f32[2,160,640]{2,1,0:T(8,128)}, f32[2,160,640]{2,1,0:T(8,128)}) custom-call(f32[32,128]{1,0:T(8,128)S(1)} %bitcast.27, f32[2,160,640]{2,1,0:T(8,128)S(1)} %copy-done.3, f32[2,160,640]{2,1,0:T(8,128)S(1)} %get-tuple-element.43.gradient_ref, f32[2,160,640]{2,1,0:T(8,128)S(1)} %copy-done.5, f32[4,2,160,640]{3,2,1,0:T(8,128)S(1)} %copy-done, ...), custom_call_target="tpu_custom_call" | custom-call | flops 8192000 | bytes 9011200 | tf_op jit(solution)/shard_map/pallas_call | solution.py:692
  (19 shorter events, 0.1 us)
Async XLA Ops:
  1.6 6.7 %collective-permute-start.1 = (bf16[128,512]{1,0:T(8,128)(2,1)S(1)}, bf16[128,512]{1,0:T(8,128)(2,1)S(1)}, u32[]{:S(2)}, u32[]{:S(2)}) collective-permute-start(bf16[128,512]{1,0:T(8,128)(2,1)S(1)} %get-tuple-element.47), channel_id=1, source_target_pairs={{0,1},{1,0},{2,3},{3,2},{4,5},{5,4},{6,7},{7,6},{8,9},{9,8},{10,11... | collective-permute-start | bytes 393224 | tf_op jit(solution)/shard_map/ppermute | solution.py:552
  4.7 15.5 %collective-permute-start.4 = (bf16[128,512]{1,0:T(8,128)(2,1)S(1)}, bf16[128,512]{1,0:T(8,128)(2,1)S(1)}, u32[]{:S(2)}, u32[]{:S(2)}) collective-permute-start(bf16[128,512]{1,0:T(8,128)(2,1)S(1)} %get-tuple-element.47), channel_id=1, source_target_pairs={{0,3},{1,2},{2,1},{3,0},{4,7},{5,6},{6,5},{7,4},{8,11},{9,10},{10,... | collective-permute-start | bytes 393224 | tf_op jit(solution)/shard_map/ppermute | solution.py:552
  7.2 13.2 %collective-permute-start.3 = (bf16[128,512]{1,0:T(8,128)(2,1)S(1)}, bf16[128,512]{1,0:T(8,128)(2,1)S(1)}, u32[]{:S(2)}, u32[]{:S(2)}) collective-permute-start(bf16[128,512]{1,0:T(8,128)(2,1)S(1)} %get-tuple-element.46), channel_id=1, source_target_pairs={{0,2},{1,3},{2,0},{3,1},{4,6},{5,7},{6,4},{7,5},{8,10},{9,11},{10,... | collective-permute-start | bytes 393224 | tf_op jit(solution)/shard_map/ppermute | solution.py:552
  8.3 12.1 %collective-permute-start.2 = (bf16[128,512]{1,0:T(8,128)(2,1)S(1)}, bf16[128,512]{1,0:T(8,128)(2,1)S(1)}, u32[]{:S(2)}, u32[]{:S(2)}) collective-permute-start(bf16[128,512]{1,0:T(8,128)(2,1)S(1)} %convert_bitcast_fusion), channel_id=1, source_target_pairs={{0,0},{1,1},{2,4},{3,5},{4,2},{5,3},{6,6},{7,7},{8,8},{9,9},{10,12... | collective-permute-start | bytes 393224 | tf_op jit(solution)/shard_map/ppermute | solution.py:552
  9.0 9.3 %collective-permute-start = (s32[1,2]{1,0:T(1,128)}, s32[1,2]{1,0:T(1,128)S(1)}, u32[]{:S(2)}, u32[]{:S(2)}) collective-permute-start(s32[1,2]{1,0:T(1,128)} %pos_ref.3), channel_id=1, source_target_pairs={{0,4},{1,5},{2,6},{3,7},{4,0},{5,1},{6,2},{7,3},{8,12},{9,13},{10,... | collective-permute-start | bytes 32 | tf_op jit(solution)/shard_map/ppermute | solution.py:552
  15.5 1.1 %copy-start.2 = (f32[2,160,640]{2,1,0:T(8,128)S(1)}, f32[2,160,640]{2,1,0:T(8,128)}, u32[]{:S(2)}) copy-start(f32[2,160,640]{2,1,0:T(8,128)} %transmission_ref.3) | copy-start | bytes 2457604
  16.6 0.7 copy-start.7
  17.3 24.2 %copy-start.6 = (bf16[2,8,128,512]{3,2,1,0:T(8,128)(2,1)S(1)}, bf16[2,8,128,512]{3,2,1,0:T(8,128)(2,1)}, u32[]{:S(2)}) copy-start(bf16[2,8,128,512]{3,2,1,0:T(8,128)(2,1)} %all_ref.1) | copy-start | bytes 6291460
  20.4 11.9 %collective-permute-start.10 = (bf16[384,512]{1,0:T(8,128)(2,1)S(1)}, bf16[384,512]{1,0:T(8,128)(2,1)S(1)}, u32[]{:S(2)}, u32[]{:S(2)}) collective-permute-start(bf16[384,512]{1,0:T(8,128)(2,1)S(1)} %pad_maximum_fusion.q0_ref), channel_id=1, source_target_pairs={{0,8},{1,9},{2,10},{3,11},{4,12},{5,13},{6,14},{7,15},{8,0},{9,1},... | collective-permute-start | bytes 1179656 | tf_op jit(solution)/shard_map/ppermute | solution.py:552
  22.0 12.0 %collective-permute-start.8 = (bf16[384,512]{1,0:T(8,128)(2,1)S(1)}, bf16[384,512]{1,0:T(8,128)(2,1)S(1)}, u32[]{:S(2)}, u32[]{:S(2)}) collective-permute-start(bf16[384,512]{1,0:T(8,128)(2,1)S(1)} %pad_maximum_fusion.q0_ref), channel_id=1, source_target_pairs={{0,16},{1,17},{2,18},{3,19},{4,20},{5,21},{6,22},{7,23},{8,24},{9,... | collective-permute-start | bytes 1179656 | tf_op jit(solution)/shard_map/ppermute | solution.py:552
  23.5 12.0 %collective-permute-start.5 = (bf16[2,160,512]{2,1,0:T(8,128)(2,1)S(1)}, bf16[2,160,512]{2,1,0:T(8,128)(2,1)S(1)}, u32[]{:S(2)}, u32[]{:S(2)}) collective-permute-start(bf16[2,160,512]{2,1,0:T(8,128)(2,1)S(1)} %shard_map.95), channel_id=1, source_target_pairs={{0,0},{1,1},{2,4},{3,5},{4,2},{5,3},{6,6},{7,7},{8,8},{9,9},{10,12... | collective-permute-start | bytes 983048 | tf_op jit(solution)/shard_map/ppermute | solution.py:552
  24.2 11.6 %collective-permute-start.6 = (bf16[2,160,512]{2,1,0:T(8,128)(2,1)S(1)}, bf16[2,160,512]{2,1,0:T(8,128)(2,1)S(1)}, u32[]{:S(2)}, u32[]{:S(2)}) collective-permute-start(bf16[2,160,512]{2,1,0:T(8,128)(2,1)S(1)} %shard_map.95), channel_id=1, source_target_pairs={{0,1},{1,0},{6,7},{7,6},{8,9},{9,8},{14,15},{15,14},{16,17},{17,16... | collective-permute-start | bytes 983048 | tf_op jit(solution)/shard_map/ppermute | solution.py:552
  28.5 7.2 %collective-permute-start.7 = (bf16[2,160,512]{2,1,0:T(8,128)(2,1)S(1)}, bf16[2,160,512]{2,1,0:T(8,128)(2,1)S(1)}, u32[]{:S(2)}, u32[]{:S(2)}) collective-permute-start(bf16[2,160,512]{2,1,0:T(8,128)(2,1)S(1)} %shard_map.95), channel_id=1, source_target_pairs={{2,5},{3,4},{4,3},{5,2},{10,13},{11,12},{12,11},{13,10},{18,21},{1... | collective-permute-start | bytes 983048 | tf_op jit(solution)/shard_map/ppermute | solution.py:552
  32.3 7.1 %collective-permute-start.11 = (bf16[192,512]{1,0:T(8,128)(2,1)S(1)}, bf16[192,512]{1,0:T(8,128)(2,1)S(1)}, u32[]{:S(2)}, u32[]{:S(2)}) collective-permute-start(bf16[192,512]{1,0:T(8,128)(2,1)S(1)} %slice.25), channel_id=1, source_target_pairs={{0,16},{1,17},{2,18},{3,19},{4,20},{5,21},{6,22},{7,23},{8,24},{9,... | collective-permute-start | bytes 589832 | tf_op jit(solution)/shard_map/ppermute | solution.py:552
  33.9 6.9 %collective-permute-start.9 = (bf16[192,512]{1,0:T(8,128)(2,1)S(1)}, bf16[192,512]{1,0:T(8,128)(2,1)S(1)}, u32[]{:S(2)}, u32[]{:S(2)}) collective-permute-start(bf16[192,512]{1,0:T(8,128)(2,1)S(1)} %slice.24), channel_id=1, source_target_pairs={{0,8},{1,9},{2,10},{3,11},{4,12},{5,13},{6,14},{7,15},{8,0},{9,1},... | collective-permute-start | bytes 589832 | tf_op jit(solution)/shard_map/ppermute | solution.py:552
  40.8 2.2 %copy-start.4 = (bf16[3,512,512]{2,1,0:T(8,128)(2,1)S(1)}, bf16[3,512,512]{2,1,0:T(8,128)(2,1)}, u32[]{:S(2)}) copy-start(bf16[3,512,512]{2,1,0:T(8,128)(2,1)} %constant.23.clone.right_ref) | copy-start | bytes 4718596
  40.8 2.0 %collective-permute-start.13 = (bf16[2,160,512]{2,1,0:T(8,128)(2,1)S(1)}, bf16[2,160,512]{2,1,0:T(8,128)(2,1)S(1)}, u32[]{:S(2)}, u32[]{:S(2)}) collective-permute-start(bf16[2,160,512]{2,1,0:T(8,128)(2,1)S(1)} %broadcast_select_fusion.side_ref), channel_id=1, source_target_pairs={{0,4},{1,5},{2,6},{3,7},{4,0},{5,1},{6,2},{7,3},{8,12},{9,13},{10,... | collective-permute-start | bytes 983048 | tf_op jit(solution)/shard_map/ppermute | solution.py:552
  40.9 2.1 %collective-permute-start.12 = (bf16[2,160,512]{2,1,0:T(8,128)(2,1)S(1)}, bf16[2,160,512]{2,1,0:T(8,128)(2,1)S(1)}, u32[]{:S(2)}, u32[]{:S(2)}) collective-permute-start(bf16[2,160,512]{2,1,0:T(8,128)(2,1)S(1)} %collective-permute-done.5.own_ref), channel_id=1, source_target_pairs={{0,4},{1,5},{2,6},{3,7},{4,0},{5,1},{6,2},{7,3},{8,12},{9,13},{10,... | collective-permute-start | bytes 983048 | tf_op jit(solution)/shard_map/ppermute | solution.py:552
  48.2 1.8 %collective-permute-start.14 = (bf16[512,256]{1,0:T(8,128)(2,1)S(1)}, bf16[512,256]{1,0:T(8,128)(2,1)S(1)}, u32[]{:S(2)}, u32[]{:S(2)}) collective-permute-start(bf16[512,256]{1,0:T(8,128)(2,1)S(1)} %get-tuple-element.37), channel_id=1, source_target_pairs={{0,4},{1,5},{2,6},{3,7},{4,0},{5,1},{6,2},{7,3},{8,12},{9,13},{10,... | collective-permute-start | bytes 786440 | tf_op jit(solution)/shard_map/ppermute | solution.py:552
  50.1 10.2 %collective-permute-start.15 = (bf16[512,256]{1,0:T(8,128)(2,1)S(1)}, bf16[512,256]{1,0:T(8,128)(2,1)S(1)}, u32[]{:S(2)}, u32[]{:S(2)}) collective-permute-start(bf16[512,256]{1,0:T(8,128)(2,1)S(1)} %fusion.2), channel_id=1, source_target_pairs={{0,1},{1,0},{2,3},{3,2},{4,5},{5,4},{6,7},{7,6},{8,9},{9,8},{10,11... | collective-permute-start | bytes 786440 | tf_op jit(solution)/shard_map/ppermute | solution.py:552
  60.3 1.6 %collective-permute-start.16 = (bf16[512,256]{1,0:T(8,128)(2,1)S(1)}, bf16[512,256]{1,0:T(8,128)(2,1)S(1)}, u32[]{:S(2)}, u32[]{:S(2)}) collective-permute-start(bf16[512,256]{1,0:T(8,128)(2,1)S(1)} %get-tuple-element.44), channel_id=1, source_target_pairs={{0,4},{1,5},{2,6},{3,7},{4,0},{5,1},{6,2},{7,3},{8,12},{9,13},{10,... | collective-permute-start | bytes 786440 | tf_op jit(solution)/shard_map/ppermute | solution.py:552
  61.9 12.4 %copy-start = (f32[4,2,160,640]{3,2,1,0:T(8,128)S(1)}, f32[4,2,160,640]{3,2,1,0:T(8,128)}, u32[]{:S(2)}) copy-start(f32[4,2,160,640]{3,2,1,0:T(8,128)} %steps_ref.5) | copy-start | bytes 9830404
  61.9 12.4 %copy-start.1 = (f32[3,2,160,640]{3,2,1,0:T(8,128)S(1)}, f32[3,2,160,640]{3,2,1,0:T(8,128)}, u32[]{:S(2)}) copy-start(f32[3,2,160,640]{3,2,1,0:T(8,128)} %changes_ref.5) | copy-start | bytes 7372804
  66.8 2.2 %collective-permute-start.17 = (bf16[2,2,160,512]{3,2,1,0:T(8,128)(2,1)S(1)}, bf16[2,2,160,512]{3,2,1,0:T(8,128)(2,1)S(1)}, u32[]{:S(2)}, u32[]{:S(2)}) collective-permute-start(bf16[2,2,160,512]{3,2,1,0:T(8,128)(2,1)S(1)} %get-tuple-element.40), channel_id=1, source_target_pairs={{0,4},{1,5},{2,6},{3,7},{4,0},{5,1},{6,2},{7,3},{8,12},{9,13},{10,... | collective-permute-start | bytes 1966088 | tf_op jit(solution)/shard_map/ppermute | solution.py:552
  69.1 11.6 %collective-permute-start.18 = (bf16[2,160,512]{2,1,0:T(8,128)(2,1)S(1)}, bf16[2,160,512]{2,1,0:T(8,128)(2,1)S(1)}, u32[]{:S(2)}, u32[]{:S(2)}) collective-permute-start(bf16[2,160,512]{2,1,0:T(8,128)(2,1)S(1)} %get-tuple-element.49), channel_id=1, source_target_pairs={{0,1},{1,0},{6,7},{7,6},{8,9},{9,8},{14,15},{15,14},{16,17},{17,16... | collective-permute-start | bytes 983048 | tf_op jit(solution)/shard_map/ppermute | solution.py:552
  72.8 8.2 %copy-start.8 = (s32[1,2]{1,0:T(1,128)S(1)}, s32[1,2]{1,0:T(1,128)}, u32[]{:S(2)}) copy-start(s32[1,2]{1,0:T(1,128)} %pos_ref.3) | copy-start | bytes 28
  72.8 8.0 %collective-permute-start.19 = (bf16[2,160,512]{2,1,0:T(8,128)(2,1)S(1)}, bf16[2,160,512]{2,1,0:T(8,128)(2,1)S(1)}, u32[]{:S(2)}, u32[]{:S(2)}) collective-permute-start(bf16[2,160,512]{2,1,0:T(8,128)(2,1)S(1)} %get-tuple-element.48), channel_id=1, source_target_pairs={{2,4},{3,5},{4,2},{5,3},{10,12},{11,13},{12,10},{13,11},{18,20},{1... | collective-permute-start | bytes 983048 | tf_op jit(solution)/shard_map/ppermute | solution.py:552
  73.5 7.3 %collective-permute-start.20 = (bf16[2,160,512]{2,1,0:T(8,128)(2,1)S(1)}, bf16[2,160,512]{2,1,0:T(8,128)(2,1)S(1)}, u32[]{:S(2)}, u32[]{:S(2)}) collective-permute-start(bf16[2,160,512]{2,1,0:T(8,128)(2,1)S(1)} %get-tuple-element.49), channel_id=1, source_target_pairs={{2,5},{3,4},{4,3},{5,2},{10,13},{11,12},{12,11},{13,10},{18,21},{1... | collective-permute-start | bytes 983048 | tf_op jit(solution)/shard_map/ppermute | solution.py:552
  76.1 4.8 %copy-start.3 = (f32[2,160,640]{2,1,0:T(8,128)S(1)}, f32[2,160,640]{2,1,0:T(8,128)}, u32[]{:S(2)}) copy-start(f32[2,160,640]{2,1,0:T(8,128)} %transmission_ref.3) | copy-start | bytes 2457604
  76.1 4.8 %copy-start.5 = (f32[2,160,640]{2,1,0:T(8,128)S(1)}, f32[2,160,640]{2,1,0:T(8,128)}, u32[]{:S(2)}) copy-start(f32[2,160,640]{2,1,0:T(8,128)} %old_ref.3) | copy-start | bytes 2457604

commit v5 on v4

--- a/solution.py
+++ b/solution.py
@@ -534,21 +534,20 @@
     return region % 2 == member // 2
 
 
-def away(region, member):
-    return not at_home(region, member)
+def beside(region, member):
+    return (region, member ^ 1) if at_home(region, member) else (region ^ 1, member ^ 3)
 
 
 def fast(mesh, transmission, probe, measured, positions, past_steps, past_changes, old_gradient):
     regions, members = mesh.shape["region"], mesh.shape["grp"]
     barrier = lax.optimization_barrier
 
-    def send(value, target, chosen=lambda region, member: True):
+    def send(value, target):
         pairs = []
         for region in range(regions):
             for member in range(members):
-                if chosen(region, member):
-                    to_region, to_member = target(region, member)
-                    pairs.append((region * members + member, to_region * members + to_member))
+                to_region, to_member = target(region, member)
+                pairs.append((region * members + member, to_region * members + to_member))
         return lax.ppermute(value, AXES, pairs)
 
     near = lambda region, member: (region, member ^ 1)
@@ -558,7 +557,6 @@
     along_x = lambda region, member: (region ^ 2, member)
     along_y = lambda region, member: (region ^ 4, member)
     diagonal = lambda region, member: (region ^ 6, member)
-    home_near = lambda region, member: (region ^ 1, member ^ 3)
 
     region, member = lax.axis_index("region"), lax.axis_index("grp")
     core, half, line = region & 1, member & 1, (region >> 1) & 3
@@ -589,12 +587,10 @@
     piece, place, target, q0 = barrier((piece, place, target, q0))
     q1, q2 = send(q0, along_x), send(q0, along_y)
     own = send(piece, home)
-    beside = send(piece, near, at_home)
-    further = send(piece, home_near, away)
+    side = send(piece, beside)
     cut = q0.shape[0] // 2
     q3a, q3b = send(q2[:cut], along_x), send(q1[cut:], along_y)
-    own, beside, further, q3a, q3b = barrier((own, beside, further, q3a, q3b))
-    side = jnp.where(is_home, beside, further)
+    own, side, q3a, q3b = barrier((own, side, q3a, q3b))
     mate_own, mate_side = send(own, mate), send(side, mate)
     whole_probe = call(
         probe_kernel,
@@ -663,9 +659,7 @@
     met = send(sent, mate)
     add = lambda a, b: (a.astype(F32) + b.astype(F32)).astype(BF)
     kept_side, kept = add(kept_side, met[0]), add(kept, met[1])
-    first, second = send(kept, home, away), send(kept_side, home_near, away)
-    beside = send(kept_side, near, at_home)
-    data = jnp.where(is_home, add(kept, beside), add(first, second))
+    data = add(send(kept, home), send(kept_side, beside))
 
     devices = regions * members
     moved = 4 * 2 * piece_len * tile_len

time: 102 us -> 102 us (level)
  starting transfers between devices: 33.3 us -> 28.2 us
  waiting for transfers between devices: 22.3 us -> 26.8 us
    ppermute x21 -> x19, starting transfers between devices: 33.3 us -> 28.2 us  [send(): return lax.ppermute(value, AXES, pairs)]
    ppermute x21 -> x19, waiting for transfers between devices: 22.3 us -> 26.8 us  [send(): return lax.ppermute(value, AXES, pairs)]
  transfers between devices with their start and end apart: 21 -> 19, of which waited for: 10 -> 9; matrix products, arithmetic and copies ran while one was open for 3% -> 3% of each run, Pallas kernels for 7% -> 7%
where the time goes in v5:
time: 102 us
  starting transfers between devices  28.2 us (28%)
  waiting for transfers between devices  26.8 us (26%)
  Pallas kernels  20.8 us (20%)
  blocking collectives  17.4 us (17%)
  local copies, waits for them, and re-layouts  4.82 us (5%)
  between operations  2.29 us (2%)
  other arithmetic  1.43 us (1%)
    ppermute x19, starting transfers between devices, send(): return lax.ppermute(value, AXES, pairs)  28.2 us
    ppermute x19, waiting for transfers between devices, send(): return lax.ppermute(value, AXES, pairs)  26.8 us
    all_to_all x1, blocking collectives, fast(): lax.all_to_all(row.reshape(devices, 1, LANES), AXES, split_axis=0, concat...  17.4 us
    pallas_call x1, Pallas kernels, fast(): call(forward_kernel, (size((2, 2, 3, frame_len, half_len), BF), half_fiel...  5.14 us
    pallas_call x1, Pallas kernels, fast(): call(backward_kernel, (size((2, 2, piece_len, frame_len), BF), piece_shap...  4.85 us
    pallas_call x1, Pallas kernels, fast(): call(gradient_kernel, (size(transmission.shape, F32), size((devices, LANE...  2.49 us
  transfers between devices with their start and end apart: 19, of which 9 were waited for; matrix products, arithmetic and copies ran while one was open for 3% of the time, Pallas kernels for 7%

profile of v5, /device:TPU:0, one launch (start us, length us, event | category | flops | bytes accessed | tf_op | source)
XLA Modules:
  0.0 101.7 jit_solution(13704324557970053296)
XLA Ops:
  0.6 1.0 dynamic-slice_bitcast_fusion
  1.6 3.1 %collective-permute-start.1 = (bf16[128,512]{1,0:T(8,128)(2,1)S(1)}, bf16[128,512]{1,0:T(8,128)(2,1)S(1)}, u32[]{:S(2)}, u32[]{:S(2)}) collective-permute-start(bf16[128,512]{1,0:T(8,128)(2,1)S(1)} %get-tuple-element.45), channel_id=1, source_target_pairs={{0,1},{1,0},{2,3},{3,2},{4,5},{5,4},{6,7},{7,6},{8,9},{9,8},{10,11... | collective-permute-start | bytes 393224 | tf_op jit(solution)/shard_map/ppermute | solution.py:551
  4.7 2.5 %collective-permute-start.4 = (bf16[128,512]{1,0:T(8,128)(2,1)S(1)}, bf16[128,512]{1,0:T(8,128)(2,1)S(1)}, u32[]{:S(2)}, u32[]{:S(2)}) collective-permute-start(bf16[128,512]{1,0:T(8,128)(2,1)S(1)} %get-tuple-element.45), channel_id=1, source_target_pairs={{0,3},{1,2},{2,1},{3,0},{4,7},{5,6},{6,5},{7,4},{8,11},{9,10},{10,... | collective-permute-start | bytes 393224 | tf_op jit(solution)/shard_map/ppermute | solution.py:551
  7.2 0.1 collective-permute-start.3
  7.3 1.0 convert_bitcast_fusion
  8.3 0.0 collective-permute-done.1
  8.3 0.7 collective-permute-start.2
  9.0 5.2 %collective-permute-start = (s32[1,2]{1,0:T(1,128)}, s32[1,2]{1,0:T(1,128)S(1)}, u32[]{:S(2)}, u32[]{:S(2)}) collective-permute-start(s32[1,2]{1,0:T(1,128)} %pos_ref.3), channel_id=1, source_target_pairs={{0,4},{1,5},{2,6},{3,7},{4,0},{5,1},{6,2},{7,3},{8,12},{9,13},{10,... | collective-permute-start | bytes 32 | tf_op jit(solution)/shard_map/ppermute | solution.py:551
  14.2 1.3 %slice.18 = s32[1,1]{1,0:T(1,128)} slice(s32[1,2]{1,0:T(1,128)} %pos_ref.3), slice={[0:1], [1:2]} | slice | bytes 8 | tf_op jit(solution)/shard_map/slice | solution.py:585
  15.5 1.1 %copy-done.2 = f32[2,160,640]{2,1,0:T(8,128)S(1)} copy-done((f32[2,160,640]{2,1,0:T(8,128)S(1)}, f32[2,160,640]{2,1,0:T(8,128)}, u32[]{:S(2)}) %copy-start.2) | copy-done | bytes 819224
  16.7 0.7 copy-done.7
  17.3 1.0 shard_map.95
  18.3 0.0 collective-permute-done
  18.4 0.6 slice.19
  20.2 0.1 stack.23.place_ref
  20.3 0.0 collective-permute-done.4
  20.3 0.1 collective-permute-done.3
  20.4 0.0 collective-permute-done.2.measured_ref
  20.4 1.6 %collective-permute-start.9 = (bf16[384,512]{1,0:T(8,128)(2,1)S(1)}, bf16[384,512]{1,0:T(8,128)(2,1)S(1)}, u32[]{:S(2)}, u32[]{:S(2)}) collective-permute-start(bf16[384,512]{1,0:T(8,128)(2,1)S(1)} %pad_maximum_fusion.q0_ref), channel_id=1, source_target_pairs={{0,8},{1,9},{2,10},{3,11},{4,12},{5,13},{6,14},{7,15},{8,0},{9,1},... | collective-permute-start | bytes 1179656 | tf_op jit(solution)/shard_map/ppermute | solution.py:551
  22.0 1.5 %collective-permute-start.7 = (bf16[384,512]{1,0:T(8,128)(2,1)S(1)}, bf16[384,512]{1,0:T(8,128)(2,1)S(1)}, u32[]{:S(2)}, u32[]{:S(2)}) collective-permute-start(bf16[384,512]{1,0:T(8,128)(2,1)S(1)} %pad_maximum_fusion.q0_ref), channel_id=1, source_target_pairs={{0,16},{1,17},{2,18},{3,19},{4,20},{5,21},{6,22},{7,23},{8,24},{9,... | collective-permute-start | bytes 1179656 | tf_op jit(solution)/shard_map/ppermute | solution.py:551
  23.5 0.7 collective-permute-start.5
  24.2 2.5 %collective-permute-start.6 = (bf16[2,160,512]{2,1,0:T(8,128)(2,1)S(1)}, bf16[2,160,512]{2,1,0:T(8,128)(2,1)S(1)}, u32[]{:S(2)}, u32[]{:S(2)}) collective-permute-start(bf16[2,160,512]{2,1,0:T(8,128)(2,1)S(1)} %shard_map.95), channel_id=1, source_target_pairs={{0,1},{1,0},{2,5},{3,4},{4,3},{5,2},{6,7},{7,6},{8,9},{9,8},{10,13... | collective-permute-start | bytes 983048 | tf_op jit(solution)/shard_map/ppermute | solution.py:551
  26.6 5.7 %collective-permute-done.9.q1_ref = bf16[384,512]{1,0:T(8,128)(2,1)S(1)} collective-permute-done((bf16[384,512]{1,0:T(8,128)(2,1)S(1)}, bf16[384,512]{1,0:T(8,128)(2,1)S(1)}, u32[]{:S(2)}, u32[]{:S(2)}) %collective-permute-start.9) | collective-permute-done | bytes 393248 | tf_op jit(solution)/shard_map/ppermute | solution.py:551
  32.3 1.6 %collective-permute-start.10 = (bf16[192,512]{1,0:T(8,128)(2,1)S(1)}, bf16[192,512]{1,0:T(8,128)(2,1)S(1)}, u32[]{:S(2)}, u32[]{:S(2)}) collective-permute-start(bf16[192,512]{1,0:T(8,128)(2,1)S(1)} %slice.25), channel_id=1, source_target_pairs={{0,16},{1,17},{2,18},{3,19},{4,20},{5,21},{6,22},{7,23},{8,24},{9,... | collective-permute-start | bytes 589832 | tf_op jit(solution)/shard_map/ppermute | solution.py:551
  33.9 0.0 collective-permute-done.7.q2_ref
  33.9 0.0 copy-start.4
  33.9 1.6 %collective-permute-start.8 = (bf16[192,512]{1,0:T(8,128)(2,1)S(1)}, bf16[192,512]{1,0:T(8,128)(2,1)S(1)}, u32[]{:S(2)}, u32[]{:S(2)}) collective-permute-start(bf16[192,512]{1,0:T(8,128)(2,1)S(1)} %slice.24), channel_id=1, source_target_pairs={{0,8},{1,9},{2,10},{3,11},{4,12},{5,13},{6,14},{7,15},{8,0},{9,1},... | collective-permute-start | bytes 589832 | tf_op jit(solution)/shard_map/ppermute | solution.py:551
  35.5 0.0 collective-permute-done.5.own_ref
  35.5 0.0 collective-permute-done.6.side_ref
  35.5 4.0 %collective-permute-done.10.q3b_ref = bf16[192,512]{1,0:T(8,128)(2,1)S(1)} collective-permute-done((bf16[192,512]{1,0:T(8,128)(2,1)S(1)}, bf16[192,512]{1,0:T(8,128)(2,1)S(1)}, u32[]{:S(2)}, u32[]{:S(2)}) %collective-permute-start.10) | collective-permute-done | bytes 196640 | tf_op jit(solution)/shard_map/ppermute | solution.py:551
  39.5 1.3 %collective-permute-done.8.q3a_ref = bf16[192,512]{1,0:T(8,128)(2,1)S(1)} collective-permute-done((bf16[192,512]{1,0:T(8,128)(2,1)S(1)}, bf16[192,512]{1,0:T(8,128)(2,1)S(1)}, u32[]{:S(2)}, u32[]{:S(2)}) %collective-permute-start.8) | collective-permute-done | bytes 196640 | tf_op jit(solution)/shard_map/ppermute | solution.py:551
  40.8 0.0 collective-permute-start.11
  40.8 0.5 collective-permute-start.12
  41.3 0.0 copy-done.6
  41.3 1.4 %shard_map.96.probe_ref = bf16[2,2,512,512]{3,2,1,0:T(8,128)(2,1)S(1)} custom-call(s32[5]{0:T(128)S(1)} %stack.23.place_ref, bf16[2,8,128,512]{3,2,1,0:T(8,128)(2,1)S(1)} %copy-done.6, bf16[384,512]{1,0:T(8,128)(2,1)S(1)} %pad_maximum_fusion.q0_ref, bf16[384,512]{1,0:T(8,128)(2,1)S(1)} %collective-permute-done.9.q1_ref, ...), custom_call_target="tpu_custom_call" | custom-call | tf_op jit(solution)/shard_map/pallas_call | solution.py:595
  42.7 0.0 collective-permute-done.11.mate_own_ref
  42.7 0.2 collective-permute-done.12.mate_side_ref
  42.9 5.1 %shard_map.97 = (bf16[2,2,3,512,256]{4,3,2,1,0:T(8,128)(2,1)S(1)}, bf16[2,2,512,256]{3,2,1,0:T(8,128)(2,1)S(1)}, bf16[512,256]{1,0:T(8,128)(2,1)S(1)}) custom-call(s32[5]{0:T(128)S(1)} %stack.23.place_ref, bf16[2,160,512]{2,1,0:T(8,128)(2,1)S(1)} %collective-permute-done.5.own_ref, bf16[2,160,512]{2,1,0:T(8,128)(2,1)S(1)} %collective-permute-done.6.side_ref, ...), custom_call_target="tpu_custom_call" | custom-call | flops 3221225472 | bytes 16777216 | tf_op jit(solution)/shard_map/pallas_call | solution.py:610
  48.1 0.2 collective-permute-start.13
  48.3 1.6 %shard_map.98 = (bf16[2,2,512,256]{3,2,1,0:T(8,128)(2,1)S(1)}, f32[512,256]{1,0:T(8,128)S(1)}) custom-call(s32[5]{0:T(128)S(1)} %stack.23.place_ref, bf16[2,2,3,512,256]{4,3,2,1,0:T(8,128)(2,1)S(1)} %get-tuple-element.33.turned_ref, bf16[128,512]{1,0:T(8,128)(2,1)S(1)} %collective-permute-done.2.measured_ref, bf16[3,512,512]{2,1,0:T(8,128)(2,1)S(1)} %copy-done.4), custom_call_target="tpu_custom_call" | custom-call | flops 1073741824 | bytes 4194304 | tf_op jit(solution)/shard_map/pallas_call | solution.py:625
  49.9 0.0 collective-permute-done.13
  49.9 0.1 fusion.2
  50.0 3.6 %collective-permute-start.14 = (bf16[512,256]{1,0:T(8,128)(2,1)S(1)}, bf16[512,256]{1,0:T(8,128)(2,1)S(1)}, u32[]{:S(2)}, u32[]{:S(2)}) collective-permute-start(bf16[512,256]{1,0:T(8,128)(2,1)S(1)} %fusion.2), channel_id=1, source_target_pairs={{0,1},{1,0},{2,3},{3,2},{4,5},{5,4},{6,7},{7,6},{8,9},{9,8},{10,11... | collective-permute-start | bytes 786440 | tf_op jit(solution)/shard_map/ppermute | solution.py:551
  53.5 6.6 %collective-permute-done.14 = bf16[512,256]{1,0:T(8,128)(2,1)S(1)} collective-permute-done((bf16[512,256]{1,0:T(8,128)(2,1)S(1)}, bf16[512,256]{1,0:T(8,128)(2,1)S(1)}, u32[]{:S(2)}, u32[]{:S(2)}) %collective-permute-start.14) | collective-permute-done | bytes 262176 | tf_op jit(solution)/shard_map/ppermute | solution.py:551
  60.1 0.1 fusion.3
  60.2 0.1 collective-permute-start.15
  60.3 1.1 %shard_map.99.own_ref = bf16[3,1024,256]{2,1,0:T(8,128)(2,1)S(1)} custom-call(bf16[2,2,512,256]{3,2,1,0:T(8,128)(2,1)S(1)} %get-tuple-element.36.far_ref, f32[512,256]{1,0:T(8,128)S(1)} %get-tuple-element.43.mine_ref, bf16[3,512,512]{2,1,0:T(8,128)(2,1)S(1)} %copy-done.4), custom_call_target="tpu_custom_call" | custom-call | flops 1073741824 | bytes 4194304 | tf_op jit(solution)/shard_map/pallas_call | solution.py:637
  61.4 0.4 collective-permute-done.15.mates_ref
  61.8 4.8 %shard_map.100 = (bf16[2,2,160,512]{3,2,1,0:T(8,128)(2,1)S(1)}, bf16[2,160,512]{2,1,0:T(8,128)(2,1)S(1)}, bf16[2,160,512]{2,1,0:T(8,128)(2,1)S(1)}) custom-call(s32[5]{0:T(128)S(1)} %stack.23.place_ref, bf16[2,2,512,256]{3,2,1,0:T(8,128)(2,1)S(1)} %get-tuple-element.32.far_ref, bf16[2,2,512,512]{3,2,1,0:T(8,128)(2,1)S(1)} %shard_map.96.probe_ref, ...), custom_call_target="tpu_custom_call" | custom-call | flops 3221225472 | bytes 12582912 | tf_op jit(solution)/shard_map/pallas_call | solution.py:646
  66.7 0.2 collective-permute-start.16
  66.9 1.9 %collective-permute-done.16 = bf16[2,2,160,512]{3,2,1,0:T(8,128)(2,1)S(1)} collective-permute-done((bf16[2,2,160,512]{3,2,1,0:T(8,128)(2,1)S(1)}, bf16[2,2,160,512]{3,2,1,0:T(8,128)(2,1)S(1)}, u32[]{:S(2)}, u32[]{:S(2)}) %collective-permute-start.16) | collective-permute-done | bytes 655392 | tf_op jit(solution)/shard_map/ppermute | solution.py:551
  68.8 0.2 fusion.1
  69.0 0.9 collective-permute-start.17
  69.9 0.0 copy-start.3
  69.9 0.0 copy-start.5
  69.9 0.0 copy-start.8
  69.9 1.8 %collective-permute-start.18 = (bf16[2,160,512]{2,1,0:T(8,128)(2,1)S(1)}, bf16[2,160,512]{2,1,0:T(8,128)(2,1)S(1)}, u32[]{:S(2)}, u32[]{:S(2)}) collective-permute-start(bf16[2,160,512]{2,1,0:T(8,128)(2,1)S(1)} %get-tuple-element.47), channel_id=1, source_target_pairs={{0,1},{1,0},{2,5},{3,4},{4,3},{5,2},{6,7},{7,6},{8,9},{9,8},{10,13... | collective-permute-start | bytes 983048 | tf_op jit(solution)/shard_map/ppermute | solution.py:551
  71.7 1.7 %shard_map.101.row_ref = f32[1,128]{1,0:T(1,128)S(1)} custom-call(f32[4,2,160,640]{3,2,1,0:T(8,128)S(1)} %copy-done, f32[3,2,160,640]{3,2,1,0:T(8,128)S(1)} %copy-done.1), custom_call_target="tpu_custom_call" | custom-call | flops 18022400 | bytes 5734400 | tf_op jit(solution)/shard_map/pallas_call | solution.py:666
  73.5 0.0 collective-permute-done.17
  73.5 6.6 %collective-permute-done.18 = bf16[2,160,512]{2,1,0:T(8,128)(2,1)S(1)} collective-permute-done((bf16[2,160,512]{2,1,0:T(8,128)(2,1)S(1)}, bf16[2,160,512]{2,1,0:T(8,128)(2,1)S(1)}, u32[]{:S(2)}, u32[]{:S(2)}) %collective-permute-start.18) | collective-permute-done | bytes 327712 | tf_op jit(solution)/shard_map/ppermute | solution.py:551
  80.1 0.1 add_convert_fusion.data_ref
  80.2 2.5 %shard_map.102 = (f32[2,160,640]{2,1,0:T(8,128)S(1)}, f32[32,128]{1,0:T(8,128)S(1)}) custom-call(s32[1,2]{1,0:T(1,128)S(1)} %copy-done.8, bf16[2,160,512]{2,1,0:T(8,128)(2,1)S(1)} %add_convert_fusion.data_ref, f32[2,160,640]{2,1,0:T(8,128)S(1)} %copy-done.3, f32[2,160,640]{2,1,0:T(8,128)S(1)} %copy-done.5, f32[4,2,160,640]{3,2,1,0:T(8,128)S(1)} %copy-done, ...), custom_call_target="tpu_custom_call" | custom-call | flops 13107200 | bytes 8192000 | tf_op jit(solution)/shard_map/pallas_call | solution.py:674
  82.7 17.4 %all_to_all.5 = f32[32,1,128]{2,1,0:T(1,128)S(1)} all-to-all(f32[32,1,128]{2,1,0:T(1,128)S(1)} %bitcast.28), channel_id=1, replica_groups=mesh['region'=8,'grp'=4] {'region','grp'}, dimensions={0} | all-to-all | bytes 32768 | tf_op jit(solution)/shard_map/all_to_all | solution.py:683
  100.1 1.5 %shard_map.103 = (f32[2,160,640]{2,1,0:T(8,128)}, f32[2,160,640]{2,1,0:T(8,128)}) custom-call(f32[32,128]{1,0:T(8,128)S(1)} %bitcast.27, f32[2,160,640]{2,1,0:T(8,128)S(1)} %copy-done.3, f32[2,160,640]{2,1,0:T(8,128)S(1)} %get-tuple-element.41.gradient_ref, f32[2,160,640]{2,1,0:T(8,128)S(1)} %copy-done.5, f32[4,2,160,640]{3,2,1,0:T(8,128)S(1)} %copy-done, ...), custom_call_target="tpu_custom_call" | custom-call | flops 8192000 | bytes 9011200 | tf_op jit(solution)/shard_map/pallas_call | solution.py:686
  (14 shorter events, 0.1 us)
Async XLA Ops:
  1.6 6.7 %collective-permute-start.1 = (bf16[128,512]{1,0:T(8,128)(2,1)S(1)}, bf16[128,512]{1,0:T(8,128)(2,1)S(1)}, u32[]{:S(2)}, u32[]{:S(2)}) collective-permute-start(bf16[128,512]{1,0:T(8,128)(2,1)S(1)} %get-tuple-element.45), channel_id=1, source_target_pairs={{0,1},{1,0},{2,3},{3,2},{4,5},{5,4},{6,7},{7,6},{8,9},{9,8},{10,11... | collective-permute-start | bytes 393224 | tf_op jit(solution)/shard_map/ppermute | solution.py:551
  4.7 15.5 %collective-permute-start.4 = (bf16[128,512]{1,0:T(8,128)(2,1)S(1)}, bf16[128,512]{1,0:T(8,128)(2,1)S(1)}, u32[]{:S(2)}, u32[]{:S(2)}) collective-permute-start(bf16[128,512]{1,0:T(8,128)(2,1)S(1)} %get-tuple-element.45), channel_id=1, source_target_pairs={{0,3},{1,2},{2,1},{3,0},{4,7},{5,6},{6,5},{7,4},{8,11},{9,10},{10,... | collective-permute-start | bytes 393224 | tf_op jit(solution)/shard_map/ppermute | solution.py:551
  7.2 13.2 %collective-permute-start.3 = (bf16[128,512]{1,0:T(8,128)(2,1)S(1)}, bf16[128,512]{1,0:T(8,128)(2,1)S(1)}, u32[]{:S(2)}, u32[]{:S(2)}) collective-permute-start(bf16[128,512]{1,0:T(8,128)(2,1)S(1)} %get-tuple-element.44), channel_id=1, source_target_pairs={{0,2},{1,3},{2,0},{3,1},{4,6},{5,7},{6,4},{7,5},{8,10},{9,11},{10,... | collective-permute-start | bytes 393224 | tf_op jit(solution)/shard_map/ppermute | solution.py:551
  8.3 12.1 %collective-permute-start.2 = (bf16[128,512]{1,0:T(8,128)(2,1)S(1)}, bf16[128,512]{1,0:T(8,128)(2,1)S(1)}, u32[]{:S(2)}, u32[]{:S(2)}) collective-permute-start(bf16[128,512]{1,0:T(8,128)(2,1)S(1)} %convert_bitcast_fusion), channel_id=1, source_target_pairs={{0,0},{1,1},{2,4},{3,5},{4,2},{5,3},{6,6},{7,7},{8,8},{9,9},{10,12... | collective-permute-start | bytes 393224 | tf_op jit(solution)/shard_map/ppermute | solution.py:551
  9.0 9.4 %collective-permute-start = (s32[1,2]{1,0:T(1,128)}, s32[1,2]{1,0:T(1,128)S(1)}, u32[]{:S(2)}, u32[]{:S(2)}) collective-permute-start(s32[1,2]{1,0:T(1,128)} %pos_ref.3), channel_id=1, source_target_pairs={{0,4},{1,5},{2,6},{3,7},{4,0},{5,1},{6,2},{7,3},{8,12},{9,13},{10,... | collective-permute-start | bytes 32 | tf_op jit(solution)/shard_map/ppermute | solution.py:551
  15.5 1.1 %copy-start.2 = (f32[2,160,640]{2,1,0:T(8,128)S(1)}, f32[2,160,640]{2,1,0:T(8,128)}, u32[]{:S(2)}) copy-start(f32[2,160,640]{2,1,0:T(8,128)} %transmission_ref.3) | copy-start | bytes 2457604
  16.7 0.7 copy-start.7
  17.3 24.0 %copy-start.6 = (bf16[2,8,128,512]{3,2,1,0:T(8,128)(2,1)S(1)}, bf16[2,8,128,512]{3,2,1,0:T(8,128)(2,1)}, u32[]{:S(2)}) copy-start(bf16[2,8,128,512]{3,2,1,0:T(8,128)(2,1)} %all_ref.1) | copy-start | bytes 6291460
  20.4 11.9 %collective-permute-start.9 = (bf16[384,512]{1,0:T(8,128)(2,1)S(1)}, bf16[384,512]{1,0:T(8,128)(2,1)S(1)}, u32[]{:S(2)}, u32[]{:S(2)}) collective-permute-start(bf16[384,512]{1,0:T(8,128)(2,1)S(1)} %pad_maximum_fusion.q0_ref), channel_id=1, source_target_pairs={{0,8},{1,9},{2,10},{3,11},{4,12},{5,13},{6,14},{7,15},{8,0},{9,1},... | collective-permute-start | bytes 1179656 | tf_op jit(solution)/shard_map/ppermute | solution.py:551
  22.0 12.0 %collective-permute-start.7 = (bf16[384,512]{1,0:T(8,128)(2,1)S(1)}, bf16[384,512]{1,0:T(8,128)(2,1)S(1)}, u32[]{:S(2)}, u32[]{:S(2)}) collective-permute-start(bf16[384,512]{1,0:T(8,128)(2,1)S(1)} %pad_maximum_fusion.q0_ref), channel_id=1, source_target_pairs={{0,16},{1,17},{2,18},{3,19},{4,20},{5,21},{6,22},{7,23},{8,24},{9,... | collective-permute-start | bytes 1179656 | tf_op jit(solution)/shard_map/ppermute | solution.py:551
  23.5 12.0 %collective-permute-start.5 = (bf16[2,160,512]{2,1,0:T(8,128)(2,1)S(1)}, bf16[2,160,512]{2,1,0:T(8,128)(2,1)S(1)}, u32[]{:S(2)}, u32[]{:S(2)}) collective-permute-start(bf16[2,160,512]{2,1,0:T(8,128)(2,1)S(1)} %shard_map.95), channel_id=1, source_target_pairs={{0,0},{1,1},{2,4},{3,5},{4,2},{5,3},{6,6},{7,7},{8,8},{9,9},{10,12... | collective-permute-start | bytes 983048 | tf_op jit(solution)/shard_map/ppermute | solution.py:551
  24.2 11.3 %collective-permute-start.6 = (bf16[2,160,512]{2,1,0:T(8,128)(2,1)S(1)}, bf16[2,160,512]{2,1,0:T(8,128)(2,1)S(1)}, u32[]{:S(2)}, u32[]{:S(2)}) collective-permute-start(bf16[2,160,512]{2,1,0:T(8,128)(2,1)S(1)} %shard_map.95), channel_id=1, source_target_pairs={{0,1},{1,0},{2,5},{3,4},{4,3},{5,2},{6,7},{7,6},{8,9},{9,8},{10,13... | collective-permute-start | bytes 983048 | tf_op jit(solution)/shard_map/ppermute | solution.py:551
  32.3 7.1 %collective-permute-start.10 = (bf16[192,512]{1,0:T(8,128)(2,1)S(1)}, bf16[192,512]{1,0:T(8,128)(2,1)S(1)}, u32[]{:S(2)}, u32[]{:S(2)}) collective-permute-start(bf16[192,512]{1,0:T(8,128)(2,1)S(1)} %slice.25), channel_id=1, source_target_pairs={{0,16},{1,17},{2,18},{3,19},{4,20},{5,21},{6,22},{7,23},{8,24},{9,... | collective-permute-start | bytes 589832 | tf_op jit(solution)/shard_map/ppermute | solution.py:551
  33.9 9.0 %copy-start.4 = (bf16[3,512,512]{2,1,0:T(8,128)(2,1)S(1)}, bf16[3,512,512]{2,1,0:T(8,128)(2,1)}, u32[]{:S(2)}) copy-start(bf16[3,512,512]{2,1,0:T(8,128)(2,1)} %constant.23.clone.right_ref) | copy-start | bytes 4718596
  33.9 6.9 %collective-permute-start.8 = (bf16[192,512]{1,0:T(8,128)(2,1)S(1)}, bf16[192,512]{1,0:T(8,128)(2,1)S(1)}, u32[]{:S(2)}, u32[]{:S(2)}) collective-permute-start(bf16[192,512]{1,0:T(8,128)(2,1)S(1)} %slice.24), channel_id=1, source_target_pairs={{0,8},{1,9},{2,10},{3,11},{4,12},{5,13},{6,14},{7,15},{8,0},{9,1},... | collective-permute-start | bytes 589832 | tf_op jit(solution)/shard_map/ppermute | solution.py:551
  40.8 1.9 %collective-permute-start.11 = (bf16[2,160,512]{2,1,0:T(8,128)(2,1)S(1)}, bf16[2,160,512]{2,1,0:T(8,128)(2,1)S(1)}, u32[]{:S(2)}, u32[]{:S(2)}) collective-permute-start(bf16[2,160,512]{2,1,0:T(8,128)(2,1)S(1)} %collective-permute-done.5.own_ref), channel_id=1, source_target_pairs={{0,4},{1,5},{2,6},{3,7},{4,0},{5,1},{6,2},{7,3},{8,12},{9,13},{10,... | collective-permute-start | bytes 983048 | tf_op jit(solution)/shard_map/ppermute | solution.py:551
  40.8 2.1 %collective-permute-start.12 = (bf16[2,160,512]{2,1,0:T(8,128)(2,1)S(1)}, bf16[2,160,512]{2,1,0:T(8,128)(2,1)S(1)}, u32[]{:S(2)}, u32[]{:S(2)}) collective-permute-start(bf16[2,160,512]{2,1,0:T(8,128)(2,1)S(1)} %collective-permute-done.6.side_ref), channel_id=1, source_target_pairs={{0,4},{1,5},{2,6},{3,7},{4,0},{5,1},{6,2},{7,3},{8,12},{9,13},{10,... | collective-permute-start | bytes 983048 | tf_op jit(solution)/shard_map/ppermute | solution.py:551
  48.1 1.8 %collective-permute-start.13 = (bf16[512,256]{1,0:T(8,128)(2,1)S(1)}, bf16[512,256]{1,0:T(8,128)(2,1)S(1)}, u32[]{:S(2)}, u32[]{:S(2)}) collective-permute-start(bf16[512,256]{1,0:T(8,128)(2,1)S(1)} %get-tuple-element.35), channel_id=1, source_target_pairs={{0,4},{1,5},{2,6},{3,7},{4,0},{5,1},{6,2},{7,3},{8,12},{9,13},{10,... | collective-permute-start | bytes 786440 | tf_op jit(solution)/shard_map/ppermute | solution.py:551
  50.0 10.2 %collective-permute-start.14 = (bf16[512,256]{1,0:T(8,128)(2,1)S(1)}, bf16[512,256]{1,0:T(8,128)(2,1)S(1)}, u32[]{:S(2)}, u32[]{:S(2)}) collective-permute-start(bf16[512,256]{1,0:T(8,128)(2,1)S(1)} %fusion.2), channel_id=1, source_target_pairs={{0,1},{1,0},{2,3},{3,2},{4,5},{5,4},{6,7},{7,6},{8,9},{9,8},{10,11... | collective-permute-start | bytes 786440 | tf_op jit(solution)/shard_map/ppermute | solution.py:551
  60.2 1.6 %collective-permute-start.15 = (bf16[512,256]{1,0:T(8,128)(2,1)S(1)}, bf16[512,256]{1,0:T(8,128)(2,1)S(1)}, u32[]{:S(2)}, u32[]{:S(2)}) collective-permute-start(bf16[512,256]{1,0:T(8,128)(2,1)S(1)} %get-tuple-element.42), channel_id=1, source_target_pairs={{0,4},{1,5},{2,6},{3,7},{4,0},{5,1},{6,2},{7,3},{8,12},{9,13},{10,... | collective-permute-start | bytes 786440 | tf_op jit(solution)/shard_map/ppermute | solution.py:551
  61.8 9.9 %copy-start = (f32[4,2,160,640]{3,2,1,0:T(8,128)S(1)}, f32[4,2,160,640]{3,2,1,0:T(8,128)}, u32[]{:S(2)}) copy-start(f32[4,2,160,640]{3,2,1,0:T(8,128)} %steps_ref.5) | copy-start | bytes 9830404
  61.8 9.9 %copy-start.1 = (f32[3,2,160,640]{3,2,1,0:T(8,128)S(1)}, f32[3,2,160,640]{3,2,1,0:T(8,128)}, u32[]{:S(2)}) copy-start(f32[3,2,160,640]{3,2,1,0:T(8,128)} %changes_ref.5) | copy-start | bytes 7372804
  66.7 2.2 %collective-permute-start.16 = (bf16[2,2,160,512]{3,2,1,0:T(8,128)(2,1)S(1)}, bf16[2,2,160,512]{3,2,1,0:T(8,128)(2,1)S(1)}, u32[]{:S(2)}, u32[]{:S(2)}) collective-permute-start(bf16[2,2,160,512]{3,2,1,0:T(8,128)(2,1)S(1)} %get-tuple-element.38), channel_id=1, source_target_pairs={{0,4},{1,5},{2,6},{3,7},{4,0},{5,1},{6,2},{7,3},{8,12},{9,13},{10,... | collective-permute-start | bytes 1966088 | tf_op jit(solution)/shard_map/ppermute | solution.py:551
  69.0 4.5 %collective-permute-start.17 = (bf16[2,160,512]{2,1,0:T(8,128)(2,1)S(1)}, bf16[2,160,512]{2,1,0:T(8,128)(2,1)S(1)}, u32[]{:S(2)}, u32[]{:S(2)}) collective-permute-start(bf16[2,160,512]{2,1,0:T(8,128)(2,1)S(1)} %get-tuple-element.46), channel_id=1, source_target_pairs={{0,0},{1,1},{2,4},{3,5},{4,2},{5,3},{6,6},{7,7},{8,8},{9,9},{10,12... | collective-permute-start | bytes 983048 | tf_op jit(solution)/shard_map/ppermute | solution.py:551
  69.9 10.3 %copy-start.3 = (f32[2,160,640]{2,1,0:T(8,128)S(1)}, f32[2,160,640]{2,1,0:T(8,128)}, u32[]{:S(2)}) copy-start(f32[2,160,640]{2,1,0:T(8,128)} %transmission_ref.3) | copy-start | bytes 2457604
  69.9 10.3 %copy-start.5 = (f32[2,160,640]{2,1,0:T(8,128)S(1)}, f32[2,160,640]{2,1,0:T(8,128)}, u32[]{:S(2)}) copy-start(f32[2,160,640]{2,1,0:T(8,128)} %old_ref.3) | copy-start | bytes 2457604
  69.9 10.3 %copy-start.8 = (s32[1,2]{1,0:T(1,128)S(1)}, s32[1,2]{1,0:T(1,128)}, u32[]{:S(2)}) copy-start(s32[1,2]{1,0:T(1,128)} %pos_ref.3) | copy-start | bytes 28
  69.9 10.2 %collective-permute-start.18 = (bf16[2,160,512]{2,1,0:T(8,128)(2,1)S(1)}, bf16[2,160,512]{2,1,0:T(8,128)(2,1)S(1)}, u32[]{:S(2)}, u32[]{:S(2)}) collective-permute-start(bf16[2,160,512]{2,1,0:T(8,128)(2,1)S(1)} %get-tuple-element.47), channel_id=1, source_target_pairs={{0,1},{1,0},{2,5},{3,4},{4,3},{5,2},{6,7},{7,6},{8,9},{9,8},{10,13... | collective-permute-start | bytes 983048 | tf_op jit(solution)/shard_map/ppermute | solution.py:551

commit v6 on v5

--- a/solution.py
+++ b/solution.py
@@ -576,22 +576,23 @@
     from_far, from_near = send(same_block, far), send(flip_block, near)
     from_cross = send(flip_block, cross)
     mate_positions = send(positions, mate)
-    piece = call(cut_kernel, size((2, piece_len, frame_len), BF), count=2, smem=(0,), limit=16)(
+    piece = call(cut_kernel, size((2, piece_len, frame_len), BF), count=2, smem=(0,), limit=12, cost=cost(0, 0))(
         positions, transmission
     )
-    measured_low, from_near = barrier((measured[0].astype(BF), from_near))
-    target = send(measured_low, home)
     q0 = jnp.concatenate([from_near, from_far, from_cross], axis=0)
     column = jnp.where(is_home, positions[0, 1], mate_positions[0, 1])
     place = jnp.stack([core, member, line, half, column]).astype(jnp.int32)
-    piece, place, target, q0 = barrier((piece, place, target, q0))
+    place, measured_low, q0 = barrier((place, measured[0].astype(BF), q0))
     q1, q2 = send(q0, along_x), send(q0, along_y)
+    target = send(measured_low, home)
     own = send(piece, home)
     side = send(piece, beside)
     cut = q0.shape[0] // 2
     q3a, q3b = send(q2[:cut], along_x), send(q1[cut:], along_y)
-    own, side, q3a, q3b = barrier((own, side, q3a, q3b))
-    mate_own, mate_side = send(own, mate), send(side, mate)
+    own, target = barrier((own, target))
+    mate_own = send(own, mate)
+    mate_own, side, q3a, q3b = barrier((mate_own, side, q3a, q3b))
+    mate_side = send(side, mate)
     whole_probe = call(
         probe_kernel,
         size((2, 2, frame_len, frame_len), BF),
@@ -599,7 +600,7 @@
         count=7,
         smem=(0,),
         far=(1,),
-        limit=16,
+        limit=12,
     )(place, probe, q0, q1, q2, q3a, q3b)
 
     right = jnp.asarray(propagator(frame_len))
@@ -618,7 +619,7 @@
         ],
         count=8,
         smem=(0,),
-        limit=24,
+        limit=20,
         cost=cost(3 * flops // 4, 16 * MIB),
     )(place, own, side, mate_own, mate_side, whole_probe, target, right)
     met = send(sent, mate)
@@ -627,7 +628,7 @@
         (half_field, size((frame_len, half_len), F32)),
         count=4,
         smem=(0,),
-        limit=24,
+        limit=20,
         cost=cost(flops // 4, 4 * MIB),
     )(place, turned, target, right)
 
@@ -638,7 +639,7 @@
         own_kernel,
         size((3, double, half_len), BF),
         count=3,
-        limit=24,
+        limit=20,
         cost=cost(flops // 4, 4 * MIB),
     )(own_far, misfit, right)
 
@@ -653,7 +654,7 @@
         ],
         count=6,
         smem=(0,),
-        limit=24,
+        limit=20,
         cost=cost(3 * flops // 4, 12 * MIB),
     )(place, mates_far, whole_probe, mates_misfit, own_left, right)
     met = send(sent, mate)
@@ -668,7 +669,7 @@
         size((1, LANES), F32),
         [pltpu.VMEM((OLD_PAIRS, 8, LANES), F32)],
         count=2,
-        limit=16,
+        limit=12,
         cost=cost(22 * moved, 7 * moved),
     )(past_steps, past_changes)
     gradient, row = call(
@@ -677,7 +678,7 @@
         [pltpu.VMEM((len(PAIRS) - OLD_PAIRS, 8, LANES), F32)],
         count=7,
         smem=(0,),
-        limit=16,
+        limit=12,
         cost=cost(16 * moved, 10 * moved),
     )(positions, data, transmission, old_gradient, past_steps, past_changes, old_row)
     all_rows = lax.all_to_all(
@@ -688,7 +689,7 @@
         (size(transmission.shape, F32), size(transmission.shape, F32)),
         [pltpu.VMEM(transmission.shape, F32), pltpu.SemaphoreType.DMA((3,))],
         count=6,
-        limit=16,
+        limit=12,
         cost=cost(10 * moved, 11 * moved),
         out_space=pl.ANY,
     )(all_rows, transmission, gradient, old_gradient, past_steps, past_changes)

time: 102 us -> 102 us (level)
  starting transfers between devices: 28.2 us -> 23.4 us
  blocking collectives: 17.4 us -> 21.1 us
  waiting for transfers between devices: 26.8 us -> 28.6 us
    ppermute x19, starting transfers between devices: 28.2 us -> 23.4 us  [send(): return lax.ppermute(value, AXES, pairs)]
    all_to_all x1, blocking collectives: 17.4 us -> 21.1 us  [fast(): lax.all_to_all(row.reshape(devices, 1, LANES), AXES, split_axis=0, concat...]
    ppermute x19, waiting for transfers between devices: 26.8 us -> 28.6 us  [send(): return lax.ppermute(value, AXES, pairs)]
  transfers between devices with their start and end apart: 19 -> 19, of which waited for: 9 -> 10; matrix products, arithmetic and copies ran while one was open for 3% -> 3% of each run, Pallas kernels for 7% -> 7%
where the time goes in v6:
time: 102 us
  waiting for transfers between devices  28.6 us (28%)
  starting transfers between devices  23.4 us (23%)
  blocking collectives  21.1 us (21%)
  Pallas kernels  20 us (20%)
  local copies, waits for them, and re-layouts  4.82 us (5%)
  between operations  2.28 us (2%)
  other arithmetic  1.39 us (1%)
    ppermute x19, waiting for transfers between devices, send(): return lax.ppermute(value, AXES, pairs)  28.6 us
    ppermute x19, starting transfers between devices, send(): return lax.ppermute(value, AXES, pairs)  23.4 us
    all_to_all x1, blocking collectives, fast(): lax.all_to_all(row.reshape(devices, 1, LANES), AXES, split_axis=0, concat...  21.1 us
    pallas_call x1, Pallas kernels, fast(): call(forward_kernel, (size((2, 2, 3, frame_len, half_len), BF), half_fiel...  5.05 us
    pallas_call x1, Pallas kernels, fast(): call(backward_kernel, (size((2, 2, piece_len, frame_len), BF), piece_shap...  4.67 us
    pallas_call x1, Pallas kernels, fast(): call(gradient_kernel, (size(transmission.shape, F32), size((devices, LANE...  2.21 us
  transfers between devices with their start and end apart: 19, of which 10 were waited for; matrix products, arithmetic and copies ran while one was open for 3% of the time, Pallas kernels for 7%

profile of v6, /device:TPU:0, one launch (start us, length us, event | category | flops | bytes accessed | tf_op | source)
XLA Modules:
  0.0 101.6 jit_solution(14631108083105285959)
XLA Ops:
  0.6 1.0 dynamic-slice_bitcast_fusion
  1.6 3.1 %collective-permute-start.1 = (bf16[128,512]{1,0:T(8,128)(2,1)S(1)}, bf16[128,512]{1,0:T(8,128)(2,1)S(1)}, u32[]{:S(2)}, u32[]{:S(2)}) collective-permute-start(bf16[128,512]{1,0:T(8,128)(2,1)S(1)} %get-tuple-element.43), channel_id=1, source_target_pairs={{0,1},{1,0},{2,3},{3,2},{4,5},{5,4},{6,7},{7,6},{8,9},{9,8},{10,11... | collective-permute-start | bytes 393224 | tf_op jit(solution)/shard_map/ppermute | solution.py:551
  4.7 2.5 %collective-permute-start.3 = (bf16[128,512]{1,0:T(8,128)(2,1)S(1)}, bf16[128,512]{1,0:T(8,128)(2,1)S(1)}, u32[]{:S(2)}, u32[]{:S(2)}) collective-permute-start(bf16[128,512]{1,0:T(8,128)(2,1)S(1)} %get-tuple-element.43), channel_id=1, source_target_pairs={{0,3},{1,2},{2,1},{3,0},{4,7},{5,6},{6,5},{7,4},{8,11},{9,10},{10,... | collective-permute-start | bytes 393224 | tf_op jit(solution)/shard_map/ppermute | solution.py:551
  7.2 0.1 collective-permute-start.2
  7.3 0.0 collective-permute-start
  7.3 1.1 %copy-done.2 = f32[2,160,640]{2,1,0:T(8,128)S(1)} copy-done((f32[2,160,640]{2,1,0:T(8,128)S(1)}, f32[2,160,640]{2,1,0:T(8,128)}, u32[]{:S(2)}) %copy-start.2) | copy-done | bytes 819224
  8.5 0.7 copy-done.7
  9.1 1.0 shard_map.95
  10.1 0.7 collective-permute-start.4
  10.8 1.3 %slice.18 = s32[1,1]{1,0:T(1,128)} slice(s32[1,2]{1,0:T(1,128)} %pos_ref.3), slice={[0:1], [1:2]} | slice | bytes 8 | tf_op jit(solution)/shard_map/slice | solution.py:583
  12.1 1.0 convert_bitcast_fusion
  13.1 0.0 collective-permute-done
  13.1 0.6 slice.19
  14.9 0.1 stack.23.place_ref
  15.0 0.0 collective-permute-done.1
  15.0 0.0 collective-permute-done.3
  15.0 7.4 %collective-permute-done.2 = bf16[128,512]{1,0:T(8,128)(2,1)S(1)} collective-permute-done((bf16[128,512]{1,0:T(8,128)(2,1)S(1)}, bf16[128,512]{1,0:T(8,128)(2,1)S(1)}, u32[]{:S(2)}, u32[]{:S(2)}) %collective-permute-start.2) | collective-permute-done | bytes 131104 | tf_op jit(solution)/shard_map/ppermute | solution.py:551
  22.5 1.6 %collective-permute-start.10 = (bf16[384,512]{1,0:T(8,128)(2,1)S(1)}, bf16[384,512]{1,0:T(8,128)(2,1)S(1)}, u32[]{:S(2)}, u32[]{:S(2)}) collective-permute-start(bf16[384,512]{1,0:T(8,128)(2,1)S(1)} %pad_maximum_fusion.q0_ref), channel_id=1, source_target_pairs={{0,8},{1,9},{2,10},{3,11},{4,12},{5,13},{6,14},{7,15},{8,0},{9,1},... | collective-permute-start | bytes 1179656 | tf_op jit(solution)/shard_map/ppermute | solution.py:551
  24.1 1.5 %collective-permute-start.8 = (bf16[384,512]{1,0:T(8,128)(2,1)S(1)}, bf16[384,512]{1,0:T(8,128)(2,1)S(1)}, u32[]{:S(2)}, u32[]{:S(2)}) collective-permute-start(bf16[384,512]{1,0:T(8,128)(2,1)S(1)} %pad_maximum_fusion.q0_ref), channel_id=1, source_target_pairs={{0,16},{1,17},{2,18},{3,19},{4,20},{5,21},{6,22},{7,23},{8,24},{9,... | collective-permute-start | bytes 1179656 | tf_op jit(solution)/shard_map/ppermute | solution.py:551
  25.6 0.7 collective-permute-start.5
  26.2 1.0 %collective-permute-start.7 = (bf16[2,160,512]{2,1,0:T(8,128)(2,1)S(1)}, bf16[2,160,512]{2,1,0:T(8,128)(2,1)S(1)}, u32[]{:S(2)}, u32[]{:S(2)}) collective-permute-start(bf16[2,160,512]{2,1,0:T(8,128)(2,1)S(1)} %shard_map.95), channel_id=1, source_target_pairs={{0,1},{1,0},{2,5},{3,4},{4,3},{5,2},{6,7},{7,6},{8,9},{9,8},{10,13... | collective-permute-start | bytes 983048 | tf_op jit(solution)/shard_map/ppermute | solution.py:551
  27.3 0.0 collective-permute-done.5.measured_ref
  27.3 0.0 collective-permute-done.4.own_ref
  27.3 4.2 %collective-permute-start.6 = (bf16[2,160,512]{2,1,0:T(8,128)(2,1)S(1)}, bf16[2,160,512]{2,1,0:T(8,128)(2,1)S(1)}, u32[]{:S(2)}, u32[]{:S(2)}) collective-permute-start(bf16[2,160,512]{2,1,0:T(8,128)(2,1)S(1)} %collective-permute-done.4.own_ref), channel_id=1, source_target_pairs={{0,4},{1,5},{2,6},{3,7},{4,0},{5,1},{6,2},{7,3},{8,12},{9,13},{10,... | collective-permute-start | bytes 983048 | tf_op jit(solution)/shard_map/ppermute | solution.py:551
  31.5 1.3 %collective-permute-done.10.q1_ref = bf16[384,512]{1,0:T(8,128)(2,1)S(1)} collective-permute-done((bf16[384,512]{1,0:T(8,128)(2,1)S(1)}, bf16[384,512]{1,0:T(8,128)(2,1)S(1)}, u32[]{:S(2)}, u32[]{:S(2)}) %collective-permute-start.10) | collective-permute-done | bytes 393248 | tf_op jit(solution)/shard_map/ppermute | solution.py:551
  32.8 1.6 %collective-permute-start.11 = (bf16[192,512]{1,0:T(8,128)(2,1)S(1)}, bf16[192,512]{1,0:T(8,128)(2,1)S(1)}, u32[]{:S(2)}, u32[]{:S(2)}) collective-permute-start(bf16[192,512]{1,0:T(8,128)(2,1)S(1)} %slice.25), channel_id=1, source_target_pairs={{0,16},{1,17},{2,18},{3,19},{4,20},{5,21},{6,22},{7,23},{8,24},{9,... | collective-permute-start | bytes 589832 | tf_op jit(solution)/shard_map/ppermute | solution.py:551
  34.4 0.0 collective-permute-done.8.q2_ref
  34.4 0.0 copy-start.4
  34.4 1.6 %collective-permute-start.9 = (bf16[192,512]{1,0:T(8,128)(2,1)S(1)}, bf16[192,512]{1,0:T(8,128)(2,1)S(1)}, u32[]{:S(2)}, u32[]{:S(2)}) collective-permute-start(bf16[192,512]{1,0:T(8,128)(2,1)S(1)} %slice.24), channel_id=1, source_target_pairs={{0,8},{1,9},{2,10},{3,11},{4,12},{5,13},{6,14},{7,15},{8,0},{9,1},... | collective-permute-start | bytes 589832 | tf_op jit(solution)/shard_map/ppermute | solution.py:551
  36.0 2.3 %collective-permute-done.7.side_ref = bf16[2,160,512]{2,1,0:T(8,128)(2,1)S(1)} collective-permute-done((bf16[2,160,512]{2,1,0:T(8,128)(2,1)S(1)}, bf16[2,160,512]{2,1,0:T(8,128)(2,1)S(1)}, u32[]{:S(2)}, u32[]{:S(2)}) %collective-permute-start.7) | collective-permute-done | bytes 327712 | tf_op jit(solution)/shard_map/ppermute | solution.py:551
  38.3 0.0 collective-permute-done.6.mate_own_ref
  38.3 0.2 collective-permute-done.11.q3b_ref
  38.6 1.6 %collective-permute-done.9.q3a_ref = bf16[192,512]{1,0:T(8,128)(2,1)S(1)} collective-permute-done((bf16[192,512]{1,0:T(8,128)(2,1)S(1)}, bf16[192,512]{1,0:T(8,128)(2,1)S(1)}, u32[]{:S(2)}, u32[]{:S(2)}) %collective-permute-start.9) | collective-permute-done | bytes 196640 | tf_op jit(solution)/shard_map/ppermute | solution.py:551
  40.2 0.0 collective-permute-start.12
  40.2 0.0 copy-done.6
  40.2 1.4 %shard_map.96.probe_ref = bf16[2,2,512,512]{3,2,1,0:T(8,128)(2,1)S(1)} custom-call(s32[5]{0:T(128)S(1)} %stack.23.place_ref, bf16[2,8,128,512]{3,2,1,0:T(8,128)(2,1)S(1)} %copy-done.6, bf16[384,512]{1,0:T(8,128)(2,1)S(1)} %pad_maximum_fusion.q0_ref, bf16[384,512]{1,0:T(8,128)(2,1)S(1)} %collective-permute-done.10.q1_ref, ...), custom_call_target="tpu_custom_call" | custom-call | tf_op jit(solution)/shard_map/pallas_call | solution.py:596
  41.6 0.2 collective-permute-done.12.mate_side_ref
  41.8 5.0 %shard_map.97 = (bf16[2,2,3,512,256]{4,3,2,1,0:T(8,128)(2,1)S(1)}, bf16[2,2,512,256]{3,2,1,0:T(8,128)(2,1)S(1)}, bf16[512,256]{1,0:T(8,128)(2,1)S(1)}) custom-call(s32[5]{0:T(128)S(1)} %stack.23.place_ref, bf16[2,160,512]{2,1,0:T(8,128)(2,1)S(1)} %collective-permute-done.4.own_ref, bf16[2,160,512]{2,1,0:T(8,128)(2,1)S(1)} %collective-permute-done.7.side_ref, ...), custom_call_target="tpu_custom_call" | custom-call | flops 3221225472 | bytes 16777216 | tf_op jit(solution)/shard_map/pallas_call | solution.py:611
  46.9 0.3 collective-permute-start.13
  47.2 1.6 %shard_map.98 = (bf16[2,2,512,256]{3,2,1,0:T(8,128)(2,1)S(1)}, f32[512,256]{1,0:T(8,128)S(1)}) custom-call(s32[5]{0:T(128)S(1)} %stack.23.place_ref, bf16[2,2,3,512,256]{4,3,2,1,0:T(8,128)(2,1)S(1)} %get-tuple-element.31.turned_ref, bf16[128,512]{1,0:T(8,128)(2,1)S(1)} %collective-permute-done.5.measured_ref, bf16[3,512,512]{2,1,0:T(8,128)(2,1)S(1)} %copy-done.4), custom_call_target="tpu_custom_call" | custom-call | flops 1073741824 | bytes 4194304 | tf_op jit(solution)/shard_map/pallas_call | solution.py:626
  48.8 0.0 collective-permute-done.13
  48.8 0.1 fusion.2
  48.9 1.7 %collective-permute-start.14 = (bf16[512,256]{1,0:T(8,128)(2,1)S(1)}, bf16[512,256]{1,0:T(8,128)(2,1)S(1)}, u32[]{:S(2)}, u32[]{:S(2)}) collective-permute-start(bf16[512,256]{1,0:T(8,128)(2,1)S(1)} %fusion.2), channel_id=1, source_target_pairs={{0,1},{1,0},{2,3},{3,2},{4,5},{5,4},{6,7},{7,6},{8,9},{9,8},{10,11... | collective-permute-start | bytes 786440 | tf_op jit(solution)/shard_map/ppermute | solution.py:551
  50.6 6.8 %collective-permute-done.14 = bf16[512,256]{1,0:T(8,128)(2,1)S(1)} collective-permute-done((bf16[512,256]{1,0:T(8,128)(2,1)S(1)}, bf16[512,256]{1,0:T(8,128)(2,1)S(1)}, u32[]{:S(2)}, u32[]{:S(2)}) %collective-permute-start.14) | collective-permute-done | bytes 262176 | tf_op jit(solution)/shard_map/ppermute | solution.py:551
  57.4 0.1 fusion.3
  57.5 0.1 collective-permute-start.15
  57.5 1.1 %shard_map.99.own_ref = bf16[3,1024,256]{2,1,0:T(8,128)(2,1)S(1)} custom-call(bf16[2,2,512,256]{3,2,1,0:T(8,128)(2,1)S(1)} %get-tuple-element.34.far_ref, f32[512,256]{1,0:T(8,128)S(1)} %get-tuple-element.41.mine_ref, bf16[3,512,512]{2,1,0:T(8,128)(2,1)S(1)} %copy-done.4), custom_call_target="tpu_custom_call" | custom-call | flops 1073741824 | bytes 4194304 | tf_op jit(solution)/shard_map/pallas_call | solution.py:638
  58.6 0.4 collective-permute-done.15.mates_ref
  59.1 4.7 %shard_map.100 = (bf16[2,2,160,512]{3,2,1,0:T(8,128)(2,1)S(1)}, bf16[2,160,512]{2,1,0:T(8,128)(2,1)S(1)}, bf16[2,160,512]{2,1,0:T(8,128)(2,1)S(1)}) custom-call(s32[5]{0:T(128)S(1)} %stack.23.place_ref, bf16[2,2,512,256]{3,2,1,0:T(8,128)(2,1)S(1)} %get-tuple-element.30.far_ref, bf16[2,2,512,512]{3,2,1,0:T(8,128)(2,1)S(1)} %shard_map.96.probe_ref, ...), custom_call_target="tpu_custom_call" | custom-call | flops 3221225472 | bytes 12582912 | tf_op jit(solution)/shard_map/pallas_call | solution.py:647
  63.8 0.2 collective-permute-start.16
  64.0 2.0 %collective-permute-done.16 = bf16[2,2,160,512]{3,2,1,0:T(8,128)(2,1)S(1)} collective-permute-done((bf16[2,2,160,512]{3,2,1,0:T(8,128)(2,1)S(1)}, bf16[2,2,160,512]{3,2,1,0:T(8,128)(2,1)S(1)}, u32[]{:S(2)}, u32[]{:S(2)}) %collective-permute-start.16) | collective-permute-done | bytes 655392 | tf_op jit(solution)/shard_map/ppermute | solution.py:551
  65.9 0.2 fusion.1
  66.1 0.9 collective-permute-start.17
  67.0 0.0 copy-start.3
  67.0 0.0 copy-start.5
  67.0 0.0 copy-start.8
  67.0 1.7 %collective-permute-start.18 = (bf16[2,160,512]{2,1,0:T(8,128)(2,1)S(1)}, bf16[2,160,512]{2,1,0:T(8,128)(2,1)S(1)}, u32[]{:S(2)}, u32[]{:S(2)}) collective-permute-start(bf16[2,160,512]{2,1,0:T(8,128)(2,1)S(1)} %get-tuple-element.45), channel_id=1, source_target_pairs={{0,1},{1,0},{2,5},{3,4},{4,3},{5,2},{6,7},{7,6},{8,9},{9,8},{10,13... | collective-permute-start | bytes 983048 | tf_op jit(solution)/shard_map/ppermute | solution.py:551
  68.7 1.6 %shard_map.101.row_ref = f32[1,128]{1,0:T(1,128)S(1)} custom-call(f32[4,2,160,640]{3,2,1,0:T(8,128)S(1)} %copy-done, f32[3,2,160,640]{3,2,1,0:T(8,128)S(1)} %copy-done.1), custom_call_target="tpu_custom_call" | custom-call | flops 18022400 | bytes 5734400 | tf_op jit(solution)/shard_map/pallas_call | solution.py:667
  70.3 0.0 collective-permute-done.17
  70.3 6.3 %collective-permute-done.18 = bf16[2,160,512]{2,1,0:T(8,128)(2,1)S(1)} collective-permute-done((bf16[2,160,512]{2,1,0:T(8,128)(2,1)S(1)}, bf16[2,160,512]{2,1,0:T(8,128)(2,1)S(1)}, u32[]{:S(2)}, u32[]{:S(2)}) %collective-permute-start.18) | collective-permute-done | bytes 327712 | tf_op jit(solution)/shard_map/ppermute | solution.py:551
  76.6 0.1 add_convert_fusion.data_ref
  76.7 2.2 %shard_map.102 = (f32[2,160,640]{2,1,0:T(8,128)S(1)}, f32[32,128]{1,0:T(8,128)S(1)}) custom-call(s32[1,2]{1,0:T(1,128)S(1)} %copy-done.8, bf16[2,160,512]{2,1,0:T(8,128)(2,1)S(1)} %add_convert_fusion.data_ref, f32[2,160,640]{2,1,0:T(8,128)S(1)} %copy-done.3, f32[2,160,640]{2,1,0:T(8,128)S(1)} %copy-done.5, f32[4,2,160,640]{3,2,1,0:T(8,128)S(1)} %copy-done, ...), custom_call_target="tpu_custom_call" | custom-call | flops 13107200 | bytes 8192000 | tf_op jit(solution)/shard_map/pallas_call | solution.py:675
  78.9 21.1 %all_to_all.5 = f32[32,1,128]{2,1,0:T(1,128)S(1)} all-to-all(f32[32,1,128]{2,1,0:T(1,128)S(1)} %bitcast.28), channel_id=1, replica_groups=mesh['region'=8,'grp'=4] {'region','grp'}, dimensions={0} | all-to-all | bytes 32768 | tf_op jit(solution)/shard_map/all_to_all | solution.py:684
  100.0 1.4 %shard_map.103 = (f32[2,160,640]{2,1,0:T(8,128)}, f32[2,160,640]{2,1,0:T(8,128)}) custom-call(f32[32,128]{1,0:T(8,128)S(1)} %bitcast.27, f32[2,160,640]{2,1,0:T(8,128)S(1)} %copy-done.3, f32[2,160,640]{2,1,0:T(8,128)S(1)} %get-tuple-element.39.gradient_ref, f32[2,160,640]{2,1,0:T(8,128)S(1)} %copy-done.5, f32[4,2,160,640]{3,2,1,0:T(8,128)S(1)} %copy-done, ...), custom_call_target="tpu_custom_call" | custom-call | flops 8192000 | bytes 9011200 | tf_op jit(solution)/shard_map/pallas_call | solution.py:687
  (14 shorter events, 0.1 us)
Async XLA Ops:
  1.6 13.4 %collective-permute-start.1 = (bf16[128,512]{1,0:T(8,128)(2,1)S(1)}, bf16[128,512]{1,0:T(8,128)(2,1)S(1)}, u32[]{:S(2)}, u32[]{:S(2)}) collective-permute-start(bf16[128,512]{1,0:T(8,128)(2,1)S(1)} %get-tuple-element.43), channel_id=1, source_target_pairs={{0,1},{1,0},{2,3},{3,2},{4,5},{5,4},{6,7},{7,6},{8,9},{9,8},{10,11... | collective-permute-start | bytes 393224 | tf_op jit(solution)/shard_map/ppermute | solution.py:551
  4.7 10.3 %collective-permute-start.3 = (bf16[128,512]{1,0:T(8,128)(2,1)S(1)}, bf16[128,512]{1,0:T(8,128)(2,1)S(1)}, u32[]{:S(2)}, u32[]{:S(2)}) collective-permute-start(bf16[128,512]{1,0:T(8,128)(2,1)S(1)} %get-tuple-element.43), channel_id=1, source_target_pairs={{0,3},{1,2},{2,1},{3,0},{4,7},{5,6},{6,5},{7,4},{8,11},{9,10},{10,... | collective-permute-start | bytes 393224 | tf_op jit(solution)/shard_map/ppermute | solution.py:551
  7.2 15.3 %collective-permute-start.2 = (bf16[128,512]{1,0:T(8,128)(2,1)S(1)}, bf16[128,512]{1,0:T(8,128)(2,1)S(1)}, u32[]{:S(2)}, u32[]{:S(2)}) collective-permute-start(bf16[128,512]{1,0:T(8,128)(2,1)S(1)} %get-tuple-element.42), channel_id=1, source_target_pairs={{0,2},{1,3},{2,0},{3,1},{4,6},{5,7},{6,4},{7,5},{8,10},{9,11},{10,... | collective-permute-start | bytes 393224 | tf_op jit(solution)/shard_map/ppermute | solution.py:551
  7.3 5.8 %collective-permute-start = (s32[1,2]{1,0:T(1,128)}, s32[1,2]{1,0:T(1,128)S(1)}, u32[]{:S(2)}, u32[]{:S(2)}) collective-permute-start(s32[1,2]{1,0:T(1,128)} %pos_ref.3), channel_id=1, source_target_pairs={{0,4},{1,5},{2,6},{3,7},{4,0},{5,1},{6,2},{7,3},{8,12},{9,13},{10,... | collective-permute-start | bytes 32 | tf_op jit(solution)/shard_map/ppermute | solution.py:551
  7.3 1.1 %copy-start.2 = (f32[2,160,640]{2,1,0:T(8,128)S(1)}, f32[2,160,640]{2,1,0:T(8,128)}, u32[]{:S(2)}) copy-start(f32[2,160,640]{2,1,0:T(8,128)} %transmission_ref.3) | copy-start | bytes 2457604
  8.5 0.7 copy-start.7
  9.1 31.0 %copy-start.6 = (bf16[2,8,128,512]{3,2,1,0:T(8,128)(2,1)S(1)}, bf16[2,8,128,512]{3,2,1,0:T(8,128)(2,1)}, u32[]{:S(2)}) copy-start(bf16[2,8,128,512]{3,2,1,0:T(8,128)(2,1)} %all_ref.1) | copy-start | bytes 6291460
  10.1 17.1 %collective-permute-start.4 = (bf16[2,160,512]{2,1,0:T(8,128)(2,1)S(1)}, bf16[2,160,512]{2,1,0:T(8,128)(2,1)S(1)}, u32[]{:S(2)}, u32[]{:S(2)}) collective-permute-start(bf16[2,160,512]{2,1,0:T(8,128)(2,1)S(1)} %shard_map.95), channel_id=1, source_target_pairs={{0,0},{1,1},{2,4},{3,5},{4,2},{5,3},{6,6},{7,7},{8,8},{9,9},{10,12... | collective-permute-start | bytes 983048 | tf_op jit(solution)/shard_map/ppermute | solution.py:551
  22.5 10.3 %collective-permute-start.10 = (bf16[384,512]{1,0:T(8,128)(2,1)S(1)}, bf16[384,512]{1,0:T(8,128)(2,1)S(1)}, u32[]{:S(2)}, u32[]{:S(2)}) collective-permute-start(bf16[384,512]{1,0:T(8,128)(2,1)S(1)} %pad_maximum_fusion.q0_ref), channel_id=1, source_target_pairs={{0,8},{1,9},{2,10},{3,11},{4,12},{5,13},{6,14},{7,15},{8,0},{9,1},... | collective-permute-start | bytes 1179656 | tf_op jit(solution)/shard_map/ppermute | solution.py:551
  24.1 10.3 %collective-permute-start.8 = (bf16[384,512]{1,0:T(8,128)(2,1)S(1)}, bf16[384,512]{1,0:T(8,128)(2,1)S(1)}, u32[]{:S(2)}, u32[]{:S(2)}) collective-permute-start(bf16[384,512]{1,0:T(8,128)(2,1)S(1)} %pad_maximum_fusion.q0_ref), channel_id=1, source_target_pairs={{0,16},{1,17},{2,18},{3,19},{4,20},{5,21},{6,22},{7,23},{8,24},{9,... | collective-permute-start | bytes 1179656 | tf_op jit(solution)/shard_map/ppermute | solution.py:551
  25.6 1.7 %collective-permute-start.5 = (bf16[128,512]{1,0:T(8,128)(2,1)S(1)}, bf16[128,512]{1,0:T(8,128)(2,1)S(1)}, u32[]{:S(2)}, u32[]{:S(2)}) collective-permute-start(bf16[128,512]{1,0:T(8,128)(2,1)S(1)} %convert_bitcast_fusion), channel_id=1, source_target_pairs={{0,0},{1,1},{2,4},{3,5},{4,2},{5,3},{6,6},{7,7},{8,8},{9,9},{10,12... | collective-permute-start | bytes 393224 | tf_op jit(solution)/shard_map/ppermute | solution.py:551
  26.2 12.1 %collective-permute-start.7 = (bf16[2,160,512]{2,1,0:T(8,128)(2,1)S(1)}, bf16[2,160,512]{2,1,0:T(8,128)(2,1)S(1)}, u32[]{:S(2)}, u32[]{:S(2)}) collective-permute-start(bf16[2,160,512]{2,1,0:T(8,128)(2,1)S(1)} %shard_map.95), channel_id=1, source_target_pairs={{0,1},{1,0},{2,5},{3,4},{4,3},{5,2},{6,7},{7,6},{8,9},{9,8},{10,13... | collective-permute-start | bytes 983048 | tf_op jit(solution)/shard_map/ppermute | solution.py:551
  27.3 11.0 %collective-permute-start.6 = (bf16[2,160,512]{2,1,0:T(8,128)(2,1)S(1)}, bf16[2,160,512]{2,1,0:T(8,128)(2,1)S(1)}, u32[]{:S(2)}, u32[]{:S(2)}) collective-permute-start(bf16[2,160,512]{2,1,0:T(8,128)(2,1)S(1)} %collective-permute-done.4.own_ref), channel_id=1, source_target_pairs={{0,4},{1,5},{2,6},{3,7},{4,0},{5,1},{6,2},{7,3},{8,12},{9,13},{10,... | collective-permute-start | bytes 983048 | tf_op jit(solution)/shard_map/ppermute | solution.py:551
  32.8 5.7 %collective-permute-start.11 = (bf16[192,512]{1,0:T(8,128)(2,1)S(1)}, bf16[192,512]{1,0:T(8,128)(2,1)S(1)}, u32[]{:S(2)}, u32[]{:S(2)}) collective-permute-start(bf16[192,512]{1,0:T(8,128)(2,1)S(1)} %slice.25), channel_id=1, source_target_pairs={{0,16},{1,17},{2,18},{3,19},{4,20},{5,21},{6,22},{7,23},{8,24},{9,... | collective-permute-start | bytes 589832 | tf_op jit(solution)/shard_map/ppermute | solution.py:551
  34.4 7.4 %copy-start.4 = (bf16[3,512,512]{2,1,0:T(8,128)(2,1)S(1)}, bf16[3,512,512]{2,1,0:T(8,128)(2,1)}, u32[]{:S(2)}) copy-start(bf16[3,512,512]{2,1,0:T(8,128)(2,1)} %constant.23.clone.right_ref) | copy-start | bytes 4718596
  34.4 5.7 %collective-permute-start.9 = (bf16[192,512]{1,0:T(8,128)(2,1)S(1)}, bf16[192,512]{1,0:T(8,128)(2,1)S(1)}, u32[]{:S(2)}, u32[]{:S(2)}) collective-permute-start(bf16[192,512]{1,0:T(8,128)(2,1)S(1)} %slice.24), channel_id=1, source_target_pairs={{0,8},{1,9},{2,10},{3,11},{4,12},{5,13},{6,14},{7,15},{8,0},{9,1},... | collective-permute-start | bytes 589832 | tf_op jit(solution)/shard_map/ppermute | solution.py:551
  40.2 1.6 %collective-permute-start.12 = (bf16[2,160,512]{2,1,0:T(8,128)(2,1)S(1)}, bf16[2,160,512]{2,1,0:T(8,128)(2,1)S(1)}, u32[]{:S(2)}, u32[]{:S(2)}) collective-permute-start(bf16[2,160,512]{2,1,0:T(8,128)(2,1)S(1)} %collective-permute-done.7.side_ref), channel_id=1, source_target_pairs={{0,4},{1,5},{2,6},{3,7},{4,0},{5,1},{6,2},{7,3},{8,12},{9,13},{10,... | collective-permute-start | bytes 983048 | tf_op jit(solution)/shard_map/ppermute | solution.py:551
  46.9 1.9 %collective-permute-start.13 = (bf16[512,256]{1,0:T(8,128)(2,1)S(1)}, bf16[512,256]{1,0:T(8,128)(2,1)S(1)}, u32[]{:S(2)}, u32[]{:S(2)}) collective-permute-start(bf16[512,256]{1,0:T(8,128)(2,1)S(1)} %get-tuple-element.33), channel_id=1, source_target_pairs={{0,4},{1,5},{2,6},{3,7},{4,0},{5,1},{6,2},{7,3},{8,12},{9,13},{10,... | collective-permute-start | bytes 786440 | tf_op jit(solution)/shard_map/ppermute | solution.py:551
  48.9 8.5 %collective-permute-start.14 = (bf16[512,256]{1,0:T(8,128)(2,1)S(1)}, bf16[512,256]{1,0:T(8,128)(2,1)S(1)}, u32[]{:S(2)}, u32[]{:S(2)}) collective-permute-start(bf16[512,256]{1,0:T(8,128)(2,1)S(1)} %fusion.2), channel_id=1, source_target_pairs={{0,1},{1,0},{2,3},{3,2},{4,5},{5,4},{6,7},{7,6},{8,9},{9,8},{10,11... | collective-permute-start | bytes 786440 | tf_op jit(solution)/shard_map/ppermute | solution.py:551
  57.5 1.6 %collective-permute-start.15 = (bf16[512,256]{1,0:T(8,128)(2,1)S(1)}, bf16[512,256]{1,0:T(8,128)(2,1)S(1)}, u32[]{:S(2)}, u32[]{:S(2)}) collective-permute-start(bf16[512,256]{1,0:T(8,128)(2,1)S(1)} %get-tuple-element.40), channel_id=1, source_target_pairs={{0,4},{1,5},{2,6},{3,7},{4,0},{5,1},{6,2},{7,3},{8,12},{9,13},{10,... | collective-permute-start | bytes 786440 | tf_op jit(solution)/shard_map/ppermute | solution.py:551
  59.1 9.7 %copy-start = (f32[4,2,160,640]{3,2,1,0:T(8,128)S(1)}, f32[4,2,160,640]{3,2,1,0:T(8,128)}, u32[]{:S(2)}) copy-start(f32[4,2,160,640]{3,2,1,0:T(8,128)} %steps_ref.5) | copy-start | bytes 9830404
  59.1 9.7 %copy-start.1 = (f32[3,2,160,640]{3,2,1,0:T(8,128)S(1)}, f32[3,2,160,640]{3,2,1,0:T(8,128)}, u32[]{:S(2)}) copy-start(f32[3,2,160,640]{3,2,1,0:T(8,128)} %changes_ref.5) | copy-start | bytes 7372804
  63.8 2.2 %collective-permute-start.16 = (bf16[2,2,160,512]{3,2,1,0:T(8,128)(2,1)S(1)}, bf16[2,2,160,512]{3,2,1,0:T(8,128)(2,1)S(1)}, u32[]{:S(2)}, u32[]{:S(2)}) collective-permute-start(bf16[2,2,160,512]{3,2,1,0:T(8,128)(2,1)S(1)} %get-tuple-element.36), channel_id=1, source_target_pairs={{0,4},{1,5},{2,6},{3,7},{4,0},{5,1},{6,2},{7,3},{8,12},{9,13},{10,... | collective-permute-start | bytes 1966088 | tf_op jit(solution)/shard_map/ppermute | solution.py:551
  66.1 4.2 %collective-permute-start.17 = (bf16[2,160,512]{2,1,0:T(8,128)(2,1)S(1)}, bf16[2,160,512]{2,1,0:T(8,128)(2,1)S(1)}, u32[]{:S(2)}, u32[]{:S(2)}) collective-permute-start(bf16[2,160,512]{2,1,0:T(8,128)(2,1)S(1)} %get-tuple-element.44), channel_id=1, source_target_pairs={{0,0},{1,1},{2,4},{3,5},{4,2},{5,3},{6,6},{7,7},{8,8},{9,9},{10,12... | collective-permute-start | bytes 983048 | tf_op jit(solution)/shard_map/ppermute | solution.py:551
  67.0 9.7 %copy-start.3 = (f32[2,160,640]{2,1,0:T(8,128)S(1)}, f32[2,160,640]{2,1,0:T(8,128)}, u32[]{:S(2)}) copy-start(f32[2,160,640]{2,1,0:T(8,128)} %transmission_ref.3) | copy-start | bytes 2457604
  67.0 9.7 %copy-start.5 = (f32[2,160,640]{2,1,0:T(8,128)S(1)}, f32[2,160,640]{2,1,0:T(8,128)}, u32[]{:S(2)}) copy-start(f32[2,160,640]{2,1,0:T(8,128)} %old_ref.3) | copy-start | bytes 2457604
  67.0 9.7 %copy-start.8 = (s32[1,2]{1,0:T(1,128)S(1)}, s32[1,2]{1,0:T(1,128)}, u32[]{:S(2)}) copy-start(s32[1,2]{1,0:T(1,128)} %pos_ref.3) | copy-start | bytes 28
  67.0 9.6 %collective-permute-start.18 = (bf16[2,160,512]{2,1,0:T(8,128)(2,1)S(1)}, bf16[2,160,512]{2,1,0:T(8,128)(2,1)S(1)}, u32[]{:S(2)}, u32[]{:S(2)}) collective-permute-start(bf16[2,160,512]{2,1,0:T(8,128)(2,1)S(1)} %get-tuple-element.45), channel_id=1, source_target_pairs={{0,1},{1,0},{2,5},{3,4},{4,3},{5,2},{6,7},{7,6},{8,9},{9,8},{10,13... | collective-permute-start | bytes 983048 | tf_op jit(solution)/shard_map/ppermute | solution.py:551

commit v7 on v5

--- a/solution.py
+++ b/solution.py
@@ -573,14 +573,15 @@
         return lax.dynamic_slice(probe, (part, mode, 0, 0), (1, 1, chunk, frame_len)).reshape(chunk, frame_len)
 
     same_block, flip_block = block(base + which), block(other_base + which)
-    from_far, from_near = send(same_block, far), send(flip_block, near)
+    from_far = send(same_block, far)
     from_cross = send(flip_block, cross)
     mate_positions = send(positions, mate)
     piece = call(cut_kernel, size((2, piece_len, frame_len), BF), count=2, smem=(0,), limit=16)(
         positions, transmission
     )
-    measured_low, from_near = barrier((measured[0].astype(BF), from_near))
-    target = send(measured_low, home)
+    flip_block, piece = barrier((flip_block, piece))
+    from_near = send(flip_block, near)
+    target = send(measured[0].astype(BF), home)
     q0 = jnp.concatenate([from_near, from_far, from_cross], axis=0)
     column = jnp.where(is_home, positions[0, 1], mate_positions[0, 1])
     place = jnp.stack([core, member, line, half, column]).astype(jnp.int32)

time: 102 us -> 102 us (level)
  starting transfers between devices: 28.2 us -> 27 us
    ppermute x19, starting transfers between devices: 28.2 us -> 27 us  [send(): return lax.ppermute(value, AXES, pairs)]
where the time goes in v7:
time: 102 us; the launch traced here: 101 us
  waiting for transfers between devices  27.4 us (27%)
  starting transfers between devices  27 us (26%)
  Pallas kernels  21.2 us (21%)
  blocking collectives  17.7 us (17%)
  local copies, waits for them, and re-layouts  4.15 us (4%)
  between operations  2.26 us (2%)
  other arithmetic  1.43 us (1%)
    ppermute x19, waiting for transfers between devices, send(): return lax.ppermute(value, AXES, pairs)  27.4 us
    ppermute x19, starting transfers between devices, send(): return lax.ppermute(value, AXES, pairs)  27 us
    all_to_all x1, blocking collectives, fast(): lax.all_to_all(row.reshape(devices, 1, LANES), AXES, split_axis=0, concat...  17.7 us
    pallas_call x1, Pallas kernels, fast(): call(forward_kernel, (size((2, 2, 3, frame_len, half_len), BF), half_fiel...  5.14 us
    pallas_call x1, Pallas kernels, fast(): call(backward_kernel, (size((2, 2, piece_len, frame_len), BF), piece_shap...  4.86 us
    pallas_call x1, Pallas kernels, fast(): call(gradient_kernel, (size(transmission.shape, F32), size((devices, LANE...  2.61 us
  transfers between devices with their start and end apart: 19, of which 9 were waited for; matrix products, arithmetic and copies ran while one was open for 3% of the time, Pallas kernels for 7%

profile of v7, /device:TPU:0, one launch (start us, length us, event | category | flops | bytes accessed | tf_op | source)
XLA Modules:
  0.0 101.2 jit_solution(5691435316239149601)
XLA Ops:
  0.6 1.0 dynamic-slice_bitcast_fusion
  1.6 5.1 %collective-permute-start.4 = (bf16[128,512]{1,0:T(8,128)(2,1)S(1)}, bf16[128,512]{1,0:T(8,128)(2,1)S(1)}, u32[]{:S(2)}, u32[]{:S(2)}) collective-permute-start(bf16[128,512]{1,0:T(8,128)(2,1)S(1)} %get-tuple-element.23), channel_id=1, source_target_pairs={{0,3},{1,2},{2,1},{3,0},{4,7},{5,6},{6,5},{7,4},{8,11},{9,10},{10,... | collective-permute-start | bytes 393224 | tf_op jit(solution)/shard_map/ppermute | solution.py:551
  6.8 1.1 %copy-done.2 = f32[2,160,640]{2,1,0:T(8,128)S(1)} copy-done((f32[2,160,640]{2,1,0:T(8,128)S(1)}, f32[2,160,640]{2,1,0:T(8,128)}, u32[]{:S(2)}) %copy-start.2) | copy-done | bytes 819224
  7.9 1.3 %shard_map.95 = bf16[2,160,512]{2,1,0:T(8,128)(2,1)S(1)} custom-call(s32[1,2]{1,0:T(1,128)} %pos_ref.3, f32[2,160,640]{2,1,0:T(8,128)S(1)} %copy-done.2), custom_call_target="tpu_custom_call" | custom-call | tf_op jit(solution)/shard_map/pallas_call | solution.py:579
  9.2 0.1 collective-permute-start.2
  9.3 0.6 collective-permute-start.3
  9.8 1.0 convert_bitcast_fusion
  10.8 0.7 collective-permute-start.1
  11.5 3.8 %collective-permute-start = (s32[1,2]{1,0:T(1,128)}, s32[1,2]{1,0:T(1,128)S(1)}, u32[]{:S(2)}, u32[]{:S(2)}) collective-permute-start(s32[1,2]{1,0:T(1,128)} %pos_ref.3), channel_id=1, source_target_pairs={{0,4},{1,5},{2,6},{3,7},{4,0},{5,1},{6,2},{7,3},{8,12},{9,13},{10,... | collective-permute-start | bytes 32 | tf_op jit(solution)/shard_map/ppermute | solution.py:551
  15.3 1.2 %slice.18 = s32[1,1]{1,0:T(1,128)} slice(s32[1,2]{1,0:T(1,128)} %pos_ref.3), slice={[0:1], [1:2]} | slice | bytes 8 | tf_op jit(solution)/shard_map/slice | solution.py:586
  16.5 0.0 collective-permute-done
  16.5 0.6 slice.19
  18.4 0.1 stack.23.place_ref
  18.5 0.0 collective-permute-done.2
  18.5 0.0 collective-permute-done.4
  18.5 0.0 collective-permute-done.3
  18.6 0.0 collective-permute-done.1.measured_ref
  18.6 1.6 %collective-permute-start.9 = (bf16[384,512]{1,0:T(8,128)(2,1)S(1)}, bf16[384,512]{1,0:T(8,128)(2,1)S(1)}, u32[]{:S(2)}, u32[]{:S(2)}) collective-permute-start(bf16[384,512]{1,0:T(8,128)(2,1)S(1)} %pad_maximum_fusion.q0_ref), channel_id=1, source_target_pairs={{0,8},{1,9},{2,10},{3,11},{4,12},{5,13},{6,14},{7,15},{8,0},{9,1},... | collective-permute-start | bytes 1179656 | tf_op jit(solution)/shard_map/ppermute | solution.py:551
  20.1 1.5 %collective-permute-start.7 = (bf16[384,512]{1,0:T(8,128)(2,1)S(1)}, bf16[384,512]{1,0:T(8,128)(2,1)S(1)}, u32[]{:S(2)}, u32[]{:S(2)}) collective-permute-start(bf16[384,512]{1,0:T(8,128)(2,1)S(1)} %pad_maximum_fusion.q0_ref), channel_id=1, source_target_pairs={{0,16},{1,17},{2,18},{3,19},{4,20},{5,21},{6,22},{7,23},{8,24},{9,... | collective-permute-start | bytes 1179656 | tf_op jit(solution)/shard_map/ppermute | solution.py:551
  21.7 0.7 collective-permute-start.5
  22.3 2.0 %collective-permute-start.6 = (bf16[2,160,512]{2,1,0:T(8,128)(2,1)S(1)}, bf16[2,160,512]{2,1,0:T(8,128)(2,1)S(1)}, u32[]{:S(2)}, u32[]{:S(2)}) collective-permute-start(bf16[2,160,512]{2,1,0:T(8,128)(2,1)S(1)} %shard_map.95), channel_id=1, source_target_pairs={{0,1},{1,0},{2,5},{3,4},{4,3},{5,2},{6,7},{7,6},{8,9},{9,8},{10,13... | collective-permute-start | bytes 983048 | tf_op jit(solution)/shard_map/ppermute | solution.py:551
  24.3 5.2 %collective-permute-done.9.q1_ref = bf16[384,512]{1,0:T(8,128)(2,1)S(1)} collective-permute-done((bf16[384,512]{1,0:T(8,128)(2,1)S(1)}, bf16[384,512]{1,0:T(8,128)(2,1)S(1)}, u32[]{:S(2)}, u32[]{:S(2)}) %collective-permute-start.9) | collective-permute-done | bytes 393248 | tf_op jit(solution)/shard_map/ppermute | solution.py:551
  29.6 1.6 %collective-permute-start.10 = (bf16[192,512]{1,0:T(8,128)(2,1)S(1)}, bf16[192,512]{1,0:T(8,128)(2,1)S(1)}, u32[]{:S(2)}, u32[]{:S(2)}) collective-permute-start(bf16[192,512]{1,0:T(8,128)(2,1)S(1)} %slice.25), channel_id=1, source_target_pairs={{0,16},{1,17},{2,18},{3,19},{4,20},{5,21},{6,22},{7,23},{8,24},{9,... | collective-permute-start | bytes 589832 | tf_op jit(solution)/shard_map/ppermute | solution.py:551
  31.2 0.2 collective-permute-done.7.q2_ref
  31.4 0.0 copy-start.4
  31.4 1.4 %collective-permute-start.8 = (bf16[192,512]{1,0:T(8,128)(2,1)S(1)}, bf16[192,512]{1,0:T(8,128)(2,1)S(1)}, u32[]{:S(2)}, u32[]{:S(2)}) collective-permute-start(bf16[192,512]{1,0:T(8,128)(2,1)S(1)} %slice.24), channel_id=1, source_target_pairs={{0,8},{1,9},{2,10},{3,11},{4,12},{5,13},{6,14},{7,15},{8,0},{9,1},... | collective-permute-start | bytes 589832 | tf_op jit(solution)/shard_map/ppermute | solution.py:551
  32.8 0.0 collective-permute-done.5.own_ref
  32.8 0.0 collective-permute-done.6.side_ref
  32.8 4.4 %collective-permute-done.10.q3b_ref = bf16[192,512]{1,0:T(8,128)(2,1)S(1)} collective-permute-done((bf16[192,512]{1,0:T(8,128)(2,1)S(1)}, bf16[192,512]{1,0:T(8,128)(2,1)S(1)}, u32[]{:S(2)}, u32[]{:S(2)}) %collective-permute-start.10) | collective-permute-done | bytes 196640 | tf_op jit(solution)/shard_map/ppermute | solution.py:551
  37.2 1.8 %collective-permute-done.8.q3a_ref = bf16[192,512]{1,0:T(8,128)(2,1)S(1)} collective-permute-done((bf16[192,512]{1,0:T(8,128)(2,1)S(1)}, bf16[192,512]{1,0:T(8,128)(2,1)S(1)}, u32[]{:S(2)}, u32[]{:S(2)}) %collective-permute-start.8) | collective-permute-done | bytes 196640 | tf_op jit(solution)/shard_map/ppermute | solution.py:551
  39.0 0.5 collective-permute-start.11
  39.5 0.1 collective-permute-start.12
  39.6 0.0 copy-done.6
  39.6 1.4 %shard_map.96.probe_ref = bf16[2,2,512,512]{3,2,1,0:T(8,128)(2,1)S(1)} custom-call(s32[5]{0:T(128)S(1)} %stack.23.place_ref, bf16[2,8,128,512]{3,2,1,0:T(8,128)(2,1)S(1)} %copy-done.6, bf16[384,512]{1,0:T(8,128)(2,1)S(1)} %pad_maximum_fusion.q0_ref, bf16[384,512]{1,0:T(8,128)(2,1)S(1)} %collective-permute-done.9.q1_ref, ...), custom_call_target="tpu_custom_call" | custom-call | tf_op jit(solution)/shard_map/pallas_call | solution.py:596
  41.0 0.0 collective-permute-done.11.mate_own_ref
  41.0 0.3 collective-permute-done.12.mate_side_ref
  41.2 0.0 copy-done.4
  41.2 5.1 %shard_map.97 = (bf16[2,2,3,512,256]{4,3,2,1,0:T(8,128)(2,1)S(1)}, bf16[2,2,512,256]{3,2,1,0:T(8,128)(2,1)S(1)}, bf16[512,256]{1,0:T(8,128)(2,1)S(1)}) custom-call(s32[5]{0:T(128)S(1)} %stack.23.place_ref, bf16[2,160,512]{2,1,0:T(8,128)(2,1)S(1)} %collective-permute-done.5.own_ref, bf16[2,160,512]{2,1,0:T(8,128)(2,1)S(1)} %collective-permute-done.6.side_ref, ...), custom_call_target="tpu_custom_call" | custom-call | flops 3221225472 | bytes 16777216 | tf_op jit(solution)/shard_map/pallas_call | solution.py:611
  46.4 0.4 collective-permute-start.13
  46.8 1.6 %shard_map.98 = (bf16[2,2,512,256]{3,2,1,0:T(8,128)(2,1)S(1)}, f32[512,256]{1,0:T(8,128)S(1)}) custom-call(s32[5]{0:T(128)S(1)} %stack.23.place_ref, bf16[2,2,3,512,256]{4,3,2,1,0:T(8,128)(2,1)S(1)} %get-tuple-element.33.turned_ref, bf16[128,512]{1,0:T(8,128)(2,1)S(1)} %collective-permute-done.1.measured_ref, bf16[3,512,512]{2,1,0:T(8,128)(2,1)S(1)} %copy-done.4), custom_call_target="tpu_custom_call" | custom-call | flops 1073741824 | bytes 4194304 | tf_op jit(solution)/shard_map/pallas_call | solution.py:626
  48.4 0.0 collective-permute-done.13
  48.4 0.1 fusion.2
  48.5 4.1 %collective-permute-start.14 = (bf16[512,256]{1,0:T(8,128)(2,1)S(1)}, bf16[512,256]{1,0:T(8,128)(2,1)S(1)}, u32[]{:S(2)}, u32[]{:S(2)}) collective-permute-start(bf16[512,256]{1,0:T(8,128)(2,1)S(1)} %fusion.2), channel_id=1, source_target_pairs={{0,1},{1,0},{2,3},{3,2},{4,5},{5,4},{6,7},{7,6},{8,9},{9,8},{10,11... | collective-permute-start | bytes 786440 | tf_op jit(solution)/shard_map/ppermute | solution.py:551
  52.6 6.6 %collective-permute-done.14 = bf16[512,256]{1,0:T(8,128)(2,1)S(1)} collective-permute-done((bf16[512,256]{1,0:T(8,128)(2,1)S(1)}, bf16[512,256]{1,0:T(8,128)(2,1)S(1)}, u32[]{:S(2)}, u32[]{:S(2)}) %collective-permute-start.14) | collective-permute-done | bytes 262176 | tf_op jit(solution)/shard_map/ppermute | solution.py:551
  59.2 0.1 fusion.3
  59.3 0.1 collective-permute-start.15
  59.4 1.1 %shard_map.99.own_ref = bf16[3,1024,256]{2,1,0:T(8,128)(2,1)S(1)} custom-call(bf16[2,2,512,256]{3,2,1,0:T(8,128)(2,1)S(1)} %get-tuple-element.36.far_ref, f32[512,256]{1,0:T(8,128)S(1)} %get-tuple-element.43.mine_ref, bf16[3,512,512]{2,1,0:T(8,128)(2,1)S(1)} %copy-done.4), custom_call_target="tpu_custom_call" | custom-call | flops 1073741824 | bytes 4194304 | tf_op jit(solution)/shard_map/pallas_call | solution.py:638
  60.5 0.4 collective-permute-done.15.mates_ref
  60.9 4.9 %shard_map.100 = (bf16[2,2,160,512]{3,2,1,0:T(8,128)(2,1)S(1)}, bf16[2,160,512]{2,1,0:T(8,128)(2,1)S(1)}, bf16[2,160,512]{2,1,0:T(8,128)(2,1)S(1)}) custom-call(s32[5]{0:T(128)S(1)} %stack.23.place_ref, bf16[2,2,512,256]{3,2,1,0:T(8,128)(2,1)S(1)} %get-tuple-element.32.far_ref, bf16[2,2,512,512]{3,2,1,0:T(8,128)(2,1)S(1)} %shard_map.96.probe_ref, ...), custom_call_target="tpu_custom_call" | custom-call | flops 3221225472 | bytes 12582912 | tf_op jit(solution)/shard_map/pallas_call | solution.py:647
  65.8 0.2 collective-permute-start.16
  66.0 2.0 %collective-permute-done.16 = bf16[2,2,160,512]{3,2,1,0:T(8,128)(2,1)S(1)} collective-permute-done((bf16[2,2,160,512]{3,2,1,0:T(8,128)(2,1)S(1)}, bf16[2,2,160,512]{3,2,1,0:T(8,128)(2,1)S(1)}, u32[]{:S(2)}, u32[]{:S(2)}) %collective-permute-start.16) | collective-permute-done | bytes 655392 | tf_op jit(solution)/shard_map/ppermute | solution.py:551
  67.9 0.2 fusion.1
  68.1 0.9 collective-permute-start.17
  69.0 0.0 copy-start.3
  69.0 0.0 copy-start.5
  69.0 1.8 %collective-permute-start.18 = (bf16[2,160,512]{2,1,0:T(8,128)(2,1)S(1)}, bf16[2,160,512]{2,1,0:T(8,128)(2,1)S(1)}, u32[]{:S(2)}, u32[]{:S(2)}) collective-permute-start(bf16[2,160,512]{2,1,0:T(8,128)(2,1)S(1)} %get-tuple-element.47), channel_id=1, source_target_pairs={{0,1},{1,0},{2,5},{3,4},{4,3},{5,2},{6,7},{7,6},{8,9},{9,8},{10,13... | collective-permute-start | bytes 983048 | tf_op jit(solution)/shard_map/ppermute | solution.py:551
  70.8 0.0 copy-done
  70.8 1.7 %shard_map.101.row_ref = f32[1,128]{1,0:T(1,128)S(1)} custom-call(f32[4,2,160,640]{3,2,1,0:T(8,128)S(1)} %copy-done, f32[3,2,160,640]{3,2,1,0:T(8,128)S(1)} %copy-done.1), custom_call_target="tpu_custom_call" | custom-call | flops 18022400 | bytes 5734400 | tf_op jit(solution)/shard_map/pallas_call | solution.py:667
  72.5 0.0 collective-permute-done.17
  72.6 6.5 %collective-permute-done.18 = bf16[2,160,512]{2,1,0:T(8,128)(2,1)S(1)} collective-permute-done((bf16[2,160,512]{2,1,0:T(8,128)(2,1)S(1)}, bf16[2,160,512]{2,1,0:T(8,128)(2,1)S(1)}, u32[]{:S(2)}, u32[]{:S(2)}) %collective-permute-start.18) | collective-permute-done | bytes 327712 | tf_op jit(solution)/shard_map/ppermute | solution.py:551
  79.1 0.1 add_convert_fusion.data_ref
  79.2 2.6 %shard_map.102 = (f32[2,160,640]{2,1,0:T(8,128)S(1)}, f32[32,128]{1,0:T(8,128)S(1)}) custom-call(s32[1,2]{1,0:T(1,128)} %pos_ref.3, bf16[2,160,512]{2,1,0:T(8,128)(2,1)S(1)} %add_convert_fusion.data_ref, f32[2,160,640]{2,1,0:T(8,128)S(1)} %copy-done.3, f32[2,160,640]{2,1,0:T(8,128)S(1)} %copy-done.5, f32[4,2,160,640]{3,2,1,0:T(8,128)S(1)} %copy-done, ...), custom_call_target="tpu_custom_call" | custom-call | flops 13107200 | bytes 8192000 | tf_op jit(solution)/shard_map/pallas_call | solution.py:675
  81.8 17.7 %all_to_all.5 = f32[32,1,128]{2,1,0:T(1,128)S(1)} all-to-all(f32[32,1,128]{2,1,0:T(1,128)S(1)} %bitcast.28), channel_id=1, replica_groups=mesh['region'=8,'grp'=4] {'region','grp'}, dimensions={0} | all-to-all | bytes 32768 | tf_op jit(solution)/shard_map/all_to_all | solution.py:684
  99.6 1.5 %shard_map.103 = (f32[2,160,640]{2,1,0:T(8,128)}, f32[2,160,640]{2,1,0:T(8,128)}) custom-call(f32[32,128]{1,0:T(8,128)S(1)} %bitcast.27, f32[2,160,640]{2,1,0:T(8,128)S(1)} %copy-done.3, f32[2,160,640]{2,1,0:T(8,128)S(1)} %get-tuple-element.41.gradient_ref, f32[2,160,640]{2,1,0:T(8,128)S(1)} %copy-done.5, f32[4,2,160,640]{3,2,1,0:T(8,128)S(1)} %copy-done, ...), custom_call_target="tpu_custom_call" | custom-call | flops 8192000 | bytes 9011200 | tf_op jit(solution)/shard_map/pallas_call | solution.py:687
  (10 shorter events, 0.1 us)
Async XLA Ops:
  1.6 16.9 %collective-permute-start.4 = (bf16[128,512]{1,0:T(8,128)(2,1)S(1)}, bf16[128,512]{1,0:T(8,128)(2,1)S(1)}, u32[]{:S(2)}, u32[]{:S(2)}) collective-permute-start(bf16[128,512]{1,0:T(8,128)(2,1)S(1)} %get-tuple-element.23), channel_id=1, source_target_pairs={{0,3},{1,2},{2,1},{3,0},{4,7},{5,6},{6,5},{7,4},{8,11},{9,10},{10,... | collective-permute-start | bytes 393224 | tf_op jit(solution)/shard_map/ppermute | solution.py:551
  6.8 1.1 %copy-start.2 = (f32[2,160,640]{2,1,0:T(8,128)S(1)}, f32[2,160,640]{2,1,0:T(8,128)}, u32[]{:S(2)}) copy-start(f32[2,160,640]{2,1,0:T(8,128)} %transmission_ref.3) | copy-start | bytes 2457604
  7.9 31.7 %copy-start.6 = (bf16[2,8,128,512]{3,2,1,0:T(8,128)(2,1)S(1)}, bf16[2,8,128,512]{3,2,1,0:T(8,128)(2,1)}, u32[]{:S(2)}) copy-start(bf16[2,8,128,512]{3,2,1,0:T(8,128)(2,1)} %all_ref.1) | copy-start | bytes 6291460
  9.2 9.3 %collective-permute-start.2 = (bf16[128,512]{1,0:T(8,128)(2,1)S(1)}, bf16[128,512]{1,0:T(8,128)(2,1)S(1)}, u32[]{:S(2)}, u32[]{:S(2)}) collective-permute-start(bf16[128,512]{1,0:T(8,128)(2,1)S(1)} %get-tuple-element.23), channel_id=1, source_target_pairs={{0,1},{1,0},{2,3},{3,2},{4,5},{5,4},{6,7},{7,6},{8,9},{9,8},{10,11... | collective-permute-start | bytes 393224 | tf_op jit(solution)/shard_map/ppermute | solution.py:551
  9.3 9.3 %collective-permute-start.3 = (bf16[128,512]{1,0:T(8,128)(2,1)S(1)}, bf16[128,512]{1,0:T(8,128)(2,1)S(1)}, u32[]{:S(2)}, u32[]{:S(2)}) collective-permute-start(bf16[128,512]{1,0:T(8,128)(2,1)S(1)} %get-tuple-element.44), channel_id=1, source_target_pairs={{0,2},{1,3},{2,0},{3,1},{4,6},{5,7},{6,4},{7,5},{8,10},{9,11},{10,... | collective-permute-start | bytes 393224 | tf_op jit(solution)/shard_map/ppermute | solution.py:551
  10.8 7.8 %collective-permute-start.1 = (bf16[128,512]{1,0:T(8,128)(2,1)S(1)}, bf16[128,512]{1,0:T(8,128)(2,1)S(1)}, u32[]{:S(2)}, u32[]{:S(2)}) collective-permute-start(bf16[128,512]{1,0:T(8,128)(2,1)S(1)} %convert_bitcast_fusion), channel_id=1, source_target_pairs={{0,0},{1,1},{2,4},{3,5},{4,2},{5,3},{6,6},{7,7},{8,8},{9,9},{10,12... | collective-permute-start | bytes 393224 | tf_op jit(solution)/shard_map/ppermute | solution.py:551
  11.5 5.1 %collective-permute-start = (s32[1,2]{1,0:T(1,128)}, s32[1,2]{1,0:T(1,128)S(1)}, u32[]{:S(2)}, u32[]{:S(2)}) collective-permute-start(s32[1,2]{1,0:T(1,128)} %pos_ref.3), channel_id=1, source_target_pairs={{0,4},{1,5},{2,6},{3,7},{4,0},{5,1},{6,2},{7,3},{8,12},{9,13},{10,... | collective-permute-start | bytes 32 | tf_op jit(solution)/shard_map/ppermute | solution.py:551
  18.6 11.0 %collective-permute-start.9 = (bf16[384,512]{1,0:T(8,128)(2,1)S(1)}, bf16[384,512]{1,0:T(8,128)(2,1)S(1)}, u32[]{:S(2)}, u32[]{:S(2)}) collective-permute-start(bf16[384,512]{1,0:T(8,128)(2,1)S(1)} %pad_maximum_fusion.q0_ref), channel_id=1, source_target_pairs={{0,8},{1,9},{2,10},{3,11},{4,12},{5,13},{6,14},{7,15},{8,0},{9,1},... | collective-permute-start | bytes 1179656 | tf_op jit(solution)/shard_map/ppermute | solution.py:551
  20.1 11.2 %collective-permute-start.7 = (bf16[384,512]{1,0:T(8,128)(2,1)S(1)}, bf16[384,512]{1,0:T(8,128)(2,1)S(1)}, u32[]{:S(2)}, u32[]{:S(2)}) collective-permute-start(bf16[384,512]{1,0:T(8,128)(2,1)S(1)} %pad_maximum_fusion.q0_ref), channel_id=1, source_target_pairs={{0,16},{1,17},{2,18},{3,19},{4,20},{5,21},{6,22},{7,23},{8,24},{9,... | collective-permute-start | bytes 1179656 | tf_op jit(solution)/shard_map/ppermute | solution.py:551
  21.7 11.1 %collective-permute-start.5 = (bf16[2,160,512]{2,1,0:T(8,128)(2,1)S(1)}, bf16[2,160,512]{2,1,0:T(8,128)(2,1)S(1)}, u32[]{:S(2)}, u32[]{:S(2)}) collective-permute-start(bf16[2,160,512]{2,1,0:T(8,128)(2,1)S(1)} %shard_map.95), channel_id=1, source_target_pairs={{0,0},{1,1},{2,4},{3,5},{4,2},{5,3},{6,6},{7,7},{8,8},{9,9},{10,12... | collective-permute-start | bytes 983048 | tf_op jit(solution)/shard_map/ppermute | solution.py:551
  22.3 10.4 %collective-permute-start.6 = (bf16[2,160,512]{2,1,0:T(8,128)(2,1)S(1)}, bf16[2,160,512]{2,1,0:T(8,128)(2,1)S(1)}, u32[]{:S(2)}, u32[]{:S(2)}) collective-permute-start(bf16[2,160,512]{2,1,0:T(8,128)(2,1)S(1)} %shard_map.95), channel_id=1, source_target_pairs={{0,1},{1,0},{2,5},{3,4},{4,3},{5,2},{6,7},{7,6},{8,9},{9,8},{10,13... | collective-permute-start | bytes 983048 | tf_op jit(solution)/shard_map/ppermute | solution.py:551
  29.6 7.6 %collective-permute-start.10 = (bf16[192,512]{1,0:T(8,128)(2,1)S(1)}, bf16[192,512]{1,0:T(8,128)(2,1)S(1)}, u32[]{:S(2)}, u32[]{:S(2)}) collective-permute-start(bf16[192,512]{1,0:T(8,128)(2,1)S(1)} %slice.25), channel_id=1, source_target_pairs={{0,16},{1,17},{2,18},{3,19},{4,20},{5,21},{6,22},{7,23},{8,24},{9,... | collective-permute-start | bytes 589832 | tf_op jit(solution)/shard_map/ppermute | solution.py:551
  31.4 9.8 %copy-start.4 = (bf16[3,512,512]{2,1,0:T(8,128)(2,1)S(1)}, bf16[3,512,512]{2,1,0:T(8,128)(2,1)}, u32[]{:S(2)}) copy-start(bf16[3,512,512]{2,1,0:T(8,128)(2,1)} %constant.23.clone.right_ref) | copy-start | bytes 4718596
  31.4 7.6 %collective-permute-start.8 = (bf16[192,512]{1,0:T(8,128)(2,1)S(1)}, bf16[192,512]{1,0:T(8,128)(2,1)S(1)}, u32[]{:S(2)}, u32[]{:S(2)}) collective-permute-start(bf16[192,512]{1,0:T(8,128)(2,1)S(1)} %slice.24), channel_id=1, source_target_pairs={{0,8},{1,9},{2,10},{3,11},{4,12},{5,13},{6,14},{7,15},{8,0},{9,1},... | collective-permute-start | bytes 589832 | tf_op jit(solution)/shard_map/ppermute | solution.py:551
  39.0 2.0 %collective-permute-start.11 = (bf16[2,160,512]{2,1,0:T(8,128)(2,1)S(1)}, bf16[2,160,512]{2,1,0:T(8,128)(2,1)S(1)}, u32[]{:S(2)}, u32[]{:S(2)}) collective-permute-start(bf16[2,160,512]{2,1,0:T(8,128)(2,1)S(1)} %collective-permute-done.5.own_ref), channel_id=1, source_target_pairs={{0,4},{1,5},{2,6},{3,7},{4,0},{5,1},{6,2},{7,3},{8,12},{9,13},{10,... | collective-permute-start | bytes 983048 | tf_op jit(solution)/shard_map/ppermute | solution.py:551
  39.5 1.7 %collective-permute-start.12 = (bf16[2,160,512]{2,1,0:T(8,128)(2,1)S(1)}, bf16[2,160,512]{2,1,0:T(8,128)(2,1)S(1)}, u32[]{:S(2)}, u32[]{:S(2)}) collective-permute-start(bf16[2,160,512]{2,1,0:T(8,128)(2,1)S(1)} %collective-permute-done.6.side_ref), channel_id=1, source_target_pairs={{0,4},{1,5},{2,6},{3,7},{4,0},{5,1},{6,2},{7,3},{8,12},{9,13},{10,... | collective-permute-start | bytes 983048 | tf_op jit(solution)/shard_map/ppermute | solution.py:551
  46.4 2.1 %collective-permute-start.13 = (bf16[512,256]{1,0:T(8,128)(2,1)S(1)}, bf16[512,256]{1,0:T(8,128)(2,1)S(1)}, u32[]{:S(2)}, u32[]{:S(2)}) collective-permute-start(bf16[512,256]{1,0:T(8,128)(2,1)S(1)} %get-tuple-element.35), channel_id=1, source_target_pairs={{0,4},{1,5},{2,6},{3,7},{4,0},{5,1},{6,2},{7,3},{8,12},{9,13},{10,... | collective-permute-start | bytes 786440 | tf_op jit(solution)/shard_map/ppermute | solution.py:551
  48.5 10.7 %collective-permute-start.14 = (bf16[512,256]{1,0:T(8,128)(2,1)S(1)}, bf16[512,256]{1,0:T(8,128)(2,1)S(1)}, u32[]{:S(2)}, u32[]{:S(2)}) collective-permute-start(bf16[512,256]{1,0:T(8,128)(2,1)S(1)} %fusion.2), channel_id=1, source_target_pairs={{0,1},{1,0},{2,3},{3,2},{4,5},{5,4},{6,7},{7,6},{8,9},{9,8},{10,11... | collective-permute-start | bytes 786440 | tf_op jit(solution)/shard_map/ppermute | solution.py:551
  59.3 1.6 %collective-permute-start.15 = (bf16[512,256]{1,0:T(8,128)(2,1)S(1)}, bf16[512,256]{1,0:T(8,128)(2,1)S(1)}, u32[]{:S(2)}, u32[]{:S(2)}) collective-permute-start(bf16[512,256]{1,0:T(8,128)(2,1)S(1)} %get-tuple-element.42), channel_id=1, source_target_pairs={{0,4},{1,5},{2,6},{3,7},{4,0},{5,1},{6,2},{7,3},{8,12},{9,13},{10,... | collective-permute-start | bytes 786440 | tf_op jit(solution)/shard_map/ppermute | solution.py:551
  60.9 9.9 %copy-start = (f32[4,2,160,640]{3,2,1,0:T(8,128)S(1)}, f32[4,2,160,640]{3,2,1,0:T(8,128)}, u32[]{:S(2)}) copy-start(f32[4,2,160,640]{3,2,1,0:T(8,128)} %steps_ref.5) | copy-start | bytes 9830404
  60.9 9.9 %copy-start.1 = (f32[3,2,160,640]{3,2,1,0:T(8,128)S(1)}, f32[3,2,160,640]{3,2,1,0:T(8,128)}, u32[]{:S(2)}) copy-start(f32[3,2,160,640]{3,2,1,0:T(8,128)} %changes_ref.5) | copy-start | bytes 7372804
  65.8 2.2 %collective-permute-start.16 = (bf16[2,2,160,512]{3,2,1,0:T(8,128)(2,1)S(1)}, bf16[2,2,160,512]{3,2,1,0:T(8,128)(2,1)S(1)}, u32[]{:S(2)}, u32[]{:S(2)}) collective-permute-start(bf16[2,2,160,512]{3,2,1,0:T(8,128)(2,1)S(1)} %get-tuple-element.38), channel_id=1, source_target_pairs={{0,4},{1,5},{2,6},{3,7},{4,0},{5,1},{6,2},{7,3},{8,12},{9,13},{10,... | collective-permute-start | bytes 1966088 | tf_op jit(solution)/shard_map/ppermute | solution.py:551
  68.1 4.4 %collective-permute-start.17 = (bf16[2,160,512]{2,1,0:T(8,128)(2,1)S(1)}, bf16[2,160,512]{2,1,0:T(8,128)(2,1)S(1)}, u32[]{:S(2)}, u32[]{:S(2)}) collective-permute-start(bf16[2,160,512]{2,1,0:T(8,128)(2,1)S(1)} %get-tuple-element.46), channel_id=1, source_target_pairs={{0,0},{1,1},{2,4},{3,5},{4,2},{5,3},{6,6},{7,7},{8,8},{9,9},{10,12... | collective-permute-start | bytes 983048 | tf_op jit(solution)/shard_map/ppermute | solution.py:551
  69.0 10.2 %copy-start.3 = (f32[2,160,640]{2,1,0:T(8,128)S(1)}, f32[2,160,640]{2,1,0:T(8,128)}, u32[]{:S(2)}) copy-start(f32[2,160,640]{2,1,0:T(8,128)} %transmission_ref.3) | copy-start | bytes 2457604
  69.0 10.2 %copy-start.5 = (f32[2,160,640]{2,1,0:T(8,128)S(1)}, f32[2,160,640]{2,1,0:T(8,128)}, u32[]{:S(2)}) copy-start(f32[2,160,640]{2,1,0:T(8,128)} %old_ref.3) | copy-start | bytes 2457604
  69.0 10.1 %collective-permute-start.18 = (bf16[2,160,512]{2,1,0:T(8,128)(2,1)S(1)}, bf16[2,160,512]{2,1,0:T(8,128)(2,1)S(1)}, u32[]{:S(2)}, u32[]{:S(2)}) collective-permute-start(bf16[2,160,512]{2,1,0:T(8,128)(2,1)S(1)} %get-tuple-element.47), channel_id=1, source_target_pairs={{0,1},{1,0},{2,5},{3,4},{4,3},{5,2},{6,7},{7,6},{8,9},{9,8},{10,13... | collective-permute-start | bytes 983048 | tf_op jit(solution)/shard_map/ppermute | solution.py:551

commit v8 on v7

--- a/solution.py
+++ b/solution.py
@@ -585,8 +585,9 @@
     q0 = jnp.concatenate([from_near, from_far, from_cross], axis=0)
     column = jnp.where(is_home, positions[0, 1], mate_positions[0, 1])
     place = jnp.stack([core, member, line, half, column]).astype(jnp.int32)
+    q1 = send(q0, along_x)
     piece, place, target, q0 = barrier((piece, place, target, q0))
-    q1, q2 = send(q0, along_x), send(q0, along_y)
+    q2 = send(q0, along_y)
     own = send(piece, home)
     side = send(piece, beside)
     cut = q0.shape[0] // 2

time: 102 us -> 102 us (level)
  waiting for transfers between devices: 27.4 us -> 35.3 us
  starting transfers between devices: 27 us -> 20.3 us
    ppermute x19, waiting for transfers between devices: 27.4 us -> 35.3 us  [send(): return lax.ppermute(value, AXES, pairs)]
    ppermute x19, starting transfers between devices: 27 us -> 20.3 us  [send(): return lax.ppermute(value, AXES, pairs)]
  transfers between devices with their start and end apart: 19 -> 19, of which waited for: 9 -> 10; matrix products, arithmetic and copies ran while one was open for 3% -> 2% of each run, Pallas kernels for 7% -> 7%
where the time goes in v8:
time: 102 us
  waiting for transfers between devices  35.3 us (35%)
  Pallas kernels  20.8 us (20%)
  starting transfers between devices  20.3 us (20%)
  blocking collectives  17.7 us (17%)
  local copies, waits for them, and re-layouts  4.19 us (4%)
  between operations  2.31 us (2%)
  other arithmetic  1.4 us (1%)
    ppermute x19, waiting for transfers between devices, send(): return lax.ppermute(value, AXES, pairs)  35.3 us
    ppermute x19, starting transfers between devices, send(): return lax.ppermute(value, AXES, pairs)  20.3 us
    all_to_all x1, blocking collectives, fast(): lax.all_to_all(row.reshape(devices, 1, LANES), AXES, split_axis=0, concat...  17.7 us
    pallas_call x1, Pallas kernels, fast(): call(forward_kernel, (size((2, 2, 3, frame_len, half_len), BF), half_fiel...  5.14 us
    pallas_call x1, Pallas kernels, fast(): call(backward_kernel, (size((2, 2, piece_len, frame_len), BF), piece_shap...  4.86 us
    pallas_call x1, Pallas kernels, fast(): call(gradient_kernel, (size(transmission.shape, F32), size((devices, LANE...  2.49 us
  transfers between devices with their start and end apart: 19, of which 10 were waited for; matrix products, arithmetic and copies ran while one was open for 2% of the time, Pallas kernels for 7%

profile of v8, /device:TPU:0, one launch (start us, length us, event | category | flops | bytes accessed | tf_op | source)
XLA Modules:
  0.0 102.1 jit_solution(18092910568107053879)
XLA Ops:
  0.6 0.0 copy-start.8
  0.7 1.0 dynamic-slice_bitcast_fusion
  1.7 5.1 %collective-permute-start.4 = (bf16[128,512]{1,0:T(8,128)(2,1)S(1)}, bf16[128,512]{1,0:T(8,128)(2,1)S(1)}, u32[]{:S(2)}, u32[]{:S(2)}) collective-permute-start(bf16[128,512]{1,0:T(8,128)(2,1)S(1)} %get-tuple-element.23), channel_id=1, source_target_pairs={{0,3},{1,2},{2,1},{3,0},{4,7},{5,6},{6,5},{7,4},{8,11},{9,10},{10,... | collective-permute-start | bytes 393224 | tf_op jit(solution)/shard_map/ppermute | solution.py:551
  6.8 0.0 collective-permute-start
  6.8 1.1 %copy-done.2 = f32[2,160,640]{2,1,0:T(8,128)S(1)} copy-done((f32[2,160,640]{2,1,0:T(8,128)S(1)}, f32[2,160,640]{2,1,0:T(8,128)}, u32[]{:S(2)}) %copy-start.2) | copy-done | bytes 819224
  7.9 0.7 copy-done.7
  8.6 1.0 shard_map.95
  9.6 0.1 collective-permute-start.2
  9.7 0.6 collective-permute-start.3
  10.3 1.0 convert_bitcast_fusion
  11.3 0.7 collective-permute-start.1
  12.0 0.6 slice.18
  12.6 0.0 collective-permute-done
  12.6 0.6 slice.19
  14.4 0.1 stack.23.place_ref
  14.5 2.2 %collective-permute-done.2 = bf16[128,512]{1,0:T(8,128)(2,1)S(1)} collective-permute-done((bf16[128,512]{1,0:T(8,128)(2,1)S(1)}, bf16[128,512]{1,0:T(8,128)(2,1)S(1)}, u32[]{:S(2)}, u32[]{:S(2)}) %collective-permute-start.2) | collective-permute-done | bytes 131104 | tf_op jit(solution)/shard_map/ppermute | solution.py:551
  16.7 4.1 %collective-permute-done.3 = bf16[128,512]{1,0:T(8,128)(2,1)S(1)} collective-permute-done((bf16[128,512]{1,0:T(8,128)(2,1)S(1)}, bf16[128,512]{1,0:T(8,128)(2,1)S(1)}, u32[]{:S(2)}, u32[]{:S(2)}) %collective-permute-start.3) | collective-permute-done | bytes 131104 | tf_op jit(solution)/shard_map/ppermute | solution.py:551
  20.8 0.0 collective-permute-done.4
  20.8 0.0 collective-permute-done.1.measured_ref
  20.9 1.6 %collective-permute-start.7 = (bf16[384,512]{1,0:T(8,128)(2,1)S(1)}, bf16[384,512]{1,0:T(8,128)(2,1)S(1)}, u32[]{:S(2)}, u32[]{:S(2)}) collective-permute-start(bf16[384,512]{1,0:T(8,128)(2,1)S(1)} %constant_dynamic-update-slice_fusion.q0_ref), channel_id=1, source_target_pairs={{0,16},{1,17},{2,18},{3,19},{4,20},{5,21},{6,22},{7,23},{8,24},{9,... | collective-permute-start | bytes 1179656 | tf_op jit(solution)/shard_map/ppermute | solution.py:551
  22.4 1.5 %collective-permute-start.9 = (bf16[384,512]{1,0:T(8,128)(2,1)S(1)}, bf16[384,512]{1,0:T(8,128)(2,1)S(1)}, u32[]{:S(2)}, u32[]{:S(2)}) collective-permute-start(bf16[384,512]{1,0:T(8,128)(2,1)S(1)} %constant_dynamic-update-slice_fusion.q0_ref), channel_id=1, source_target_pairs={{0,8},{1,9},{2,10},{3,11},{4,12},{5,13},{6,14},{7,15},{8,0},{9,1},... | collective-permute-start | bytes 1179656 | tf_op jit(solution)/shard_map/ppermute | solution.py:551
  23.9 0.7 collective-permute-start.5
  24.6 0.1 collective-permute-start.6
  24.7 8.1 %collective-permute-done.7.q2_ref = bf16[384,512]{1,0:T(8,128)(2,1)S(1)} collective-permute-done((bf16[384,512]{1,0:T(8,128)(2,1)S(1)}, bf16[384,512]{1,0:T(8,128)(2,1)S(1)}, u32[]{:S(2)}, u32[]{:S(2)}) %collective-permute-start.7) | collective-permute-done | bytes 393248 | tf_op jit(solution)/shard_map/ppermute | solution.py:551
  32.8 1.6 %collective-permute-start.8 = (bf16[192,512]{1,0:T(8,128)(2,1)S(1)}, bf16[192,512]{1,0:T(8,128)(2,1)S(1)}, u32[]{:S(2)}, u32[]{:S(2)}) collective-permute-start(bf16[192,512]{1,0:T(8,128)(2,1)S(1)} %slice.24), channel_id=1, source_target_pairs={{0,8},{1,9},{2,10},{3,11},{4,12},{5,13},{6,14},{7,15},{8,0},{9,1},... | collective-permute-start | bytes 589832 | tf_op jit(solution)/shard_map/ppermute | solution.py:551
  34.4 0.0 collective-permute-done.9.q1_ref
  34.4 0.0 copy-start.4
  34.4 1.6 %collective-permute-start.10 = (bf16[192,512]{1,0:T(8,128)(2,1)S(1)}, bf16[192,512]{1,0:T(8,128)(2,1)S(1)}, u32[]{:S(2)}, u32[]{:S(2)}) collective-permute-start(bf16[192,512]{1,0:T(8,128)(2,1)S(1)} %slice.25), channel_id=1, source_target_pairs={{0,16},{1,17},{2,18},{3,19},{4,20},{5,21},{6,22},{7,23},{8,24},{9,... | collective-permute-start | bytes 589832 | tf_op jit(solution)/shard_map/ppermute | solution.py:551
  36.0 0.0 collective-permute-done.5.own_ref
  36.0 0.0 collective-permute-done.6.side_ref
  36.0 3.9 %collective-permute-done.8.q3a_ref = bf16[192,512]{1,0:T(8,128)(2,1)S(1)} collective-permute-done((bf16[192,512]{1,0:T(8,128)(2,1)S(1)}, bf16[192,512]{1,0:T(8,128)(2,1)S(1)}, u32[]{:S(2)}, u32[]{:S(2)}) %collective-permute-start.8) | collective-permute-done | bytes 196640 | tf_op jit(solution)/shard_map/ppermute | solution.py:551
  39.9 1.3 %collective-permute-done.10.q3b_ref = bf16[192,512]{1,0:T(8,128)(2,1)S(1)} collective-permute-done((bf16[192,512]{1,0:T(8,128)(2,1)S(1)}, bf16[192,512]{1,0:T(8,128)(2,1)S(1)}, u32[]{:S(2)}, u32[]{:S(2)}) %collective-permute-start.10) | collective-permute-done | bytes 196640 | tf_op jit(solution)/shard_map/ppermute | solution.py:551
  41.2 0.0 collective-permute-start.11
  41.2 0.5 collective-permute-start.12
  41.7 1.4 %shard_map.96.probe_ref = bf16[2,2,512,512]{3,2,1,0:T(8,128)(2,1)S(1)} custom-call(s32[5]{0:T(128)S(1)} %stack.23.place_ref, bf16[2,8,128,512]{3,2,1,0:T(8,128)(2,1)S(1)} %copy-done.6, bf16[384,512]{1,0:T(8,128)(2,1)S(1)} %constant_dynamic-update-slice_fusion.q0_ref, bf16[384,512]{1,0:T(8,128)(2,1)S(1)} %collective-permute-done.9.q1_ref, ...), custom_call_target="tpu_custom_call" | custom-call | tf_op jit(solution)/shard_map/pallas_call | solution.py:597
  43.1 0.0 collective-permute-done.11.mate_own_ref
  43.1 0.2 collective-permute-done.12.mate_side_ref
  43.3 0.0 copy-done.4
  43.3 5.1 %shard_map.97 = (bf16[2,2,3,512,256]{4,3,2,1,0:T(8,128)(2,1)S(1)}, bf16[2,2,512,256]{3,2,1,0:T(8,128)(2,1)S(1)}, bf16[512,256]{1,0:T(8,128)(2,1)S(1)}) custom-call(s32[5]{0:T(128)S(1)} %stack.23.place_ref, bf16[2,160,512]{2,1,0:T(8,128)(2,1)S(1)} %collective-permute-done.5.own_ref, bf16[2,160,512]{2,1,0:T(8,128)(2,1)S(1)} %collective-permute-done.6.side_ref, ...), custom_call_target="tpu_custom_call" | custom-call | flops 3221225472 | bytes 16777216 | tf_op jit(solution)/shard_map/pallas_call | solution.py:612
  48.5 0.2 collective-permute-start.13
  48.7 1.6 %shard_map.98 = (bf16[2,2,512,256]{3,2,1,0:T(8,128)(2,1)S(1)}, f32[512,256]{1,0:T(8,128)S(1)}) custom-call(s32[5]{0:T(128)S(1)} %stack.23.place_ref, bf16[2,2,3,512,256]{4,3,2,1,0:T(8,128)(2,1)S(1)} %get-tuple-element.33.turned_ref, bf16[128,512]{1,0:T(8,128)(2,1)S(1)} %collective-permute-done.1.measured_ref, bf16[3,512,512]{2,1,0:T(8,128)(2,1)S(1)} %copy-done.4), custom_call_target="tpu_custom_call" | custom-call | flops 1073741824 | bytes 4194304 | tf_op jit(solution)/shard_map/pallas_call | solution.py:627
  50.3 0.0 collective-permute-done.13
  50.3 0.1 fusion.2
  50.4 3.2 %collective-permute-start.14 = (bf16[512,256]{1,0:T(8,128)(2,1)S(1)}, bf16[512,256]{1,0:T(8,128)(2,1)S(1)}, u32[]{:S(2)}, u32[]{:S(2)}) collective-permute-start(bf16[512,256]{1,0:T(8,128)(2,1)S(1)} %fusion.2), channel_id=1, source_target_pairs={{0,1},{1,0},{2,3},{3,2},{4,5},{5,4},{6,7},{7,6},{8,9},{9,8},{10,11... | collective-permute-start | bytes 786440 | tf_op jit(solution)/shard_map/ppermute | solution.py:551
  53.6 6.6 %collective-permute-done.14 = bf16[512,256]{1,0:T(8,128)(2,1)S(1)} collective-permute-done((bf16[512,256]{1,0:T(8,128)(2,1)S(1)}, bf16[512,256]{1,0:T(8,128)(2,1)S(1)}, u32[]{:S(2)}, u32[]{:S(2)}) %collective-permute-start.14) | collective-permute-done | bytes 262176 | tf_op jit(solution)/shard_map/ppermute | solution.py:551
  60.2 0.1 fusion.3
  60.3 0.1 collective-permute-start.15
  60.3 1.1 %shard_map.99.own_ref = bf16[3,1024,256]{2,1,0:T(8,128)(2,1)S(1)} custom-call(bf16[2,2,512,256]{3,2,1,0:T(8,128)(2,1)S(1)} %get-tuple-element.36.far_ref, f32[512,256]{1,0:T(8,128)S(1)} %get-tuple-element.43.mine_ref, bf16[3,512,512]{2,1,0:T(8,128)(2,1)S(1)} %copy-done.4), custom_call_target="tpu_custom_call" | custom-call | flops 1073741824 | bytes 4194304 | tf_op jit(solution)/shard_map/pallas_call | solution.py:639
  61.5 0.4 collective-permute-done.15.mates_ref
  61.9 4.9 %shard_map.100 = (bf16[2,2,160,512]{3,2,1,0:T(8,128)(2,1)S(1)}, bf16[2,160,512]{2,1,0:T(8,128)(2,1)S(1)}, bf16[2,160,512]{2,1,0:T(8,128)(2,1)S(1)}) custom-call(s32[5]{0:T(128)S(1)} %stack.23.place_ref, bf16[2,2,512,256]{3,2,1,0:T(8,128)(2,1)S(1)} %get-tuple-element.32.far_ref, bf16[2,2,512,512]{3,2,1,0:T(8,128)(2,1)S(1)} %shard_map.96.probe_ref, ...), custom_call_target="tpu_custom_call" | custom-call | flops 3221225472 | bytes 12582912 | tf_op jit(solution)/shard_map/pallas_call | solution.py:648
  66.7 0.2 collective-permute-start.16
  66.9 1.9 %collective-permute-done.16 = bf16[2,2,160,512]{3,2,1,0:T(8,128)(2,1)S(1)} collective-permute-done((bf16[2,2,160,512]{3,2,1,0:T(8,128)(2,1)S(1)}, bf16[2,2,160,512]{3,2,1,0:T(8,128)(2,1)S(1)}, u32[]{:S(2)}, u32[]{:S(2)}) %collective-permute-start.16) | collective-permute-done | bytes 655392 | tf_op jit(solution)/shard_map/ppermute | solution.py:551
  68.9 0.2 fusion.1
  69.1 0.9 collective-permute-start.17
  69.9 0.0 copy-start.3
  70.0 0.0 copy-start.5
  70.0 1.8 %collective-permute-start.18 = (bf16[2,160,512]{2,1,0:T(8,128)(2,1)S(1)}, bf16[2,160,512]{2,1,0:T(8,128)(2,1)S(1)}, u32[]{:S(2)}, u32[]{:S(2)}) collective-permute-start(bf16[2,160,512]{2,1,0:T(8,128)(2,1)S(1)} %get-tuple-element.47), channel_id=1, source_target_pairs={{0,1},{1,0},{2,5},{3,4},{4,3},{5,2},{6,7},{7,6},{8,9},{9,8},{10,13... | collective-permute-start | bytes 983048 | tf_op jit(solution)/shard_map/ppermute | solution.py:551
  71.8 1.7 %shard_map.101.row_ref = f32[1,128]{1,0:T(1,128)S(1)} custom-call(f32[4,2,160,640]{3,2,1,0:T(8,128)S(1)} %copy-done, f32[3,2,160,640]{3,2,1,0:T(8,128)S(1)} %copy-done.1), custom_call_target="tpu_custom_call" | custom-call | flops 18022400 | bytes 5734400 | tf_op jit(solution)/shard_map/pallas_call | solution.py:668
  73.5 0.0 collective-permute-done.17
  73.5 6.5 %collective-permute-done.18 = bf16[2,160,512]{2,1,0:T(8,128)(2,1)S(1)} collective-permute-done((bf16[2,160,512]{2,1,0:T(8,128)(2,1)S(1)}, bf16[2,160,512]{2,1,0:T(8,128)(2,1)S(1)}, u32[]{:S(2)}, u32[]{:S(2)}) %collective-permute-start.18) | collective-permute-done | bytes 327712 | tf_op jit(solution)/shard_map/ppermute | solution.py:551
  80.1 0.1 add_convert_fusion.data_ref
  80.2 2.5 %shard_map.102 = (f32[2,160,640]{2,1,0:T(8,128)S(1)}, f32[32,128]{1,0:T(8,128)S(1)}) custom-call(s32[1,2]{1,0:T(1,128)S(1)} %copy-done.8, bf16[2,160,512]{2,1,0:T(8,128)(2,1)S(1)} %add_convert_fusion.data_ref, f32[2,160,640]{2,1,0:T(8,128)S(1)} %copy-done.3, f32[2,160,640]{2,1,0:T(8,128)S(1)} %copy-done.5, f32[4,2,160,640]{3,2,1,0:T(8,128)S(1)} %copy-done, ...), custom_call_target="tpu_custom_call" | custom-call | flops 13107200 | bytes 8192000 | tf_op jit(solution)/shard_map/pallas_call | solution.py:676
  82.7 17.7 %all_to_all.5 = f32[32,1,128]{2,1,0:T(1,128)S(1)} all-to-all(f32[32,1,128]{2,1,0:T(1,128)S(1)} %bitcast.28), channel_id=1, replica_groups=mesh['region'=8,'grp'=4] {'region','grp'}, dimensions={0} | all-to-all | bytes 32768 | tf_op jit(solution)/shard_map/all_to_all | solution.py:685
  100.4 1.5 %shard_map.103 = (f32[2,160,640]{2,1,0:T(8,128)}, f32[2,160,640]{2,1,0:T(8,128)}) custom-call(f32[32,128]{1,0:T(8,128)S(1)} %bitcast.27, f32[2,160,640]{2,1,0:T(8,128)S(1)} %copy-done.3, f32[2,160,640]{2,1,0:T(8,128)S(1)} %get-tuple-element.41.gradient_ref, f32[2,160,640]{2,1,0:T(8,128)S(1)} %copy-done.5, f32[4,2,160,640]{3,2,1,0:T(8,128)S(1)} %copy-done, ...), custom_call_target="tpu_custom_call" | custom-call | flops 8192000 | bytes 9011200 | tf_op jit(solution)/shard_map/pallas_call | solution.py:688
  (16 shorter events, 0.1 us)
Async XLA Ops:
  0.6 11.3 %copy-start.8 = (s32[1,2]{1,0:T(1,128)S(1)}, s32[1,2]{1,0:T(1,128)}, u32[]{:S(2)}) copy-start(s32[1,2]{1,0:T(1,128)} %pos_ref.3) | copy-start | bytes 28
  1.7 19.2 %collective-permute-start.4 = (bf16[128,512]{1,0:T(8,128)(2,1)S(1)}, bf16[128,512]{1,0:T(8,128)(2,1)S(1)}, u32[]{:S(2)}, u32[]{:S(2)}) collective-permute-start(bf16[128,512]{1,0:T(8,128)(2,1)S(1)} %get-tuple-element.23), channel_id=1, source_target_pairs={{0,3},{1,2},{2,1},{3,0},{4,7},{5,6},{6,5},{7,4},{8,11},{9,10},{10,... | collective-permute-start | bytes 393224 | tf_op jit(solution)/shard_map/ppermute | solution.py:551
  6.8 5.9 %collective-permute-start = (s32[1,2]{1,0:T(1,128)}, s32[1,2]{1,0:T(1,128)S(1)}, u32[]{:S(2)}, u32[]{:S(2)}) collective-permute-start(s32[1,2]{1,0:T(1,128)} %pos_ref.3), channel_id=1, source_target_pairs={{0,4},{1,5},{2,6},{3,7},{4,0},{5,1},{6,2},{7,3},{8,12},{9,13},{10,... | collective-permute-start | bytes 32 | tf_op jit(solution)/shard_map/ppermute | solution.py:551
  6.8 1.1 %copy-start.2 = (f32[2,160,640]{2,1,0:T(8,128)S(1)}, f32[2,160,640]{2,1,0:T(8,128)}, u32[]{:S(2)}) copy-start(f32[2,160,640]{2,1,0:T(8,128)} %transmission_ref.3) | copy-start | bytes 2457604
  7.9 0.7 copy-start.7
  8.6 33.2 %copy-start.6 = (bf16[2,8,128,512]{3,2,1,0:T(8,128)(2,1)S(1)}, bf16[2,8,128,512]{3,2,1,0:T(8,128)(2,1)}, u32[]{:S(2)}) copy-start(bf16[2,8,128,512]{3,2,1,0:T(8,128)(2,1)} %all_ref.1) | copy-start | bytes 6291460
  9.6 7.1 %collective-permute-start.2 = (bf16[128,512]{1,0:T(8,128)(2,1)S(1)}, bf16[128,512]{1,0:T(8,128)(2,1)S(1)}, u32[]{:S(2)}, u32[]{:S(2)}) collective-permute-start(bf16[128,512]{1,0:T(8,128)(2,1)S(1)} %get-tuple-element.23), channel_id=1, source_target_pairs={{0,1},{1,0},{2,3},{3,2},{4,5},{5,4},{6,7},{7,6},{8,9},{9,8},{10,11... | collective-permute-start | bytes 393224 | tf_op jit(solution)/shard_map/ppermute | solution.py:551
  9.7 11.1 %collective-permute-start.3 = (bf16[128,512]{1,0:T(8,128)(2,1)S(1)}, bf16[128,512]{1,0:T(8,128)(2,1)S(1)}, u32[]{:S(2)}, u32[]{:S(2)}) collective-permute-start(bf16[128,512]{1,0:T(8,128)(2,1)S(1)} %get-tuple-element.44), channel_id=1, source_target_pairs={{0,2},{1,3},{2,0},{3,1},{4,6},{5,7},{6,4},{7,5},{8,10},{9,11},{10,... | collective-permute-start | bytes 393224 | tf_op jit(solution)/shard_map/ppermute | solution.py:551
  11.3 9.6 %collective-permute-start.1 = (bf16[128,512]{1,0:T(8,128)(2,1)S(1)}, bf16[128,512]{1,0:T(8,128)(2,1)S(1)}, u32[]{:S(2)}, u32[]{:S(2)}) collective-permute-start(bf16[128,512]{1,0:T(8,128)(2,1)S(1)} %convert_bitcast_fusion), channel_id=1, source_target_pairs={{0,0},{1,1},{2,4},{3,5},{4,2},{5,3},{6,6},{7,7},{8,8},{9,9},{10,12... | collective-permute-start | bytes 393224 | tf_op jit(solution)/shard_map/ppermute | solution.py:551
  20.9 11.9 %collective-permute-start.7 = (bf16[384,512]{1,0:T(8,128)(2,1)S(1)}, bf16[384,512]{1,0:T(8,128)(2,1)S(1)}, u32[]{:S(2)}, u32[]{:S(2)}) collective-permute-start(bf16[384,512]{1,0:T(8,128)(2,1)S(1)} %constant_dynamic-update-slice_fusion.q0_ref), channel_id=1, source_target_pairs={{0,16},{1,17},{2,18},{3,19},{4,20},{5,21},{6,22},{7,23},{8,24},{9,... | collective-permute-start | bytes 1179656 | tf_op jit(solution)/shard_map/ppermute | solution.py:551
  22.4 11.9 %collective-permute-start.9 = (bf16[384,512]{1,0:T(8,128)(2,1)S(1)}, bf16[384,512]{1,0:T(8,128)(2,1)S(1)}, u32[]{:S(2)}, u32[]{:S(2)}) collective-permute-start(bf16[384,512]{1,0:T(8,128)(2,1)S(1)} %constant_dynamic-update-slice_fusion.q0_ref), channel_id=1, source_target_pairs={{0,8},{1,9},{2,10},{3,11},{4,12},{5,13},{6,14},{7,15},{8,0},{9,1},... | collective-permute-start | bytes 1179656 | tf_op jit(solution)/shard_map/ppermute | solution.py:551
  23.9 12.0 %collective-permute-start.5 = (bf16[2,160,512]{2,1,0:T(8,128)(2,1)S(1)}, bf16[2,160,512]{2,1,0:T(8,128)(2,1)S(1)}, u32[]{:S(2)}, u32[]{:S(2)}) collective-permute-start(bf16[2,160,512]{2,1,0:T(8,128)(2,1)S(1)} %shard_map.95), channel_id=1, source_target_pairs={{0,0},{1,1},{2,4},{3,5},{4,2},{5,3},{6,6},{7,7},{8,8},{9,9},{10,12... | collective-permute-start | bytes 983048 | tf_op jit(solution)/shard_map/ppermute | solution.py:551
  24.6 11.4 %collective-permute-start.6 = (bf16[2,160,512]{2,1,0:T(8,128)(2,1)S(1)}, bf16[2,160,512]{2,1,0:T(8,128)(2,1)S(1)}, u32[]{:S(2)}, u32[]{:S(2)}) collective-permute-start(bf16[2,160,512]{2,1,0:T(8,128)(2,1)S(1)} %shard_map.95), channel_id=1, source_target_pairs={{0,1},{1,0},{2,5},{3,4},{4,3},{5,2},{6,7},{7,6},{8,9},{9,8},{10,13... | collective-permute-start | bytes 983048 | tf_op jit(solution)/shard_map/ppermute | solution.py:551
  32.8 7.1 %collective-permute-start.8 = (bf16[192,512]{1,0:T(8,128)(2,1)S(1)}, bf16[192,512]{1,0:T(8,128)(2,1)S(1)}, u32[]{:S(2)}, u32[]{:S(2)}) collective-permute-start(bf16[192,512]{1,0:T(8,128)(2,1)S(1)} %slice.24), channel_id=1, source_target_pairs={{0,8},{1,9},{2,10},{3,11},{4,12},{5,13},{6,14},{7,15},{8,0},{9,1},... | collective-permute-start | bytes 589832 | tf_op jit(solution)/shard_map/ppermute | solution.py:551
  34.4 9.0 %copy-start.4 = (bf16[3,512,512]{2,1,0:T(8,128)(2,1)S(1)}, bf16[3,512,512]{2,1,0:T(8,128)(2,1)}, u32[]{:S(2)}) copy-start(bf16[3,512,512]{2,1,0:T(8,128)(2,1)} %constant.23.clone.right_ref) | copy-start | bytes 4718596
  34.4 6.8 %collective-permute-start.10 = (bf16[192,512]{1,0:T(8,128)(2,1)S(1)}, bf16[192,512]{1,0:T(8,128)(2,1)S(1)}, u32[]{:S(2)}, u32[]{:S(2)}) collective-permute-start(bf16[192,512]{1,0:T(8,128)(2,1)S(1)} %slice.25), channel_id=1, source_target_pairs={{0,16},{1,17},{2,18},{3,19},{4,20},{5,21},{6,22},{7,23},{8,24},{9,... | collective-permute-start | bytes 589832 | tf_op jit(solution)/shard_map/ppermute | solution.py:551
  41.2 1.9 %collective-permute-start.11 = (bf16[2,160,512]{2,1,0:T(8,128)(2,1)S(1)}, bf16[2,160,512]{2,1,0:T(8,128)(2,1)S(1)}, u32[]{:S(2)}, u32[]{:S(2)}) collective-permute-start(bf16[2,160,512]{2,1,0:T(8,128)(2,1)S(1)} %collective-permute-done.5.own_ref), channel_id=1, source_target_pairs={{0,4},{1,5},{2,6},{3,7},{4,0},{5,1},{6,2},{7,3},{8,12},{9,13},{10,... | collective-permute-start | bytes 983048 | tf_op jit(solution)/shard_map/ppermute | solution.py:551
  41.2 2.1 %collective-permute-start.12 = (bf16[2,160,512]{2,1,0:T(8,128)(2,1)S(1)}, bf16[2,160,512]{2,1,0:T(8,128)(2,1)S(1)}, u32[]{:S(2)}, u32[]{:S(2)}) collective-permute-start(bf16[2,160,512]{2,1,0:T(8,128)(2,1)S(1)} %collective-permute-done.6.side_ref), channel_id=1, source_target_pairs={{0,4},{1,5},{2,6},{3,7},{4,0},{5,1},{6,2},{7,3},{8,12},{9,13},{10,... | collective-permute-start | bytes 983048 | tf_op jit(solution)/shard_map/ppermute | solution.py:551
  48.5 1.8 %collective-permute-start.13 = (bf16[512,256]{1,0:T(8,128)(2,1)S(1)}, bf16[512,256]{1,0:T(8,128)(2,1)S(1)}, u32[]{:S(2)}, u32[]{:S(2)}) collective-permute-start(bf16[512,256]{1,0:T(8,128)(2,1)S(1)} %get-tuple-element.35), channel_id=1, source_target_pairs={{0,4},{1,5},{2,6},{3,7},{4,0},{5,1},{6,2},{7,3},{8,12},{9,13},{10,... | collective-permute-start | bytes 786440 | tf_op jit(solution)/shard_map/ppermute | solution.py:551
  50.4 9.8 %collective-permute-start.14 = (bf16[512,256]{1,0:T(8,128)(2,1)S(1)}, bf16[512,256]{1,0:T(8,128)(2,1)S(1)}, u32[]{:S(2)}, u32[]{:S(2)}) collective-permute-start(bf16[512,256]{1,0:T(8,128)(2,1)S(1)} %fusion.2), channel_id=1, source_target_pairs={{0,1},{1,0},{2,3},{3,2},{4,5},{5,4},{6,7},{7,6},{8,9},{9,8},{10,11... | collective-permute-start | bytes 786440 | tf_op jit(solution)/shard_map/ppermute | solution.py:551
  60.3 1.6 %collective-permute-start.15 = (bf16[512,256]{1,0:T(8,128)(2,1)S(1)}, bf16[512,256]{1,0:T(8,128)(2,1)S(1)}, u32[]{:S(2)}, u32[]{:S(2)}) collective-permute-start(bf16[512,256]{1,0:T(8,128)(2,1)S(1)} %get-tuple-element.42), channel_id=1, source_target_pairs={{0,4},{1,5},{2,6},{3,7},{4,0},{5,1},{6,2},{7,3},{8,12},{9,13},{10,... | collective-permute-start | bytes 786440 | tf_op jit(solution)/shard_map/ppermute | solution.py:551
  61.9 9.9 %copy-start = (f32[4,2,160,640]{3,2,1,0:T(8,128)S(1)}, f32[4,2,160,640]{3,2,1,0:T(8,128)}, u32[]{:S(2)}) copy-start(f32[4,2,160,640]{3,2,1,0:T(8,128)} %steps_ref.5) | copy-start | bytes 9830404
  61.9 9.9 %copy-start.1 = (f32[3,2,160,640]{3,2,1,0:T(8,128)S(1)}, f32[3,2,160,640]{3,2,1,0:T(8,128)}, u32[]{:S(2)}) copy-start(f32[3,2,160,640]{3,2,1,0:T(8,128)} %changes_ref.5) | copy-start | bytes 7372804
  66.7 2.2 %collective-permute-start.16 = (bf16[2,2,160,512]{3,2,1,0:T(8,128)(2,1)S(1)}, bf16[2,2,160,512]{3,2,1,0:T(8,128)(2,1)S(1)}, u32[]{:S(2)}, u32[]{:S(2)}) collective-permute-start(bf16[2,2,160,512]{3,2,1,0:T(8,128)(2,1)S(1)} %get-tuple-element.38), channel_id=1, source_target_pairs={{0,4},{1,5},{2,6},{3,7},{4,0},{5,1},{6,2},{7,3},{8,12},{9,13},{10,... | collective-permute-start | bytes 1966088 | tf_op jit(solution)/shard_map/ppermute | solution.py:551
  69.1 4.4 %collective-permute-start.17 = (bf16[2,160,512]{2,1,0:T(8,128)(2,1)S(1)}, bf16[2,160,512]{2,1,0:T(8,128)(2,1)S(1)}, u32[]{:S(2)}, u32[]{:S(2)}) collective-permute-start(bf16[2,160,512]{2,1,0:T(8,128)(2,1)S(1)} %get-tuple-element.46), channel_id=1, source_target_pairs={{0,0},{1,1},{2,4},{3,5},{4,2},{5,3},{6,6},{7,7},{8,8},{9,9},{10,12... | collective-permute-start | bytes 983048 | tf_op jit(solution)/shard_map/ppermute | solution.py:551
  69.9 10.2 %copy-start.3 = (f32[2,160,640]{2,1,0:T(8,128)S(1)}, f32[2,160,640]{2,1,0:T(8,128)}, u32[]{:S(2)}) copy-start(f32[2,160,640]{2,1,0:T(8,128)} %transmission_ref.3) | copy-start | bytes 2457604
  70.0 10.2 %copy-start.5 = (f32[2,160,640]{2,1,0:T(8,128)S(1)}, f32[2,160,640]{2,1,0:T(8,128)}, u32[]{:S(2)}) copy-start(f32[2,160,640]{2,1,0:T(8,128)} %old_ref.3) | copy-start | bytes 2457604
  70.0 10.1 %collective-permute-start.18 = (bf16[2,160,512]{2,1,0:T(8,128)(2,1)S(1)}, bf16[2,160,512]{2,1,0:T(8,128)(2,1)S(1)}, u32[]{:S(2)}, u32[]{:S(2)}) collective-permute-start(bf16[2,160,512]{2,1,0:T(8,128)(2,1)S(1)} %get-tuple-element.47), channel_id=1, source_target_pairs={{0,1},{1,0},{2,5},{3,4},{4,3},{5,2},{6,7},{7,6},{8,9},{9,8},{10,13... | collective-permute-start | bytes 983048 | tf_op jit(solution)/shard_map/ppermute | solution.py:551
